TPU v7x, 32 devices: a whole 2x2x4 slice. The times are simulated.
32 devices in a mesh: seq: 16 (over z, y, x), tp: 2 (over core).
Axes of the slice: x: 2, y: 2, z: 4, core: 2. Of those that a mesh axis runs over, the one named last changes fastest.
Arguments:
- query_proj: bfloat16 [4096, 2048], P('tp', 'seq'), may hold values from -6 to 6
- key_proj: bfloat16 [4096, 2048], P('tp', 'seq'), may hold values from -6 to 6
- value_proj: bfloat16 [4096, 2048], P('tp', 'seq'), may hold values from -6 to 6
- short_taps: float32 [3, 3, 4096], P(None, None, 'tp'), may hold values from -3.5 to 3.5
- long_filters: float32 [4096, 2048], P(('tp', 'seq')), may hold values from -2 to 2
- out_weight: bfloat16 [4096, 8192], P('seq', 'tp'), may hold values from -0.09375 to 0.09375
Outputs:
- block_out: bfloat16 [2048, 8192], P('seq', 'tp')
All inputs are finite; a program needn't handle non-finite values.
Results may differ from a plain program's by a relative error of at most 0.0058.
Values may be sent and summed in bfloat16 or wider, within the bound.
No kernel may reach another device: no remote copies, remote signals or barrier semaphores. Data moves between devices by JAX's collectives and lax.ppermute only.
A program may use at most 128 MiB of HBM per device.

v0:
```python
import math

import jax
import jax.numpy as jnp
from jax import lax
from jax.sharding import PartitionSpec as P

precise = lax.Precision.HIGHEST


def shifted(value, axis, steps):
    count = lax.axis_size(axis)
    initial, last = (max(0, -steps), min(count, count - steps))
    return lax.ppermute(value, axis, [(source, source + steps) for source in range(initial, last)])


def short_filter(extended, tap_weights):
    return (
        tap_weights[0][:, None] * extended[:, 2:]
        + tap_weights[1][:, None] * extended[:, 1:-1]
        + tap_weights[2][:, None] * extended[:, :-2]
    )


def phase_table(period, out_size, in_size, direction):
    out_index = lax.broadcasted_iota(jnp.int32, (out_size, in_size), 0)
    in_index = lax.broadcasted_iota(jnp.int32, (out_size, in_size), 1)
    phase_angle = (out_index * in_index % period).astype(jnp.float32) * (
        direction * 2.0 * math.pi / period
    )
    return (jnp.cos(phase_angle), jnp.sin(phase_angle))


def left_apply(phase, signal):
    return jnp.einsum("kn,cnm->ckm", phase, signal, precision=precise)


def right_apply(signal, phase):
    return jnp.einsum("ckn,nm->ckm", signal, phase, precision=precise)


def forward_spectrum(signal, inner_size):
    channels_here, length = signal.shape
    period = 2 * length
    outer_size = period // inner_size
    blocks = signal.reshape(channels_here, outer_size // 2, inner_size)
    left_re, left_im = phase_table(outer_size, outer_size, outer_size // 2, -1.0)
    section_re = left_apply(left_re, blocks)
    section_im = left_apply(left_im, blocks)
    twist_re, twist_im = phase_table(period, outer_size, inner_size, -1.0)
    turned_re = section_re * twist_re - section_im * twist_im
    turned_im = section_re * twist_im + section_im * twist_re
    right_re, right_im = phase_table(inner_size, inner_size, inner_size, -1.0)
    spec_re = right_apply(turned_re, right_re) - right_apply(turned_im, right_im)
    spec_im = right_apply(turned_re, right_im) + right_apply(turned_im, right_re)
    return (spec_re, spec_im)


def inverse_signal(spec_re, spec_im, length, inner_size):
    channels_here = spec_re.shape[0]
    period = 2 * length
    outer_size = period // inner_size
    right_re, right_im = phase_table(inner_size, inner_size, inner_size, 1.0)
    mid_re = right_apply(spec_re, right_re) - right_apply(spec_im, right_im)
    mid_im = right_apply(spec_re, right_im) + right_apply(spec_im, right_re)
    twist_re, twist_im = phase_table(period, outer_size, inner_size, 1.0)
    turned_re = mid_re * twist_re - mid_im * twist_im
    turned_im = mid_re * twist_im + mid_im * twist_re
    left_re, left_im = phase_table(outer_size, outer_size // 2, outer_size, 1.0)
    signal = left_apply(left_re, turned_re) - left_apply(left_im, turned_im)
    return signal.reshape(channels_here, length) / period


def long_convolve(signal, filters, inner_size):
    length = signal.shape[1]
    data_re, data_im = forward_spectrum(signal, inner_size)
    filt_re, filt_im = forward_spectrum(filters, inner_size)
    prod_re = data_re * filt_re - data_im * filt_im
    prod_im = data_re * filt_im + data_im * filt_re
    return inverse_signal(prod_re, prod_im, length, inner_size)


def shards(query_proj, key_proj, value_proj, short_taps, long_filters, out_weight):
    tok_rows = query_proj.shape[1]
    inner_size = tok_rows // 2
    tail_cols = jnp.stack([query_proj[:, -2:], key_proj[:, -2:], value_proj[:, -2:]])
    before = shifted(tail_cols, "seq", 1)
    shorts = []
    for stream_index, stream in enumerate((query_proj, key_proj, value_proj)):
        extended = jnp.concatenate([before[stream_index], stream], axis=1).astype(jnp.float32)
        shorts.append(short_filter(extended, short_taps[stream_index]))
    query_short, key_short, value_short = shorts
    product = (key_short * value_short).astype(jnp.bfloat16)
    spread = lax.all_to_all(product, "seq", split_axis=0, concat_axis=1, tiled=True)
    mixed_conv = long_convolve(spread.astype(jnp.float32), long_filters, inner_size)
    returned = lax.all_to_all(mixed_conv, "seq", split_axis=1, concat_axis=0, tiled=True)
    gated_out = (query_short * returned).astype(jnp.bfloat16)
    full_rows = lax.all_gather(gated_out, "tp", axis=0, tiled=True)
    result = lax.dot_general(
        full_rows,
        lax.all_gather(out_weight, "seq", axis=0, tiled=True),
        (((0,), (0,)), ((), ())),
        preferred_element_type=jnp.float32,
    )
    return result.astype(jnp.bfloat16)


def solution(mesh):
    return jax.shard_map(
        shards,
        mesh=mesh,
        in_specs=(
            P("tp", "seq"),
            P("tp", "seq"),
            P("tp", "seq"),
            P(None, None, "tp"),
            P(("tp", "seq"), None),
            P("seq", "tp"),
        ),
        out_specs=P("seq", "tp"),
        check_vma=False,
    )
```

profile of v0, /device:TPU:0, one launch (start us, length us, event | category | flops | bytes accessed | tf_op | source)
XLA Modules:
  0.0 512.3 jit_solution(18286504048867099184)
XLA Ops:
  6.5 1.3 slice.94
  7.9 0.2 copy.85
  8.1 1.4 slice.95
  9.5 0.2 copy.86
  9.7 0.2 slice.96
  9.9 0.2 copy.87
  10.2 4.8 collective-permute-start
  15.0 0.1 multiply_sine_fusion.3
  15.2 0.1 multiply_cosine_fusion
  15.4 0.3 copy.70
  15.7 2.4 fusion.53
  18.1 3.3 subtract_bitcast_fusion
  21.5 4.6 fusion.6
  26.1 0.1 multiply_sine_fusion
  26.3 0.1 copy.80
  26.4 1.1 copy.90
  27.5 1.1 copy.89
  28.6 2.0 maximum_convert_fusion.1
  30.5 3.7 fusion.45
  34.2 6.4 %all-to-all-start = ((bf16[16,128,128]{2,1,0:T(8,128)(2,1)}), bf16[16,128,128]{2,1,0:T(8,128)(2,1)S(1)}, u32[]{:S(2)}, u32[]{:S(2)}) async-start(bf16[16,128,128]{2,1,0:T(8,128)(2,1)} %bitcast.15), calls=%async_computation | async-start | bytes 1048576 | tf_op jit(solution)/shard_map/all_to_all | solution.py:94
  40.7 5.0 fusion.8
  45.7 4.7 fusion.31
  50.4 4.7 fusion.28
  55.1 0.3 copy.65
  55.4 1.1 fusion.59
  56.5 2.3 fusion
  58.8 3.3 fusion.16
  62.1 3.3 fusion.14
  65.4 3.3 fusion.22
  68.8 4.2 multiply_add_fusion.1
  73.0 2.1 fusion.67
  75.1 2.1 fusion.63
  77.3 2.1 convolution_subtract_fusion
  79.4 3.1 multiply_subtract_fusion
  82.5 2.9 fusion.2
  85.5 2.5 fusion.40
  88.0 1.6 copy.83
  89.6 6.9 %all-to-all-start.1 = ((f32[128,16,128]{0,2,1:T(8,128)}), f32[128,16,128]{0,2,1:T(8,128)S(1)}, u32[]{:S(2)}, u32[]{:S(2)}) async-start(f32[128,16,128]{0,2,1:T(8,128)} %bitcast.32), calls=%async_computation.1 | async-start | bytes 2097152 | tf_op jit(solution)/shard_map/all_to_all | solution.py:96
  96.5 1.1 copy.88
  97.6 1.6 maximum_convert_fusion
  99.2 20.9 %all-to-all-done.1 = f32[128,16,128]{0,2,1:T(8,128)S(1)} async-done(((f32[128,16,128]{0,2,1:T(8,128)}), f32[128,16,128]{0,2,1:T(8,128)S(1)}, u32[]{:S(2)}, u32[]{:S(2)}) %all-to-all-start.1) | async-done | bytes 1048608 | tf_op jit(solution)/shard_map/all_to_all | solution.py:96
  120.1 1.3 copy.84
  121.4 3.2 fusion.51
  124.7 0.2 all-gather.5.cloned.1.call-start
  124.9 0.5 all-gather.5.cloned.1.call-update
  125.4 8.6 %all-gather.3.cloned.1.call-done = bf16[4096,128]{1,0:T(8,128)(2,1)} async-done(((bf16[2048,128]{1,0:T(8,128)(2,1)}), bf16[4096,128]{1,0:T(8,128)(2,1)}) %all-gather.3.cloned.1.call-update) | async-done | bytes 1048592 | tf_op jit(solution)/shard_map/all_gather | solution.py:98
  134.0 354.8 %all-gather.5.cloned.1.call-done = bf16[4096,4096]{1,0:T(8,128)(2,1)} async-done(((bf16[256,4096]{1,0:T(8,128)(2,1)}), bf16[4096,4096]{1,0:T(8,128)(2,1)}) %all-gather.5.cloned.1.call-update) | async-done | bytes 33554448 | tf_op jit(solution)/shard_map/all_gather | solution.py:101
  488.9 16.4 %convolution_convert_fusion = bf16[128,4096]{1,0:T(8,128)(2,1)} fusion(bf16[4096,128]{1,0:T(8,128)(2,1)} %all-gather.3.cloned.1.call-done, bf16[4096,4096]{1,0:T(8,128)(2,1)} %all-gather.5.cloned.1.call-done), kind=kOutput, calls=%fused_computation | convolution fusion | flops 4295491584 | bytes 35651584 | tf_op jit(solution)/shard_map/dot_general | solution.py:99
  (26 shorter events, 0.3 us)
Async XLA Ops:
  6.5 3.1 copy-start.4
  7.8 7.5 %copy-start.8 = (f32[3,3,2048]{2,1,0:T(4,128)S(1)}, f32[3,3,2048]{2,1,0:T(4,128)}, u32[]{:S(2)}) copy-start(f32[3,3,2048]{2,1,0:T(4,128)} %param.9) | copy-start | bytes 221188
  7.9 7.5 %copy-start.7 = (f32[128,2048]{1,0:T(8,128)S(1)}, f32[128,2048]{1,0:T(8,128)}, u32[]{:S(2)}) copy-start(f32[128,2048]{1,0:T(8,128)} %param.10) | copy-start | bytes 3145732
  10.2 16.2 %collective-permute-start = (bf16[3,2048,2]{1,2,0:T(2,128)(2,1)S(1)}, bf16[3,2048,2]{1,2,0:T(2,128)(2,1)S(1)}, u32[]{:S(2)}, u32[]{:S(2)}) collective-permute-start(bf16[3,2048,2]{1,2,0:T(2,128)(2,1)S(1)} %pad_maximum_fusion), channel_id=1, source_target_pairs={{0,2},{2,4},{4,6},{6,8},{8,10},{10,12},{12,14},{14,16},{16,18},{18... | collective-permute-start | bytes 73736 | tf_op jit(solution)/shard_map/ppermute | solution.py:14
  21.4 4.7 copy-start
  21.4 7.1 %copy-start.5 = (bf16[2048,128]{1,0:T(8,128)(2,1)S(1)}, bf16[2048,128]{1,0:T(8,128)(2,1)}, u32[]{:S(2)}) copy-start(bf16[2048,128]{1,0:T(8,128)(2,1)} %param.8) | copy-start | bytes 1572868
  21.5 7.1 %copy-start.6 = (bf16[2048,128]{1,0:T(8,128)(2,1)S(1)}, bf16[2048,128]{1,0:T(8,128)(2,1)}, u32[]{:S(2)}) copy-start(bf16[2048,128]{1,0:T(8,128)(2,1)} %param.7) | copy-start | bytes 1572868
  34.2 20.9 %all-to-all-start = ((bf16[16,128,128]{2,1,0:T(8,128)(2,1)}), bf16[16,128,128]{2,1,0:T(8,128)(2,1)S(1)}, u32[]{:S(2)}, u32[]{:S(2)}) async-start(bf16[16,128,128]{2,1,0:T(8,128)(2,1)} %bitcast.15), calls=%async_computation | async-start | bytes 1048576 | tf_op jit(solution)/shard_map/all_to_all | solution.py:94
  40.7 5.0 copy-start.3
  65.4 3.3 copy-start.1
  65.4 3.3 copy-start.2
  89.6 30.5 %all-to-all-start.1 = ((f32[128,16,128]{0,2,1:T(8,128)}), f32[128,16,128]{0,2,1:T(8,128)S(1)}, u32[]{:S(2)}, u32[]{:S(2)}) async-start(f32[128,16,128]{0,2,1:T(8,128)} %bitcast.32), calls=%async_computation.1 | async-start | bytes 2097152 | tf_op jit(solution)/shard_map/all_to_all | solution.py:96
  96.5 37.6 %all-gather.3.cloned.1.call-start = ((), (), s32[]{:S(2)}) async-start(), calls=%async_computation.2 | async-start | bytes 1572864 | tf_op jit(solution)/shard_map/all_gather | solution.py:98
  124.7 364.2 %all-gather.5.cloned.1.call-start = ((), (), s32[]{:S(2)}) async-start(), calls=%async_computation.3 | async-start | bytes 35651584 | tf_op jit(solution)/shard_map/all_gather | solution.py:101
Sparse Core Ops, SparseCore 0:
  124.8 9.2 all-gather.2
  136.8 352.0 all-gather.4
where the time goes:
time: 522 us; the launch traced here: 512 us
  waiting for transfers between devices  385 us (74%)
  matrix products  73.6 us (14%)
  starting transfers between devices  18.4 us (4%)
  between operations  13.9 us (3%)
  other arithmetic  11 us (2%)
  local copies, waits for them, and re-layouts  10.5 us (2%)
    all_gather x1, waiting for transfers between devices, shards(): lax.all_gather(out_weight, 'seq', axis=0, tiled=True)  355 us
    dot_general x12, matrix products, right_apply(): return jnp.einsum('ckn,nm->ckm', signal, phase, precision=precise)  42.7 us
    all_to_all x1, waiting for transfers between devices, shards(): lax.all_to_all(mixed_conv, 'seq', split_axis=1, concat_axis=0, tiled=True)  20.9 us
    dot_general x1, matrix products, shards(): lax.dot_general(full_rows, lax.all_gather(out_weight, 'seq', axis=0, tile...  16.4 us
    dot_general x6, matrix products, left_apply(): return jnp.einsum('kn,cnm->ckm', phase, signal, precision=precise)  14.5 us
  transfers between devices with their start and end apart: 5, of which 3 were waited for; matrix products, arithmetic and copies ran while one was open for 6% of the time, Pallas kernels for 0%

commit v1 on v0

--- a/solution.py
+++ b/solution.py
@@ -1,11 +1,15 @@
+import functools
 import math
 
 import jax
 import jax.numpy as jnp
 from jax import lax
+from jax.experimental import pallas as pl
+from jax.experimental.pallas import tpu as pltpu
 from jax.sharding import PartitionSpec as P
 
-precise = lax.Precision.HIGHEST
+PLANE = 4
+VMEM_LIMIT = 40 * 2**20
 
 
 def shifted(value, axis, steps):
@@ -22,6 +26,216 @@
     )
 
 
+def filtered_streams(streams, taps):
+    before = shifted(jnp.stack([stream[:, -2:] for stream in streams]), "seq", 1)
+    extended = [
+        jnp.concatenate([before[index], stream], axis=1).astype(jnp.float32)
+        for index, stream in enumerate(streams)
+    ]
+    return [short_filter(value, tap) for value, tap in zip(extended, taps)]
+
+
+def delayed(value, steps, lane, row):
+    rolled = pltpu.roll(value, steps, 1)
+    above = jnp.where(row >= 1, pltpu.roll(rolled, 1, 0), 0.0)
+    return jnp.where(lane >= steps, rolled, above)
+
+
+def conv_kernel(place_ref, taps_ref, x_ref, h_ref, q_ref, *rest):
+    outs, (xpad, gated) = rest[:-2], rest[-2:]
+    channels, blocks, width = x_ref.shape
+    keep = lax.broadcasted_iota(jnp.int32, (width, width), 1) >= lax.broadcasted_iota(
+        jnp.int32, (width, width), 0
+    )
+    lane = lax.broadcasted_iota(jnp.int32, (blocks, width), 1)
+    row = lax.broadcasted_iota(jnp.int32, (blocks, width), 0)
+    xpad[:blocks] = jnp.zeros((blocks, width), jnp.float32)
+
+    def one_channel(channel, carry):
+        xpad[blocks:] = x_ref[channel].astype(jnp.float32)
+        earlier = jnp.zeros((width, width), jnp.float32)
+        total = jnp.zeros((blocks, width), jnp.float32)
+        bands, shifts = [], []
+        for lag in range(blocks):
+            rolled = pltpu.roll(
+                jnp.broadcast_to(h_ref[channel, lag : lag + 1, :], (width, width)),
+                0,
+                1,
+                stride=1,
+                stride_axis=0,
+            )
+            bands.append(jnp.where(keep, rolled, earlier).astype(jnp.bfloat16))
+            earlier = rolled
+            shifts.append(xpad[pl.ds(blocks - lag, blocks), :].astype(jnp.bfloat16))
+            if len(bands) == 2:
+                total += jnp.dot(
+                    jnp.concatenate(shifts, axis=1),
+                    jnp.concatenate(bands, axis=0),
+                    preferred_element_type=jnp.float32,
+                )
+                bands, shifts = [], []
+        query = q_ref[channel].astype(jnp.float32)
+        query_short = (
+            taps_ref[0, channel] * query
+            + taps_ref[1, channel] * delayed(query, 1, lane, row)
+            + taps_ref[2, channel] * delayed(query, 2, lane, row)
+        )
+        gated[pl.ds(pl.multiple_of(channel * blocks, blocks), blocks), :] = query_short * total
+        return carry
+
+    lax.fori_loop(0, channels, one_channel, 0, unroll=4)
+    inner = len(outs)
+    for offset, out in enumerate(outs):
+        for outer in range(blocks // inner):
+            block = outer * inner + jnp.bitwise_xor(place_ref[0], offset)
+            tile = gated[pl.ds(block, channels, stride=blocks), :]
+            out[outer] = tile.T.astype(jnp.bfloat16)
+
+
+def convolve_and_gate(place, taps, product, filters, query, inner):
+    channels, blocks, width = product.shape
+    vmem = pl.BlockSpec(memory_space=pltpu.VMEM)
+    smem = pl.BlockSpec(memory_space=pltpu.SMEM)
+    return pl.pallas_call(
+        conv_kernel,
+        out_shape=[jax.ShapeDtypeStruct((blocks // inner, width, channels), jnp.bfloat16)] * inner,
+        in_specs=[smem, smem, vmem, vmem, vmem],
+        out_specs=[vmem] * inner,
+        scratch_shapes=[
+            pltpu.VMEM((2 * blocks, width), jnp.float32),
+            pltpu.VMEM((channels * blocks, width), jnp.float32),
+        ],
+        compiler_params=pltpu.CompilerParams(vmem_limit_bytes=VMEM_LIMIT),
+        cost_estimate=pl.CostEstimate(
+            flops=2 * channels * width * width * blocks * blocks,
+            bytes_accessed=12 * channels * blocks * width,
+            transcendentals=0,
+        ),
+    )(place, taps, product, filters, query)
+
+
+def project_kernel(pieces, place_ref, *refs):
+    gates, weights, outs = refs[: 8 * pieces], refs[8 * pieces : -pieces], refs[-pieces:]
+    tiles = [ref[...] for ref in weights[:3]] + [
+        jnp.concatenate([weights[3][...], weights[4][...]], axis=0)
+    ]
+    depth = tiles[0].shape[0] // 2
+    for piece in range(pieces):
+        mine = [ref[...].reshape(-1, depth) for ref in gates[8 * piece : 8 * piece + 8]]
+        total = None
+        for index, tile in enumerate(tiles):
+            left = jnp.concatenate([mine[2 * index], mine[2 * index + 1]], axis=1)
+            term = jnp.dot(left, tile, preferred_element_type=jnp.float32)
+            total = term if total is None else total + term
+        outs[piece][...] = total.astype(outs[piece].dtype)
+
+
+def project(place, gates, weights, steps, dtype, tile=512):
+    _, _, planes, rows, depth = gates.shape
+    columns = weights[0].shape[1]
+
+    def gate_spec(step, offset, half):
+        def index(column, place_ref):
+            inner, outer, core = place_ref[0], place_ref[1], place_ref[2]
+            owner = inner ^ offset
+            source = 2 * (owner % 2) + half
+            return ((owner // 2) ^ core, source ^ inner, (outer + step) % planes, 0, 0)
+
+        return pl.BlockSpec((1, 1, 1, rows, depth), index)
+
+    gate_specs = [
+        gate_spec(step, offset, half) for step in steps for offset in range(PLANE) for half in range(2)
+    ]
+    weight_specs = [
+        pl.BlockSpec((weight.shape[0], tile), lambda column, place_ref: (0, column))
+        for weight in weights
+    ]
+    return pl.pallas_call(
+        functools.partial(project_kernel, len(steps)),
+        out_shape=[jax.ShapeDtypeStruct((rows, columns), dtype)] * len(steps),
+        grid_spec=pltpu.PrefetchScalarGridSpec(
+            num_scalar_prefetch=1,
+            grid=(columns // tile,),
+            in_specs=gate_specs + weight_specs,
+            out_specs=[pl.BlockSpec((rows, tile), lambda column, place_ref: (0, column))] * len(steps),
+        ),
+        compiler_params=pltpu.CompilerParams(vmem_limit_bytes=VMEM_LIMIT),
+        cost_estimate=pl.CostEstimate(
+            flops=2 * len(steps) * rows * 8 * depth * columns,
+            bytes_accessed=16 * depth * columns + 4 * len(steps) * rows * columns,
+            transcendentals=0,
+        ),
+    )(place, *[gates] * len(gate_specs), *weights)
+
+
+def by_planes(query_proj, key_proj, value_proj, short_taps, long_filters, out_weight):
+    seq_count, tp_count = lax.axis_size("seq"), lax.axis_size("tp")
+    planes = seq_count // PLANE
+    place_seq, core = lax.axis_index("seq"), lax.axis_index("tp")
+    inner, outer = place_seq % PLANE, place_seq // PLANE
+    place = jnp.stack([inner, outer, core]).astype(jnp.int32)
+    channels, width = long_filters.shape[0], query_proj.shape[1]
+
+    across = [(source, source ^ 1) for source in range(seq_count)]
+    along = [(source, source ^ 2) for source in range(seq_count)]
+    up = [(source, (source + PLANE) % seq_count) for source in range(seq_count)]
+    down = [(target, source) for source, target in up]
+
+    def spread(stream):
+        parts = lax.all_to_all(
+            stream.reshape(seq_count, channels, width), "seq", split_axis=0, concat_axis=0, tiled=True
+        )
+        return parts.transpose(1, 0, 2)
+
+    weight_x = lax.ppermute(out_weight, "seq", across)
+    weight_y = lax.ppermute(out_weight, "seq", along)
+    half_rows = out_weight.shape[0] // 2
+    weight_top = lax.ppermute(weight_y[:half_rows], "seq", across)
+    weight_end = lax.ppermute(weight_x[half_rows:], "seq", along)
+    weights = [out_weight, weight_x, weight_y, weight_top, weight_end]
+
+    query = spread(query_proj)
+    key_short, value_short = filtered_streams((key_proj, value_proj), short_taps[1:])
+    product = spread((key_short * value_short).astype(jnp.bfloat16))
+    taps = lax.dynamic_slice_in_dim(short_taps[0], place_seq * channels, channels, axis=1)
+    filters = long_filters.reshape(channels, seq_count, width)
+    gated = convolve_and_gate(place, taps, product, filters, query, PLANE)
+
+    landed = []
+    for offset, message in enumerate(gated):
+        pairs = []
+        for source in range(seq_count):
+            z, q = divmod(source, PLANE)
+            for tp in range(tp_count):
+                target = (planes // tp_count * tp + z // tp_count) * PLANE + (q ^ offset)
+                pairs.append((source * tp_count + tp, target * tp_count + z % tp_count))
+        landed.append(lax.ppermute(message, ("seq", "tp"), pairs))
+    own = jnp.stack(landed)
+    other = lax.ppermute(own, "tp", [(0, 1), (1, 0)])
+    gates = jnp.stack([own, other])
+
+    (far,) = project(place, gates, weights, (2,), jnp.bfloat16)
+    half = far.shape[1] // 2
+    far_left = lax.ppermute(far[:, :half], "seq", up)
+    far_right = lax.ppermute(far[:, half:], "seq", down)
+    ahead, behind = project(place, gates, weights, (1, planes - 1), jnp.bfloat16)
+    near_right = lax.ppermute(ahead[:, half:], "seq", up)
+    near_left = lax.ppermute(behind[:, :half], "seq", down)
+    (mine,) = project(place, gates, weights, (0,), jnp.float32)
+
+    def added(first, second):
+        return (first.astype(jnp.float32) + second.astype(jnp.float32)).astype(jnp.bfloat16)
+
+    sum_left = lax.ppermute(added(ahead[:, :half], far_left), "seq", up)
+    sum_right = lax.ppermute(added(behind[:, half:], far_right), "seq", down)
+    left = mine[:, :half] + near_left.astype(jnp.float32) + sum_left.astype(jnp.float32)
+    right = mine[:, half:] + near_right.astype(jnp.float32) + sum_right.astype(jnp.float32)
+    return jnp.concatenate([left, right], axis=1).astype(jnp.bfloat16)
+
+
+PRECISE = lax.Precision.HIGHEST
+
+
 def phase_table(period, out_size, in_size, direction):
     out_index = lax.broadcasted_iota(jnp.int32, (out_size, in_size), 0)
     in_index = lax.broadcasted_iota(jnp.int32, (out_size, in_size), 1)
@@ -32,11 +246,11 @@
 
 
 def left_apply(phase, signal):
-    return jnp.einsum("kn,cnm->ckm", phase, signal, precision=precise)
+    return jnp.einsum("kn,cnm->ckm", phase, signal, precision=PRECISE)
 
 
 def right_apply(signal, phase):
-    return jnp.einsum("ckn,nm->ckm", signal, phase, precision=precise)
+    return jnp.einsum("ckn,nm->ckm", signal, phase, precision=PRECISE)
 
 
 def forward_spectrum(signal, inner_size):
@@ -80,24 +294,18 @@
     return inverse_signal(prod_re, prod_im, length, inner_size)
 
 
-def shards(query_proj, key_proj, value_proj, short_taps, long_filters, out_weight):
-    tok_rows = query_proj.shape[1]
-    inner_size = tok_rows // 2
-    tail_cols = jnp.stack([query_proj[:, -2:], key_proj[:, -2:], value_proj[:, -2:]])
-    before = shifted(tail_cols, "seq", 1)
-    shorts = []
-    for stream_index, stream in enumerate((query_proj, key_proj, value_proj)):
-        extended = jnp.concatenate([before[stream_index], stream], axis=1).astype(jnp.float32)
-        shorts.append(short_filter(extended, short_taps[stream_index]))
-    query_short, key_short, value_short = shorts
+def by_whole_rows(query_proj, key_proj, value_proj, short_taps, long_filters, out_weight):
+    inner_size = query_proj.shape[1] // 2
+    query_short, key_short, value_short = filtered_streams(
+        (query_proj, key_proj, value_proj), short_taps
+    )
     product = (key_short * value_short).astype(jnp.bfloat16)
     spread = lax.all_to_all(product, "seq", split_axis=0, concat_axis=1, tiled=True)
     mixed_conv = long_convolve(spread.astype(jnp.float32), long_filters, inner_size)
     returned = lax.all_to_all(mixed_conv, "seq", split_axis=1, concat_axis=0, tiled=True)
     gated_out = (query_short * returned).astype(jnp.bfloat16)
-    full_rows = lax.all_gather(gated_out, "tp", axis=0, tiled=True)
     result = lax.dot_general(
-        full_rows,
+        lax.all_gather(gated_out, "tp", axis=0, tiled=True),
         lax.all_gather(out_weight, "seq", axis=0, tiled=True),
         (((0,), (0,)), ((), ())),
         preferred_element_type=jnp.float32,
@@ -106,8 +314,10 @@
 
 
 def solution(mesh):
+    planes, cores = mesh.shape["seq"] // PLANE, mesh.shape["tp"]
+    plan = by_planes if planes == PLANE and cores == 2 else by_whole_rows
     return jax.shard_map(
-        shards,
+        plan,
         mesh=mesh,
         in_specs=(
             P("tp", "seq"),

time: 522 us -> 226 us (0.43); the launches traced: 512 us -> 225 us
  waiting for transfers between devices: 385 us -> 123 us
  matrix products: 73.6 us -> 0 us
  Pallas kernels: 0 us -> 44.3 us
  starting transfers between devices: 18.4 us -> 32.8 us
  between operations: 13.9 us -> 0.29 us
  local copies, waits for them, and re-layouts: 10.5 us -> 16.5 us
    all_gather x2 -> x0, waiting for transfers between devices: 363 us -> none  [the longest x1 355 us: shards(): lax.all_gather(out_weight, 'seq', axis=0, tiled=True)]
    ppermute x0 -> x15, waiting for transfers between devices: none -> 79.3 us  [the longest x4 26.9 us: by_planes(): landed.append(lax.ppermute(message, ('seq', 'tp'), pairs))]
    dot_general x19 -> x0, matrix products: 73.6 us -> none  [the longest x12 42.7 us: right_apply(): return jnp.einsum('ckn,nm->ckm', signal, phase, precision=precise)]
    pallas_call x0 -> x4, Pallas kernels: none -> 44.3 us  [the longest x1 24.8 us: convolve_and_gate(): pl.pallas_call(conv_kernel, out_shape=[jax.ShapeDtypeStruct((blocks // in...]
    ppermute x1, waiting for transfers between devices: 0.01 us -> 34 us  [shifted(): lax.ppermute(value, axis, [(source, source + steps) for source in range(i...]
    ppermute x0 -> x15, starting transfers between devices: none -> 16.4 us  [the longest x4 4.16 us: by_planes(): landed.append(lax.ppermute(message, ('seq', 'tp'), pairs))]
    all_to_all x2, waiting for transfers between devices: 20.9 us -> 9.74 us  [spread(): lax.all_to_all(stream.reshape(seq_count, channels, width), 'seq', split_a...]
  transfers between devices with their start and end apart: 5 -> 18, of which waited for: 3 -> 10; matrix products, arithmetic and copies ran while one was open for 6% -> 10% of each run, Pallas kernels for 0% -> 17%
where the time goes in v1:
time: 226 us; the launch traced here: 225 us
  waiting for transfers between devices  123 us (54%)
  Pallas kernels  44.3 us (20%)
  starting transfers between devices  32.8 us (15%)
  local copies, waits for them, and re-layouts  16.5 us (7%)
  other arithmetic  7.78 us (3%)
    ppermute x1, waiting for transfers between devices, shifted(): lax.ppermute(value, axis, [(source, source + steps) for source in range(i...  34 us
    ppermute x4, waiting for transfers between devices, by_planes(): landed.append(lax.ppermute(message, ('seq', 'tp'), pairs))  26.9 us
    pallas_call x1, Pallas kernels, convolve_and_gate(): pl.pallas_call(conv_kernel, out_shape=[jax.ShapeDtypeStruct((blocks // in...  24.8 us
    ppermute x1, waiting for transfers between devices, by_planes(): sum_right = lax.ppermute(added(behind[:, half:], far_right), 'seq', down)  21.4 us
    pallas_call x3, Pallas kernels, project(): pl.pallas_call(functools.partial(project_kernel, len(steps)), out_shape=[...  19.5 us
    ppermute x1, waiting for transfers between devices, by_planes(): far_right = lax.ppermute(far[:, half:], 'seq', down)  14.6 us
    all_to_all x2, starting transfers between devices, spread(): lax.all_to_all(stream.reshape(seq_count, channels, width), 'seq', split_a...  14 us
    ppermute x1, waiting for transfers between devices, by_planes(): near_left = lax.ppermute(behind[:, :half], 'seq', down)  13.8 us
  transfers between devices with their start and end apart: 18, of which 10 were waited for; matrix products, arithmetic and copies ran while one was open for 10% of the time, Pallas kernels for 17%

profile of v1, /device:TPU:0, one launch (start us, length us, event | category | flops | bytes accessed | tf_op | source)
XLA Modules:
  0.0 224.6 jit_solution(9088564231522676292)
XLA Ops:
  0.0 3.0 %collective-permute-start.7 = (bf16[256,4096]{1,0:T(8,128)(2,1)}, bf16[256,4096]{1,0:T(8,128)(2,1)S(1)}, u32[]{:S(2)}, u32[]{:S(2)}) collective-permute-start(bf16[256,4096]{1,0:T(8,128)(2,1)} %refs_8_.3), channel_id=1, source_target_pairs={{0,4},{2,6},{4,0},{6,2},{8,12},{10,14},{12,8},{14,10},{16,20},{18,... | collective-permute-start | bytes 6291464 | tf_op jit(solution)/shard_map/ppermute | solution.py:191
  3.0 1.5 collective-permute-start.6
  4.5 2.0 slice.98
  6.5 1.3 copy.15
  7.8 2.0 slice.99
  9.9 1.2 copy.16
  11.2 2.4 %collective-permute-start = (bf16[2,2048,2]{1,2,0:T(2,128)(2,1)S(1)}, bf16[2,2048,2]{1,2,0:T(2,128)(2,1)S(1)}, u32[]{:S(2)}, u32[]{:S(2)}) collective-permute-start(bf16[2,2048,2]{1,2,0:T(2,128)(2,1)S(1)} %pad_maximum_fusion.3), channel_id=1, source_target_pairs={{0,2},{2,4},{4,6},{6,8},{8,10},{10,12},{12,14},{14,16},{16,18},{18... | collective-permute-start | bytes 49160 | tf_op jit(solution)/shard_map/ppermute | solution.py:18
  13.6 6.9 %all-to-all-start.1 = ((bf16[16,128,128]{2,1,0:T(8,128)(2,1)}), bf16[16,128,128]{2,1,0:T(8,128)(2,1)}, u32[]{:S(2)}, u32[]{:S(2)}) async-start(bf16[16,128,128]{2,1,0:T(8,128)(2,1)} %bitcast.38), calls=%async_computation.1 | async-start | bytes 1048576 | tf_op jit(solution)/shard_map/all_to_all | solution.py:185
  20.6 34.0 %collective-permute-done = bf16[2,2048,2]{1,2,0:T(2,128)(2,1)S(1)} collective-permute-done((bf16[2,2048,2]{1,2,0:T(2,128)(2,1)S(1)}, bf16[2,2048,2]{1,2,0:T(2,128)(2,1)S(1)}, u32[]{:S(2)}, u32[]{:S(2)}) %collective-permute-start) | collective-permute-done | bytes 16416 | tf_op jit(solution)/shard_map/ppermute | solution.py:18
  54.6 1.1 copy.18
  55.6 1.1 copy.17
  56.7 2.0 maximum_convert_fusion
  58.7 3.7 %fusion.6 = bf16[2048,128]{1,0:T(8,128)(2,1)} fusion(f32[2048,130]{1,0:T(8,128)S(1)} %get-tuple-element.32, f32[2048,130]{1,0:T(8,128)S(1)} %get-tuple-element.31, f32[2048]{0:T(1024)S(1)} %bitcast.48, f32[2048]{0:T(1024)S(1)} %bitcast.49, f32[2048]{0:T(1024)S(1)} %bitcast.45, f32[2048]{0:T(1024)S(1)} %bitcast.46, f32[2048]{0:T(1024)S(1)} %bitcast.47, ...), kind=kLoop, calls=%fused_computation.9 | loop fusion | flops 3145728 | bytes 6864896 | tf_op jit(solution)/shard_map/convert_element_type | solution.py:199
  62.4 7.1 %all-to-all-start = ((bf16[16,128,128]{2,1,0:T(8,128)(2,1)}), bf16[16,128,128]{2,1,0:T(8,128)(2,1)}, u32[]{:S(2)}, u32[]{:S(2)}) async-start(bf16[16,128,128]{2,1,0:T(8,128)(2,1)} %bitcast.14), calls=%async_computation | async-start | bytes 1048576 | tf_op jit(solution)/shard_map/all_to_all | solution.py:185
  69.5 1.4 copy.19
  71.0 2.2 copy.22
  73.2 9.7 %all-to-all-done = bf16[16,128,128]{2,1,0:T(8,128)(2,1)} async-done(((bf16[16,128,128]{2,1,0:T(8,128)(2,1)}), bf16[16,128,128]{2,1,0:T(8,128)(2,1)}, u32[]{:S(2)}, u32[]{:S(2)}) %all-to-all-start) | async-done | bytes 524320 | tf_op jit(solution)/shard_map/all_to_all | solution.py:185
  82.9 1.4 copy.23
  84.3 1.0 copy-done.1
  85.3 24.8 %shard_map.64 = (bf16[4,128,128]{2,1,0:T(8,128)(2,1)S(1)}, bf16[4,128,128]{2,1,0:T(8,128)(2,1)S(1)}, bf16[4,128,128]{2,1,0:T(8,128)(2,1)S(1)}, bf16[4,128,128]{2,1,0:T(8,128)(2,1)S(1)}) custom-call(s32[3]{0:T(128)S(1)} %pad_add_fusion.place_ref, f32[3,128]{1,0:T(4,128)S(1)} %dynamic-slice_bitcast_fusion.taps_ref, bf16[128,16,128]{2,1,0:T(8,128)(2,1)S(1)} %bitcast.34, ...), custom_call_target="tpu_custom_call" | custom-call | flops 1073741824 | bytes 3145728 | tf_op jit(solution)/shard_map/pallas_call | solution.py:99
  110.2 0.7 collective-permute-start.1
  111.0 0.6 collective-permute-start.8
  111.6 1.3 slice.132
  112.9 1.0 collective-permute-start.9
  113.9 1.5 collective-permute-start.2
  115.4 1.1 collective-permute-start.3
  116.5 0.9 collective-permute-start.4
  117.4 23.9 %collective-permute-done.2 = bf16[4,128,128]{2,1,0:T(8,128)(2,1)S(1)} collective-permute-done((bf16[4,128,128]{2,1,0:T(8,128)(2,1)S(1)}, bf16[4,128,128]{2,1,0:T(8,128)(2,1)S(1)}, u32[]{:S(2)}, u32[]{:S(2)}) %collective-permute-start.2) | collective-permute-done | bytes 131104 | tf_op jit(solution)/shard_map/ppermute | solution.py:212
  141.3 3.0 %collective-permute-done.3 = bf16[4,128,128]{2,1,0:T(8,128)(2,1)S(1)} collective-permute-done((bf16[4,128,128]{2,1,0:T(8,128)(2,1)S(1)}, bf16[4,128,128]{2,1,0:T(8,128)(2,1)S(1)}, u32[]{:S(2)}, u32[]{:S(2)}) %collective-permute-start.3) | collective-permute-done | bytes 131104 | tf_op jit(solution)/shard_map/ppermute | solution.py:212
  144.4 1.9 collective-permute-done.5
  146.3 0.1 pad_maximum_fusion.refs_0_.refs_1_.refs_2_.refs_3_.refs_4_.refs_5_.refs_6_.refs_7_.refs_8_.refs_9_.refs_10_.refs_11_.refs_12_.refs_13_.refs_14_.refs_15_
  146.5 6.2 %shard_map.67 = bf16[128,4096]{1,0:T(8,128)(2,1)S(1)} custom-call(s32[3]{0:T(128)S(1)} %pad_add_fusion.place_ref, bf16[2,4,4,128,128]{4,3,2,1,0:T(8,128)(2,1)S(1)} %pad_maximum_fusion.refs_0_.refs_1_.refs_2_.refs_3_.refs_4_.refs_5_.refs_6_.refs_7_.refs_8_.refs_9_.refs_10_.refs_11_.refs_12_.refs_13_.refs_14_.refs_15_, ...), custom_call_target="tpu_custom_call" | custom-call | flops 1073741824 | bytes 10485760 | tf_op jit(solution)/shard_map/pallas_call | solution.py:153
  152.7 0.1 fusion.11
  152.9 2.0 collective-permute-start.11
  154.9 7.0 %shard_map.66 = (bf16[128,4096]{1,0:T(8,128)(2,1)S(1)}, bf16[128,4096]{1,0:T(8,128)(2,1)S(1)}) custom-call(s32[3]{0:T(128)S(1)} %pad_add_fusion.place_ref, bf16[2,4,4,128,128]{4,3,2,1,0:T(8,128)(2,1)S(1)} %pad_maximum_fusion.refs_0_.refs_1_.refs_2_.refs_3_.refs_4_.refs_5_.refs_6_.refs_7_.refs_8_.refs_9_.refs_10_.refs_11_.refs_12_.refs_13_.refs_14_.refs_15_, ...), custom_call_target="tpu_custom_call" | custom-call | flops 2147483648 | bytes 12582912 | tf_op jit(solution)/shard_map/pallas_call | solution.py:153
  161.9 1.9 collective-permute-start.10
  163.9 0.2 collective-permute-start.13
  164.1 14.6 %collective-permute-done.14 = bf16[128,2048]{1,0:T(8,128)(2,1)S(1)} collective-permute-done((bf16[128,2048]{1,0:T(8,128)(2,1)S(1)}, bf16[128,2048]{1,0:T(8,128)(2,1)S(1)}, u32[]{:S(2)}, u32[]{:S(2)}) %collective-permute-start.14) | collective-permute-done | bytes 524320 | tf_op jit(solution)/shard_map/ppermute | solution.py:220
  178.7 0.1 add_convert_fusion
  178.9 0.3 collective-permute-done.11
  179.1 0.1 add_convert_fusion.1
  179.3 1.8 collective-permute-start.12
  181.1 6.3 %shard_map.65 = f32[128,4096]{1,0:T(8,128)S(1)} custom-call(s32[3]{0:T(128)S(1)} %pad_add_fusion.place_ref, bf16[2,4,4,128,128]{4,3,2,1,0:T(8,128)(2,1)S(1)} %pad_maximum_fusion.refs_0_.refs_1_.refs_2_.refs_3_.refs_4_.refs_5_.refs_6_.refs_7_.refs_8_.refs_9_.refs_10_.refs_11_.refs_12_.refs_13_.refs_14_.refs_15_, ...), custom_call_target="tpu_custom_call" | custom-call | flops 1073741824 | bytes 10485760 | tf_op jit(solution)/shard_map/pallas_call | solution.py:153
  187.3 13.8 %collective-permute-done.10 = bf16[128,2048]{1,0:T(8,128)(2,1)S(1)} collective-permute-done((bf16[128,2048]{1,0:T(8,128)(2,1)S(1)}, bf16[128,2048]{1,0:T(8,128)(2,1)S(1)}, u32[]{:S(2)}, u32[]{:S(2)}) %collective-permute-start.10) | collective-permute-done | bytes 524320 | tf_op jit(solution)/shard_map/ppermute | solution.py:223
  201.1 0.6 collective-permute-done.13
  201.6 21.4 %collective-permute-done.15 = bf16[128,2048]{1,0:T(8,128)(2,1)S(1)} collective-permute-done((bf16[128,2048]{1,0:T(8,128)(2,1)S(1)}, bf16[128,2048]{1,0:T(8,128)(2,1)S(1)}, u32[]{:S(2)}, u32[]{:S(2)}) %collective-permute-start.15) | collective-permute-done | bytes 524320 | tf_op jit(solution)/shard_map/ppermute | solution.py:230
  223.0 0.5 fusion.3
  223.5 1.1 pad_maximum_fusion.1
  (31 shorter events, 0.7 us)
Async XLA Ops:
  0.0 20.5 %copy-start.4 = (f32[3,3,2048]{2,1,0:T(4,128)S(1)}, f32[3,3,2048]{2,1,0:T(4,128)}, u32[]{:S(2)}) copy-start(f32[3,3,2048]{2,1,0:T(4,128)} %param.9) | copy-start | bytes 221188
  0.0 110.9 %collective-permute-start.7 = (bf16[256,4096]{1,0:T(8,128)(2,1)}, bf16[256,4096]{1,0:T(8,128)(2,1)S(1)}, u32[]{:S(2)}, u32[]{:S(2)}) collective-permute-start(bf16[256,4096]{1,0:T(8,128)(2,1)} %refs_8_.3), channel_id=1, source_target_pairs={{0,4},{2,6},{4,0},{6,2},{8,12},{10,14},{12,8},{14,10},{16,20},{18,... | collective-permute-start | bytes 6291464 | tf_op jit(solution)/shard_map/ppermute | solution.py:191
  3.0 108.6 %collective-permute-start.6 = (bf16[256,4096]{1,0:T(8,128)(2,1)}, bf16[256,4096]{1,0:T(8,128)(2,1)}, u32[]{:S(2)}, u32[]{:S(2)}) collective-permute-start(bf16[256,4096]{1,0:T(8,128)(2,1)} %refs_8_.3), channel_id=1, source_target_pairs={{0,2},{2,0},{4,6},{6,4},{8,10},{10,8},{12,14},{14,12},{16,18},{18,... | collective-permute-start | bytes 6291464 | tf_op jit(solution)/shard_map/ppermute | solution.py:190
  6.5 50.2 %copy-start.2 = (bf16[2048,128]{1,0:T(8,128)(2,1)S(1)}, bf16[2048,128]{1,0:T(8,128)(2,1)}, u32[]{:S(2)}) copy-start(bf16[2048,128]{1,0:T(8,128)(2,1)} %param.7) | copy-start | bytes 1572868
  6.5 50.2 %copy-start.3 = (bf16[2048,128]{1,0:T(8,128)(2,1)S(1)}, bf16[2048,128]{1,0:T(8,128)(2,1)}, u32[]{:S(2)}) copy-start(bf16[2048,128]{1,0:T(8,128)(2,1)} %param.8) | copy-start | bytes 1572868
  11.2 43.4 %collective-permute-start = (bf16[2,2048,2]{1,2,0:T(2,128)(2,1)S(1)}, bf16[2,2048,2]{1,2,0:T(2,128)(2,1)S(1)}, u32[]{:S(2)}, u32[]{:S(2)}) collective-permute-start(bf16[2,2048,2]{1,2,0:T(2,128)(2,1)S(1)} %pad_maximum_fusion.3), channel_id=1, source_target_pairs={{0,2},{2,4},{4,6},{6,8},{8,10},{10,12},{12,14},{14,16},{16,18},{18... | collective-permute-start | bytes 49160 | tf_op jit(solution)/shard_map/ppermute | solution.py:18
  13.6 48.7 %all-to-all-start.1 = ((bf16[16,128,128]{2,1,0:T(8,128)(2,1)}), bf16[16,128,128]{2,1,0:T(8,128)(2,1)}, u32[]{:S(2)}, u32[]{:S(2)}) async-start(bf16[16,128,128]{2,1,0:T(8,128)(2,1)} %bitcast.38), calls=%async_computation.1 | async-start | bytes 1048576 | tf_op jit(solution)/shard_map/all_to_all | solution.py:185
  62.4 8.6 %slice-start = ((f32[3,3,2048]{2,1,0:T(4,128)}), f32[1,3,2048]{2,1,0:T(4,128)S(1)}, s32[]{:S(2)}) async-start(f32[3,3,2048]{2,1,0:T(4,128)} %param.9), calls=%async_computation.2 | async-start | bytes 65536 | tf_op jit(solution)/shard_map/slice | solution.py:200
  62.4 20.5 %all-to-all-start = ((bf16[16,128,128]{2,1,0:T(8,128)(2,1)}), bf16[16,128,128]{2,1,0:T(8,128)(2,1)}, u32[]{:S(2)}, u32[]{:S(2)}) async-start(bf16[16,128,128]{2,1,0:T(8,128)(2,1)} %bitcast.14), calls=%async_computation | async-start | bytes 1048576 | tf_op jit(solution)/shard_map/all_to_all | solution.py:185
  84.3 1.0 copy-start.1
  110.2 6.3 %collective-permute-start.1 = (bf16[4,128,128]{2,1,0:T(8,128)(2,1)S(1)}, bf16[4,128,128]{2,1,0:T(8,128)(2,1)S(1)}, u32[]{:S(2)}, u32[]{:S(2)}) collective-permute-start(bf16[4,128,128]{2,1,0:T(8,128)(2,1)S(1)} %get-tuple-element.11), channel_id=1, source_target_pairs={{0,0},{1,16},{2,2},{3,18},{4,4},{5,20},{6,6},{7,22},{8,1},{9,17},{... | collective-permute-start | bytes 393224 | tf_op jit(solution)/shard_map/ppermute | solution.py:212
  111.0 35.5 %collective-permute-start.8 = (bf16[128,4096]{1,0:T(8,128)(2,1)S(1)}, bf16[128,4096]{1,0:T(8,128)(2,1)S(1)}, u32[]{:S(2)}, u32[]{:S(2)}) collective-permute-start(bf16[128,4096]{1,0:T(8,128)(2,1)S(1)} %slice.131), channel_id=1, source_target_pairs={{0,2},{2,0},{4,6},{6,4},{8,10},{10,8},{12,14},{14,12},{16,18},{18,... | collective-permute-start | bytes 3145736 | tf_op jit(solution)/shard_map/ppermute | solution.py:193
  112.9 33.5 %copy-start = (bf16[256,4096]{1,0:T(8,128)(2,1)S(1)}, bf16[256,4096]{1,0:T(8,128)(2,1)}, u32[]{:S(2)}) copy-start(bf16[256,4096]{1,0:T(8,128)(2,1)} %refs_8_.3) | copy-start | bytes 6291460
  112.9 33.5 %collective-permute-start.9 = (bf16[128,4096]{1,0:T(8,128)(2,1)S(1)}, bf16[128,4096]{1,0:T(8,128)(2,1)S(1)}, u32[]{:S(2)}, u32[]{:S(2)}) collective-permute-start(bf16[128,4096]{1,0:T(8,128)(2,1)S(1)} %slice.132), channel_id=1, source_target_pairs={{0,4},{2,6},{4,0},{6,2},{8,12},{10,14},{12,8},{14,10},{16,20},{18,... | collective-permute-start | bytes 3145736 | tf_op jit(solution)/shard_map/ppermute | solution.py:194
  113.9 27.4 %collective-permute-start.2 = (bf16[4,128,128]{2,1,0:T(8,128)(2,1)S(1)}, bf16[4,128,128]{2,1,0:T(8,128)(2,1)S(1)}, u32[]{:S(2)}, u32[]{:S(2)}) collective-permute-start(bf16[4,128,128]{2,1,0:T(8,128)(2,1)S(1)} %get-tuple-element.12), channel_id=1, source_target_pairs={{0,2},{1,18},{2,0},{3,16},{4,6},{5,22},{6,4},{7,20},{8,3},{9,19},{... | collective-permute-start | bytes 393224 | tf_op jit(solution)/shard_map/ppermute | solution.py:212
  115.4 28.9 %collective-permute-start.3 = (bf16[4,128,128]{2,1,0:T(8,128)(2,1)S(1)}, bf16[4,128,128]{2,1,0:T(8,128)(2,1)S(1)}, u32[]{:S(2)}, u32[]{:S(2)}) collective-permute-start(bf16[4,128,128]{2,1,0:T(8,128)(2,1)S(1)} %get-tuple-element.13), channel_id=1, source_target_pairs={{0,4},{1,20},{2,6},{3,22},{4,0},{5,16},{6,2},{7,18},{8,5},{9,21},{... | collective-permute-start | bytes 393224 | tf_op jit(solution)/shard_map/ppermute | solution.py:212
  116.5 27.8 %collective-permute-start.4 = (bf16[4,128,128]{2,1,0:T(8,128)(2,1)S(1)}, bf16[4,128,128]{2,1,0:T(8,128)(2,1)S(1)}, u32[]{:S(2)}, u32[]{:S(2)}) collective-permute-start(bf16[4,128,128]{2,1,0:T(8,128)(2,1)S(1)} %get-tuple-element.14), channel_id=1, source_target_pairs={{0,6},{1,22},{2,4},{3,20},{4,2},{5,18},{6,0},{7,16},{8,7},{9,23},{... | collective-permute-start | bytes 393224 | tf_op jit(solution)/shard_map/ppermute | solution.py:212
  144.4 2.0 collective-permute-start.5
  152.8 25.8 %collective-permute-start.14 = (bf16[128,2048]{1,0:T(8,128)(2,1)S(1)}, bf16[128,2048]{1,0:T(8,128)(2,1)S(1)}, u32[]{:S(2)}, u32[]{:S(2)}) collective-permute-start(bf16[128,2048]{1,0:T(8,128)(2,1)S(1)} %get-tuple-element.20), channel_id=1, source_target_pairs={{8,0},{10,2},{12,4},{14,6},{16,8},{18,10},{20,12},{22,14},{24,16},... | collective-permute-start | bytes 1572872 | tf_op jit(solution)/shard_map/ppermute | solution.py:220
  152.9 26.2 %collective-permute-start.11 = (bf16[128,2048]{1,0:T(8,128)(2,1)S(1)}, bf16[128,2048]{1,0:T(8,128)(2,1)S(1)}, u32[]{:S(2)}, u32[]{:S(2)}) collective-permute-start(bf16[128,2048]{1,0:T(8,128)(2,1)S(1)} %get-tuple-element.19), channel_id=1, source_target_pairs={{0,8},{2,10},{4,12},{6,14},{8,16},{10,18},{12,20},{14,22},{16,24},... | collective-permute-start | bytes 1572872 | tf_op jit(solution)/shard_map/ppermute | solution.py:219
  161.9 39.2 %collective-permute-start.10 = (bf16[128,2048]{1,0:T(8,128)(2,1)S(1)}, bf16[128,2048]{1,0:T(8,128)(2,1)S(1)}, u32[]{:S(2)}, u32[]{:S(2)}) collective-permute-start(bf16[128,2048]{1,0:T(8,128)(2,1)S(1)} %slice.116), channel_id=1, source_target_pairs={{8,0},{10,2},{12,4},{14,6},{16,8},{18,10},{20,12},{22,14},{24,16},... | collective-permute-start | bytes 1572872 | tf_op jit(solution)/shard_map/ppermute | solution.py:223
  163.9 37.7 %collective-permute-start.13 = (bf16[128,2048]{1,0:T(8,128)(2,1)S(1)}, bf16[128,2048]{1,0:T(8,128)(2,1)S(1)}, u32[]{:S(2)}, u32[]{:S(2)}) collective-permute-start(bf16[128,2048]{1,0:T(8,128)(2,1)S(1)} %slice.120), channel_id=1, source_target_pairs={{0,8},{2,10},{4,12},{6,14},{8,16},{10,18},{12,20},{14,22},{16,24},... | collective-permute-start | bytes 1572872 | tf_op jit(solution)/shard_map/ppermute | solution.py:222
  178.8 44.2 %collective-permute-start.15 = (bf16[128,2048]{1,0:T(8,128)(2,1)S(1)}, bf16[128,2048]{1,0:T(8,128)(2,1)S(1)}, u32[]{:S(2)}, u32[]{:S(2)}) collective-permute-start(bf16[128,2048]{1,0:T(8,128)(2,1)S(1)} %add_convert_fusion), channel_id=1, source_target_pairs={{8,0},{10,2},{12,4},{14,6},{16,8},{18,10},{20,12},{22,14},{24,16},... | collective-permute-start | bytes 1572872 | tf_op jit(solution)/shard_map/ppermute | solution.py:230
  179.3 43.8 %collective-permute-start.12 = (bf16[128,2048]{1,0:T(8,128)(2,1)S(1)}, bf16[128,2048]{1,0:T(8,128)(2,1)S(1)}, u32[]{:S(2)}, u32[]{:S(2)}) collective-permute-start(bf16[128,2048]{1,0:T(8,128)(2,1)S(1)} %add_convert_fusion.1), channel_id=1, source_target_pairs={{0,8},{2,10},{4,12},{6,14},{8,16},{10,18},{12,20},{14,22},{16,24},... | collective-permute-start | bytes 1572872 | tf_op jit(solution)/shard_map/ppermute | solution.py:229

commit v2 on v1

--- a/solution.py
+++ b/solution.py
@@ -115,48 +115,39 @@
 
 
 def project_kernel(pieces, place_ref, *refs):
-    gates, weights, outs = refs[: 8 * pieces], refs[8 * pieces : -pieces], refs[-pieces:]
-    tiles = [ref[...] for ref in weights[:3]] + [
-        jnp.concatenate([weights[3][...], weights[4][...]], axis=0)
-    ]
-    depth = tiles[0].shape[0] // 2
+    gates, weight, outs = refs[: 8 * pieces], refs[8 * pieces], refs[-pieces:]
+    depth = weight.shape[0] // 8
     for piece in range(pieces):
         mine = [ref[...].reshape(-1, depth) for ref in gates[8 * piece : 8 * piece + 8]]
-        total = None
-        for index, tile in enumerate(tiles):
-            left = jnp.concatenate([mine[2 * index], mine[2 * index + 1]], axis=1)
-            term = jnp.dot(left, tile, preferred_element_type=jnp.float32)
-            total = term if total is None else total + term
+        total = jnp.dot(
+            jnp.concatenate(mine, axis=1), weight[...], preferred_element_type=jnp.float32
+        )
         outs[piece][...] = total.astype(outs[piece].dtype)
 
 
-def project(place, gates, weights, steps, dtype, tile=512):
+def project(place, gates, weight, steps, dtype, tile=512):
     _, _, planes, rows, depth = gates.shape
-    columns = weights[0].shape[1]
-
-    def gate_spec(step, offset, half):
+    columns = weight.shape[1]
+
+    def gate_spec(step, owner, half):
         def index(column, place_ref):
             inner, outer, core = place_ref[0], place_ref[1], place_ref[2]
-            owner = inner ^ offset
             source = 2 * (owner % 2) + half
             return ((owner // 2) ^ core, source ^ inner, (outer + step) % planes, 0, 0)
 
         return pl.BlockSpec((1, 1, 1, rows, depth), index)
 
     gate_specs = [
-        gate_spec(step, offset, half) for step in steps for offset in range(PLANE) for half in range(2)
+        gate_spec(step, owner, half) for step in steps for owner in range(PLANE) for half in range(2)
     ]
-    weight_specs = [
-        pl.BlockSpec((weight.shape[0], tile), lambda column, place_ref: (0, column))
-        for weight in weights
-    ]
+    weight_spec = pl.BlockSpec((weight.shape[0], tile), lambda column, place_ref: (0, column))
     return pl.pallas_call(
         functools.partial(project_kernel, len(steps)),
         out_shape=[jax.ShapeDtypeStruct((rows, columns), dtype)] * len(steps),
         grid_spec=pltpu.PrefetchScalarGridSpec(
             num_scalar_prefetch=1,
             grid=(columns // tile,),
-            in_specs=gate_specs + weight_specs,
+            in_specs=gate_specs + [weight_spec],
             out_specs=[pl.BlockSpec((rows, tile), lambda column, place_ref: (0, column))] * len(steps),
         ),
         compiler_params=pltpu.CompilerParams(vmem_limit_bytes=VMEM_LIMIT),
@@ -165,7 +156,7 @@
             bytes_accessed=16 * depth * columns + 4 * len(steps) * rows * columns,
             transcendentals=0,
         ),
-    )(place, *[gates] * len(gate_specs), *weights)
+    )(place, *[gates] * len(gate_specs), weight)
 
 
 def by_planes(query_proj, key_proj, value_proj, short_taps, long_filters, out_weight):
@@ -176,8 +167,6 @@
     place = jnp.stack([inner, outer, core]).astype(jnp.int32)
     channels, width = long_filters.shape[0], query_proj.shape[1]
 
-    across = [(source, source ^ 1) for source in range(seq_count)]
-    along = [(source, source ^ 2) for source in range(seq_count)]
     up = [(source, (source + PLANE) % seq_count) for source in range(seq_count)]
     down = [(target, source) for source, target in up]
 
@@ -187,12 +176,8 @@
         )
         return parts.transpose(1, 0, 2)
 
-    weight_x = lax.ppermute(out_weight, "seq", across)
-    weight_y = lax.ppermute(out_weight, "seq", along)
-    half_rows = out_weight.shape[0] // 2
-    weight_top = lax.ppermute(weight_y[:half_rows], "seq", across)
-    weight_end = lax.ppermute(weight_x[half_rows:], "seq", along)
-    weights = [out_weight, weight_x, weight_y, weight_top, weight_end]
+    groups = [list(range(first, first + PLANE)) for first in range(0, seq_count, PLANE)]
+    weight = lax.all_gather(out_weight, "seq", axis=0, tiled=True, axis_index_groups=groups)
 
     query = spread(query_proj)
     key_short, value_short = filtered_streams((key_proj, value_proj), short_taps[1:])
@@ -214,14 +199,14 @@
     other = lax.ppermute(own, "tp", [(0, 1), (1, 0)])
     gates = jnp.stack([own, other])
 
-    (far,) = project(place, gates, weights, (2,), jnp.bfloat16)
+    (far,) = project(place, gates, weight, (2,), jnp.bfloat16)
     half = far.shape[1] // 2
     far_left = lax.ppermute(far[:, :half], "seq", up)
     far_right = lax.ppermute(far[:, half:], "seq", down)
-    ahead, behind = project(place, gates, weights, (1, planes - 1), jnp.bfloat16)
+    ahead, behind = project(place, gates, weight, (1, planes - 1), jnp.bfloat16)
     near_right = lax.ppermute(ahead[:, half:], "seq", up)
     near_left = lax.ppermute(behind[:, :half], "seq", down)
-    (mine,) = project(place, gates, weights, (0,), jnp.float32)
+    (mine,) = project(place, gates, weight, (0,), jnp.float32)
 
     def added(first, second):
         return (first.astype(jnp.float32) + second.astype(jnp.float32)).astype(jnp.bfloat16)

time: 226 us -> 202 us (0.89)
  waiting for transfers between devices: 123 us -> 105 us
  between operations: 0.29 us -> 13.7 us
  local copies, waits for them, and re-layouts: 16.5 us -> 6.31 us
  Pallas kernels: 44.3 us -> 37.5 us
    ppermute x1, waiting for transfers between devices: 34 us -> 0.01 us  [shifted(): lax.ppermute(value, axis, [(source, source + steps) for source in range(i...]
    all_gather x0 -> x1, waiting for transfers between devices: none -> 18 us  [by_planes(): lax.all_gather(out_weight, 'seq', axis=0, tiled=True, axis_index_groups=g...]
    ppermute x4, waiting for transfers between devices: 26.9 us -> 11.7 us  [by_planes(): landed.append(lax.ppermute(message, ('seq', 'tp'), pairs))]
    all_to_all x2, waiting for transfers between devices: 9.74 us -> 23.4 us  [spread(): lax.all_to_all(stream.reshape(seq_count, channels, width), 'seq', split_a...]
    ppermute x1, waiting for transfers between devices: 0.55 us -> 12.2 us  [by_planes(): near_right = lax.ppermute(ahead[:, half:], 'seq', up)]
    ppermute x1, waiting for transfers between devices: 14.6 us -> 3.31 us  [by_planes(): far_right = lax.ppermute(far[:, half:], 'seq', down)]
    ppermute x1, waiting for transfers between devices: 21.4 us -> 10.3 us  [by_planes(): sum_right = lax.ppermute(added(behind[:, half:], far_right), 'seq', down)]
    ppermute x1, waiting for transfers between devices: 0.01 us -> 11 us  [by_planes(): sum_left = lax.ppermute(added(ahead[:, :half], far_left), 'seq', up)]
  transfers between devices with their start and end apart: 18 -> 15, of which waited for: 10 -> 13; matrix products, arithmetic and copies ran while one was open for 10% -> 4% of each run, Pallas kernels for 17% -> 17%
where the time goes in v2:
time: 202 us; the launch traced here: 201 us
  waiting for transfers between devices  105 us (52%)
  Pallas kernels  37.5 us (19%)
  starting transfers between devices  32.3 us (16%)
  between operations  13.7 us (7%)
  other arithmetic  6.56 us (3%)
  local copies, waits for them, and re-layouts  6.31 us (3%)
    pallas_call x1, Pallas kernels, convolve_and_gate(): pl.pallas_call(conv_kernel, out_shape=[jax.ShapeDtypeStruct((blocks // in...  24.8 us
    all_to_all x2, waiting for transfers between devices, spread(): lax.all_to_all(stream.reshape(seq_count, channels, width), 'seq', split_a...  23.4 us
    all_gather x1, waiting for transfers between devices, by_planes(): lax.all_gather(out_weight, 'seq', axis=0, tiled=True, axis_index_groups=g...  18 us
    pallas_call x3, Pallas kernels, project(): pl.pallas_call(functools.partial(project_kernel, len(steps)), out_shape=[...  12.7 us
    ppermute x1, waiting for transfers between devices, by_planes(): near_right = lax.ppermute(ahead[:, half:], 'seq', up)  12.2 us
    ppermute x4, waiting for transfers between devices, by_planes(): landed.append(lax.ppermute(message, ('seq', 'tp'), pairs))  11.7 us
    ppermute x1, waiting for transfers between devices, by_planes(): sum_left = lax.ppermute(added(ahead[:, :half], far_left), 'seq', up)  11 us
    ppermute x1, waiting for transfers between devices, by_planes(): sum_right = lax.ppermute(added(behind[:, half:], far_right), 'seq', down)  10.3 us
  transfers between devices with their start and end apart: 15, of which 13 were waited for; matrix products, arithmetic and copies ran while one was open for 4% of the time, Pallas kernels for 17%

profile of v2, /device:TPU:0, one launch (start us, length us, event | category | flops | bytes accessed | tf_op | source)
XLA Modules:
  0.0 201.4 jit_solution(15244951146169395123)
XLA Ops:
  6.5 0.7 all-gather.2.cloned.1.call-update
  7.3 0.3 copy-done.1
  7.6 0.2 slice.92
  7.8 0.2 copy.15
  8.0 0.2 slice.93
  8.2 0.2 copy.16
  8.5 4.8 %collective-permute-start = (bf16[2,2048,2]{1,2,0:T(2,128)(2,1)S(1)}, bf16[2,2048,2]{1,2,0:T(2,128)(2,1)S(1)}, u32[]{:S(2)}, u32[]{:S(2)}) collective-permute-start(bf16[2,2048,2]{1,2,0:T(2,128)(2,1)S(1)} %pad_maximum_fusion.3), channel_id=1, source_target_pairs={{0,2},{2,4},{4,6},{6,8},{8,10},{10,12},{12,14},{14,16},{16,18},{18... | collective-permute-start | bytes 49160 | tf_op jit(solution)/shard_map/ppermute | solution.py:18
  13.3 6.0 %all-to-all-start.1 = ((bf16[16,128,128]{2,1,0:T(8,128)(2,1)}), bf16[16,128,128]{2,1,0:T(8,128)(2,1)S(1)}, u32[]{:S(2)}, u32[]{:S(2)}) async-start(bf16[16,128,128]{2,1,0:T(8,128)(2,1)} %bitcast.16), calls=%async_computation.1 | async-start | bytes 1048576 | tf_op jit(solution)/shard_map/all_to_all | solution.py:174
  19.4 0.3 copy.18
  19.7 0.3 copy.17
  20.0 0.8 maximum_convert_fusion
  20.8 3.7 %fusion.6 = bf16[2048,128]{1,0:T(8,128)(2,1)} fusion(f32[2048,130]{1,0:T(8,128)S(1)} %get-tuple-element.32, f32[2048,130]{1,0:T(8,128)S(1)} %get-tuple-element.31, f32[2048]{0:T(1024)S(1)} %bitcast.47, f32[2048]{0:T(1024)S(1)} %bitcast.48, f32[2048]{0:T(1024)S(1)} %bitcast.44, f32[2048]{0:T(1024)S(1)} %bitcast.45, f32[2048]{0:T(1024)S(1)} %bitcast.46, ...), kind=kLoop, calls=%fused_computation.9 | loop fusion | flops 3145728 | bytes 6864896 | tf_op jit(solution)/shard_map/convert_element_type | solution.py:184
  24.5 9.7 %all-to-all-done.1 = bf16[16,128,128]{2,1,0:T(8,128)(2,1)S(1)} async-done(((bf16[16,128,128]{2,1,0:T(8,128)(2,1)}), bf16[16,128,128]{2,1,0:T(8,128)(2,1)S(1)}, u32[]{:S(2)}, u32[]{:S(2)}) %all-to-all-start.1) | async-done | bytes 524320 | tf_op jit(solution)/shard_map/all_to_all | solution.py:174
  34.3 4.0 %all-to-all-start = ((bf16[16,128,128]{2,1,0:T(8,128)(2,1)}), bf16[16,128,128]{2,1,0:T(8,128)(2,1)S(1)}, u32[]{:S(2)}, u32[]{:S(2)}) async-start(bf16[16,128,128]{2,1,0:T(8,128)(2,1)} %bitcast.14), calls=%async_computation | async-start | bytes 1048576 | tf_op jit(solution)/shard_map/all_to_all | solution.py:174
  38.3 0.2 copy.19
  38.6 0.3 copy.22
  38.9 13.7 %all-to-all-done = bf16[16,128,128]{2,1,0:T(8,128)(2,1)S(1)} async-done(((bf16[16,128,128]{2,1,0:T(8,128)(2,1)}), bf16[16,128,128]{2,1,0:T(8,128)(2,1)S(1)}, u32[]{:S(2)}, u32[]{:S(2)}) %all-to-all-start) | async-done | bytes 524320 | tf_op jit(solution)/shard_map/all_to_all | solution.py:174
  52.6 0.3 copy.23
  53.0 24.8 %shard_map.64 = (bf16[4,128,128]{2,1,0:T(8,128)(2,1)S(1)}, bf16[4,128,128]{2,1,0:T(8,128)(2,1)S(1)}, bf16[4,128,128]{2,1,0:T(8,128)(2,1)S(1)}, bf16[4,128,128]{2,1,0:T(8,128)(2,1)S(1)}) custom-call(s32[3]{0:T(128)S(1)} %pad_add_fusion.place_ref, f32[3,128]{1,0:T(4,128)S(1)} %dynamic-slice_bitcast_fusion.taps_ref, bf16[128,16,128]{2,1,0:T(8,128)(2,1)S(1)} %bitcast.34, ...), custom_call_target="tpu_custom_call" | custom-call | flops 1073741824 | bytes 3145728 | tf_op jit(solution)/shard_map/pallas_call | solution.py:99
  77.8 0.7 collective-permute-start.1
  78.5 0.6 collective-permute-start.2
  79.1 0.9 collective-permute-start.3
  80.0 2.0 collective-permute-start.4
  82.0 5.7 %collective-permute-done.2 = bf16[4,128,128]{2,1,0:T(8,128)(2,1)S(1)} collective-permute-done((bf16[4,128,128]{2,1,0:T(8,128)(2,1)S(1)}, bf16[4,128,128]{2,1,0:T(8,128)(2,1)S(1)}, u32[]{:S(2)}, u32[]{:S(2)}) %collective-permute-start.2) | collective-permute-done | bytes 131104 | tf_op jit(solution)/shard_map/ppermute | solution.py:197
  87.7 0.6 collective-permute-done.3
  88.3 5.4 %collective-permute-done.4 = bf16[4,128,128]{2,1,0:T(8,128)(2,1)S(1)} collective-permute-done((bf16[4,128,128]{2,1,0:T(8,128)(2,1)S(1)}, bf16[4,128,128]{2,1,0:T(8,128)(2,1)S(1)}, u32[]{:S(2)}, u32[]{:S(2)}) %collective-permute-start.4) | collective-permute-done | bytes 131104 | tf_op jit(solution)/shard_map/ppermute | solution.py:197
  93.9 1.9 collective-permute-done.5
  95.7 0.1 pad_maximum_fusion.refs_0_.refs_1_.refs_2_.refs_3_.refs_4_.refs_5_.refs_6_.refs_7_.refs_8_.refs_9_.refs_10_.refs_11_.refs_12_.refs_13_.refs_14_.refs_15_
  95.8 18.0 %all-gather.2.cloned.1.call-done.refs_8_.refs_16_ = bf16[1024,4096]{1,0:T(8,128)(2,1)} async-done(((bf16[256,4096]{1,0:T(8,128)(2,1)}), bf16[1024,4096]{1,0:T(8,128)(2,1)}) %all-gather.2.cloned.1.call-update) | async-done | bytes 8388624 | tf_op jit(solution)/shard_map/all_gather | solution.py:180
  113.9 3.4 %copy-done = bf16[1024,4096]{1,0:T(8,128)(2,1)S(1)} copy-done((bf16[1024,4096]{1,0:T(8,128)(2,1)S(1)}, bf16[1024,4096]{1,0:T(8,128)(2,1)}, u32[]{:S(2)}) %copy-start) | copy-done | bytes 8388632
  117.3 3.8 %shard_map.67 = bf16[128,4096]{1,0:T(8,128)(2,1)S(1)} custom-call(s32[3]{0:T(128)S(1)} %pad_add_fusion.place_ref, bf16[2,4,4,128,128]{4,3,2,1,0:T(8,128)(2,1)S(1)} %pad_maximum_fusion.refs_0_.refs_1_.refs_2_.refs_3_.refs_4_.refs_5_.refs_6_.refs_7_.refs_8_.refs_9_.refs_10_.refs_11_.refs_12_.refs_13_.refs_14_.refs_15_, ...), custom_call_target="tpu_custom_call" | custom-call | flops 1073741824 | bytes 10485760 | tf_op jit(solution)/shard_map/pallas_call | solution.py:144
  121.1 0.1 fusion.11
  121.2 3.4 %collective-permute-start.10 = (bf16[128,2048]{1,0:T(8,128)(2,1)S(1)}, bf16[128,2048]{1,0:T(8,128)(2,1)S(1)}, u32[]{:S(2)}, u32[]{:S(2)}) collective-permute-start(bf16[128,2048]{1,0:T(8,128)(2,1)S(1)} %get-tuple-element.20), channel_id=1, source_target_pairs={{8,0},{10,2},{12,4},{14,6},{16,8},{18,10},{20,12},{22,14},{24,16},... | collective-permute-start | bytes 1572872 | tf_op jit(solution)/shard_map/ppermute | solution.py:205
  124.7 5.0 %shard_map.66 = (bf16[128,4096]{1,0:T(8,128)(2,1)S(1)}, bf16[128,4096]{1,0:T(8,128)(2,1)S(1)}) custom-call(s32[3]{0:T(128)S(1)} %pad_add_fusion.place_ref, bf16[2,4,4,128,128]{4,3,2,1,0:T(8,128)(2,1)S(1)} %pad_maximum_fusion.refs_0_.refs_1_.refs_2_.refs_3_.refs_4_.refs_5_.refs_6_.refs_7_.refs_8_.refs_9_.refs_10_.refs_11_.refs_12_.refs_13_.refs_14_.refs_15_, ...), custom_call_target="tpu_custom_call" | custom-call | flops 2147483648 | bytes 12582912 | tf_op jit(solution)/shard_map/pallas_call | solution.py:144
  129.7 3.9 %collective-permute-start.6 = (bf16[128,2048]{1,0:T(8,128)(2,1)S(1)}, bf16[128,2048]{1,0:T(8,128)(2,1)S(1)}, u32[]{:S(2)}, u32[]{:S(2)}) collective-permute-start(bf16[128,2048]{1,0:T(8,128)(2,1)S(1)} %slice.108), channel_id=1, source_target_pairs={{8,0},{10,2},{12,4},{14,6},{16,8},{18,10},{20,12},{22,14},{24,16},... | collective-permute-start | bytes 1572872 | tf_op jit(solution)/shard_map/ppermute | solution.py:208
  133.7 3.3 %collective-permute-done.10 = bf16[128,2048]{1,0:T(8,128)(2,1)S(1)} collective-permute-done((bf16[128,2048]{1,0:T(8,128)(2,1)S(1)}, bf16[128,2048]{1,0:T(8,128)(2,1)S(1)}, u32[]{:S(2)}, u32[]{:S(2)}) %collective-permute-start.10) | collective-permute-done | bytes 524320 | tf_op jit(solution)/shard_map/ppermute | solution.py:205
  137.0 0.1 add_convert_fusion
  137.1 4.3 %collective-permute-start.11 = (bf16[128,2048]{1,0:T(8,128)(2,1)S(1)}, bf16[128,2048]{1,0:T(8,128)(2,1)S(1)}, u32[]{:S(2)}, u32[]{:S(2)}) collective-permute-start(bf16[128,2048]{1,0:T(8,128)(2,1)S(1)} %add_convert_fusion), channel_id=1, source_target_pairs={{8,0},{10,2},{12,4},{14,6},{16,8},{18,10},{20,12},{22,14},{24,16},... | collective-permute-start | bytes 1572872 | tf_op jit(solution)/shard_map/ppermute | solution.py:215
  141.4 7.8 %collective-permute-done.7 = bf16[128,2048]{1,0:T(8,128)(2,1)S(1)} collective-permute-done((bf16[128,2048]{1,0:T(8,128)(2,1)S(1)}, bf16[128,2048]{1,0:T(8,128)(2,1)S(1)}, u32[]{:S(2)}, u32[]{:S(2)}) %collective-permute-start.7) | collective-permute-done | bytes 524320 | tf_op jit(solution)/shard_map/ppermute | solution.py:204
  149.2 0.1 add_convert_fusion.1
  149.3 1.5 collective-permute-start.8
  150.9 3.9 %shard_map.65 = f32[128,4096]{1,0:T(8,128)S(1)} custom-call(s32[3]{0:T(128)S(1)} %pad_add_fusion.place_ref, bf16[2,4,4,128,128]{4,3,2,1,0:T(8,128)(2,1)S(1)} %pad_maximum_fusion.refs_0_.refs_1_.refs_2_.refs_3_.refs_4_.refs_5_.refs_6_.refs_7_.refs_8_.refs_9_.refs_10_.refs_11_.refs_12_.refs_13_.refs_14_.refs_15_, ...), custom_call_target="tpu_custom_call" | custom-call | flops 1073741824 | bytes 10485760 | tf_op jit(solution)/shard_map/pallas_call | solution.py:144
  154.8 4.7 %collective-permute-done.6 = bf16[128,2048]{1,0:T(8,128)(2,1)S(1)} collective-permute-done((bf16[128,2048]{1,0:T(8,128)(2,1)S(1)}, bf16[128,2048]{1,0:T(8,128)(2,1)S(1)}, u32[]{:S(2)}, u32[]{:S(2)}) %collective-permute-start.6) | collective-permute-done | bytes 524320 | tf_op jit(solution)/shard_map/ppermute | solution.py:208
  159.5 12.2 %collective-permute-done.9 = bf16[128,2048]{1,0:T(8,128)(2,1)S(1)} collective-permute-done((bf16[128,2048]{1,0:T(8,128)(2,1)S(1)}, bf16[128,2048]{1,0:T(8,128)(2,1)S(1)}, u32[]{:S(2)}, u32[]{:S(2)}) %collective-permute-start.9) | collective-permute-done | bytes 524320 | tf_op jit(solution)/shard_map/ppermute | solution.py:207
  171.7 10.3 %collective-permute-done.11 = bf16[128,2048]{1,0:T(8,128)(2,1)S(1)} collective-permute-done((bf16[128,2048]{1,0:T(8,128)(2,1)S(1)}, bf16[128,2048]{1,0:T(8,128)(2,1)S(1)}, u32[]{:S(2)}, u32[]{:S(2)}) %collective-permute-start.11) | collective-permute-done | bytes 524320 | tf_op jit(solution)/shard_map/ppermute | solution.py:215
  182.0 11.0 %collective-permute-done.8 = bf16[128,2048]{1,0:T(8,128)(2,1)S(1)} collective-permute-done((bf16[128,2048]{1,0:T(8,128)(2,1)S(1)}, bf16[128,2048]{1,0:T(8,128)(2,1)S(1)}, u32[]{:S(2)}, u32[]{:S(2)}) %collective-permute-start.8) | collective-permute-done | bytes 524320 | tf_op jit(solution)/shard_map/ppermute | solution.py:214
  193.0 0.5 fusion.3
  193.5 1.0 pad_maximum_fusion.1
  (24 shorter events, 0.5 us)
Async XLA Ops:
  6.5 1.0 copy-start.1
  6.5 1.5 copy-start.2
  6.5 107.3 %all-gather.2.cloned.1.call-start = ((), (), s32[]{:S(2)}) async-start(), calls=%async_computation.2 | async-start | bytes 10485760 | tf_op jit(solution)/shard_map/all_gather | solution.py:180
  7.6 11.7 %copy-start.4 = (f32[3,3,2048]{2,1,0:T(4,128)S(1)}, f32[3,3,2048]{2,1,0:T(4,128)}, u32[]{:S(2)}) copy-start(f32[3,3,2048]{2,1,0:T(4,128)} %param.9) | copy-start | bytes 221188
  8.5 10.9 %collective-permute-start = (bf16[2,2048,2]{1,2,0:T(2,128)(2,1)S(1)}, bf16[2,2048,2]{1,2,0:T(2,128)(2,1)S(1)}, u32[]{:S(2)}, u32[]{:S(2)}) collective-permute-start(bf16[2,2048,2]{1,2,0:T(2,128)(2,1)S(1)} %pad_maximum_fusion.3), channel_id=1, source_target_pairs={{0,2},{2,4},{4,6},{6,8},{8,10},{10,12},{12,14},{14,16},{16,18},{18... | collective-permute-start | bytes 49160 | tf_op jit(solution)/shard_map/ppermute | solution.py:18
  13.3 20.9 %all-to-all-start.1 = ((bf16[16,128,128]{2,1,0:T(8,128)(2,1)}), bf16[16,128,128]{2,1,0:T(8,128)(2,1)S(1)}, u32[]{:S(2)}, u32[]{:S(2)}) async-start(bf16[16,128,128]{2,1,0:T(8,128)(2,1)} %bitcast.16), calls=%async_computation.1 | async-start | bytes 1048576 | tf_op jit(solution)/shard_map/all_to_all | solution.py:174
  20.8 17.5 %copy-start.3 = (f32[128,2048]{1,0:T(8,128)S(1)}, f32[128,2048]{1,0:T(8,128)}, u32[]{:S(2)}) copy-start(f32[128,2048]{1,0:T(8,128)} %param.10) | copy-start | bytes 3145732
  24.5 14.1 %slice-start = ((f32[3,3,2048]{2,1,0:T(4,128)}), f32[1,3,2048]{2,1,0:T(4,128)S(1)}, s32[]{:S(2)}) async-start(f32[3,3,2048]{2,1,0:T(4,128)} %param.9), calls=%async_computation.3 | async-start | bytes 65536 | tf_op jit(solution)/shard_map/slice | solution.py:185
  34.3 18.4 %all-to-all-start = ((bf16[16,128,128]{2,1,0:T(8,128)(2,1)}), bf16[16,128,128]{2,1,0:T(8,128)(2,1)S(1)}, u32[]{:S(2)}, u32[]{:S(2)}) async-start(bf16[16,128,128]{2,1,0:T(8,128)(2,1)} %bitcast.14), calls=%async_computation | async-start | bytes 1048576 | tf_op jit(solution)/shard_map/all_to_all | solution.py:174
  77.8 4.2 %collective-permute-start.1 = (bf16[4,128,128]{2,1,0:T(8,128)(2,1)S(1)}, bf16[4,128,128]{2,1,0:T(8,128)(2,1)S(1)}, u32[]{:S(2)}, u32[]{:S(2)}) collective-permute-start(bf16[4,128,128]{2,1,0:T(8,128)(2,1)S(1)} %get-tuple-element.11), channel_id=1, source_target_pairs={{0,0},{1,16},{2,2},{3,18},{4,4},{5,20},{6,6},{7,22},{8,1},{9,17},{... | collective-permute-start | bytes 393224 | tf_op jit(solution)/shard_map/ppermute | solution.py:197
  78.5 9.2 %collective-permute-start.2 = (bf16[4,128,128]{2,1,0:T(8,128)(2,1)S(1)}, bf16[4,128,128]{2,1,0:T(8,128)(2,1)S(1)}, u32[]{:S(2)}, u32[]{:S(2)}) collective-permute-start(bf16[4,128,128]{2,1,0:T(8,128)(2,1)S(1)} %get-tuple-element.12), channel_id=1, source_target_pairs={{0,2},{1,18},{2,0},{3,16},{4,6},{5,22},{6,4},{7,20},{8,3},{9,19},{... | collective-permute-start | bytes 393224 | tf_op jit(solution)/shard_map/ppermute | solution.py:197
  79.1 9.2 %collective-permute-start.3 = (bf16[4,128,128]{2,1,0:T(8,128)(2,1)S(1)}, bf16[4,128,128]{2,1,0:T(8,128)(2,1)S(1)}, u32[]{:S(2)}, u32[]{:S(2)}) collective-permute-start(bf16[4,128,128]{2,1,0:T(8,128)(2,1)S(1)} %get-tuple-element.13), channel_id=1, source_target_pairs={{0,4},{1,20},{2,6},{3,22},{4,0},{5,16},{6,2},{7,18},{8,5},{9,21},{... | collective-permute-start | bytes 393224 | tf_op jit(solution)/shard_map/ppermute | solution.py:197
  80.0 13.6 %collective-permute-start.4 = (bf16[4,128,128]{2,1,0:T(8,128)(2,1)S(1)}, bf16[4,128,128]{2,1,0:T(8,128)(2,1)S(1)}, u32[]{:S(2)}, u32[]{:S(2)}) collective-permute-start(bf16[4,128,128]{2,1,0:T(8,128)(2,1)S(1)} %get-tuple-element.14), channel_id=1, source_target_pairs={{0,6},{1,22},{2,4},{3,20},{4,2},{5,18},{6,0},{7,16},{8,7},{9,23},{... | collective-permute-start | bytes 393224 | tf_op jit(solution)/shard_map/ppermute | solution.py:197
  93.8 2.0 collective-permute-start.5
  113.9 3.4 %copy-start = (bf16[1024,4096]{1,0:T(8,128)(2,1)S(1)}, bf16[1024,4096]{1,0:T(8,128)(2,1)}, u32[]{:S(2)}) copy-start(bf16[1024,4096]{1,0:T(8,128)(2,1)} %all-gather.2.cloned.1.call-done.refs_8_.refs_16_) | copy-start | bytes 25165828
  121.2 15.8 %collective-permute-start.10 = (bf16[128,2048]{1,0:T(8,128)(2,1)S(1)}, bf16[128,2048]{1,0:T(8,128)(2,1)S(1)}, u32[]{:S(2)}, u32[]{:S(2)}) collective-permute-start(bf16[128,2048]{1,0:T(8,128)(2,1)S(1)} %get-tuple-element.20), channel_id=1, source_target_pairs={{8,0},{10,2},{12,4},{14,6},{16,8},{18,10},{20,12},{22,14},{24,16},... | collective-permute-start | bytes 1572872 | tf_op jit(solution)/shard_map/ppermute | solution.py:205
  124.6 24.6 %collective-permute-start.7 = (bf16[128,2048]{1,0:T(8,128)(2,1)S(1)}, bf16[128,2048]{1,0:T(8,128)(2,1)S(1)}, u32[]{:S(2)}, u32[]{:S(2)}) collective-permute-start(bf16[128,2048]{1,0:T(8,128)(2,1)S(1)} %get-tuple-element.19), channel_id=1, source_target_pairs={{0,8},{2,10},{4,12},{6,14},{8,16},{10,18},{12,20},{14,22},{16,24},... | collective-permute-start | bytes 1572872 | tf_op jit(solution)/shard_map/ppermute | solution.py:204
  129.7 29.8 %collective-permute-start.6 = (bf16[128,2048]{1,0:T(8,128)(2,1)S(1)}, bf16[128,2048]{1,0:T(8,128)(2,1)S(1)}, u32[]{:S(2)}, u32[]{:S(2)}) collective-permute-start(bf16[128,2048]{1,0:T(8,128)(2,1)S(1)} %slice.108), channel_id=1, source_target_pairs={{8,0},{10,2},{12,4},{14,6},{16,8},{18,10},{20,12},{22,14},{24,16},... | collective-permute-start | bytes 1572872 | tf_op jit(solution)/shard_map/ppermute | solution.py:208
  133.6 38.1 %collective-permute-start.9 = (bf16[128,2048]{1,0:T(8,128)(2,1)S(1)}, bf16[128,2048]{1,0:T(8,128)(2,1)S(1)}, u32[]{:S(2)}, u32[]{:S(2)}) collective-permute-start(bf16[128,2048]{1,0:T(8,128)(2,1)S(1)} %slice.112), channel_id=1, source_target_pairs={{0,8},{2,10},{4,12},{6,14},{8,16},{10,18},{12,20},{14,22},{16,24},... | collective-permute-start | bytes 1572872 | tf_op jit(solution)/shard_map/ppermute | solution.py:207
  137.1 44.9 %collective-permute-start.11 = (bf16[128,2048]{1,0:T(8,128)(2,1)S(1)}, bf16[128,2048]{1,0:T(8,128)(2,1)S(1)}, u32[]{:S(2)}, u32[]{:S(2)}) collective-permute-start(bf16[128,2048]{1,0:T(8,128)(2,1)S(1)} %add_convert_fusion), channel_id=1, source_target_pairs={{8,0},{10,2},{12,4},{14,6},{16,8},{18,10},{20,12},{22,14},{24,16},... | collective-permute-start | bytes 1572872 | tf_op jit(solution)/shard_map/ppermute | solution.py:215
  149.3 43.7 %collective-permute-start.8 = (bf16[128,2048]{1,0:T(8,128)(2,1)S(1)}, bf16[128,2048]{1,0:T(8,128)(2,1)S(1)}, u32[]{:S(2)}, u32[]{:S(2)}) collective-permute-start(bf16[128,2048]{1,0:T(8,128)(2,1)S(1)} %add_convert_fusion.1), channel_id=1, source_target_pairs={{0,8},{2,10},{4,12},{6,14},{8,16},{10,18},{12,20},{14,22},{16,24},... | collective-permute-start | bytes 1572872 | tf_op jit(solution)/shard_map/ppermute | solution.py:214
Sparse Core Ops, SparseCore 0:
  9.2 104.6 all-gather.1

commit v3 on v1

--- a/solution.py
+++ b/solution.py
@@ -8,6 +8,7 @@
 from jax.experimental.pallas import tpu as pltpu
 from jax.sharding import PartitionSpec as P
 
+EARLY_EIGHTHS = 5
 PLANE = 4
 VMEM_LIMIT = 40 * 2**20
 
@@ -26,8 +27,12 @@
     )
 
 
-def filtered_streams(streams, taps):
-    before = shifted(jnp.stack([stream[:, -2:] for stream in streams]), "seq", 1)
+def last_positions(streams):
+    return jnp.stack([stream[:, -2:] for stream in streams])
+
+
+def filtered_streams(streams, tails, taps):
+    before = shifted(tails, "seq", 1)
     extended = [
         jnp.concatenate([before[index], stream], axis=1).astype(jnp.float32)
         for index, stream in enumerate(streams)
@@ -35,55 +40,108 @@
     return [short_filter(value, tap) for value, tap in zip(extended, taps)]
 
 
+BAND = 32
+GROUP = 8
+
+
+def conv_kernel(x_ref, h_ref, y_ref, shifted_x):
+    channels, blocks, width = x_ref.shape
+    parts = width // BAND
+    band_lane = lax.broadcasted_iota(jnp.int32, (BAND, width), 1)
+    keep = band_lane > lax.broadcasted_iota(jnp.int32, (BAND, width), 0)
+    lane = lax.broadcasted_iota(jnp.int32, (blocks, width), 1)
+    row = lax.broadcasted_iota(jnp.int32, (blocks, width), 0)
+    shifted_x[...] = jnp.zeros(shifted_x.shape, jnp.float32)
+
+    def one_channel(slot, channel):
+        signal = x_ref[channel].astype(jnp.float32)
+        shifted_x[slot, 0, blocks : 2 * blocks] = signal
+        for part in range(1, parts):
+            left = width - BAND * part
+            turned = pltpu.roll(signal, left, 1)
+            following = jnp.where(row == blocks - 1, 0.0, pltpu.roll(turned, blocks - 1, 0))
+            shifted_x[slot, part, blocks : 2 * blocks] = jnp.where(lane < left, turned, following)
+            shifted_x[slot, part, blocks - 8 : blocks] = jnp.where(
+                (lane[:8] >= left) & (row[:8] == 7), jnp.broadcast_to(turned[:1], (8, width)), 0.0
+            )
+        earlier = jnp.zeros((BAND, width), jnp.float32)
+        bands, signals = [], []
+        for lag in range(blocks + 1):
+            delayed_filter = jnp.zeros((BAND, width), jnp.float32)
+            if lag < blocks:
+                delayed_filter = pltpu.roll(
+                    jnp.broadcast_to(h_ref[channel, lag : lag + 1, :], (BAND, width)),
+                    1,
+                    1,
+                    stride=1,
+                    stride_axis=0,
+                )
+            bands.append(jnp.where(keep, delayed_filter, earlier).astype(jnp.bfloat16))
+            earlier = delayed_filter
+            ahead = [shifted_x[slot, part, lag : lag + blocks, :] for part in range(parts)]
+            signals.append(jnp.concatenate(ahead, axis=0).astype(jnp.bfloat16))
+        total = lax.dot_general(
+            jnp.concatenate(signals, axis=1),
+            jnp.concatenate(bands, axis=1),
+            (((1,), (1,)), ((), ())),
+            preferred_element_type=jnp.float32,
+        )
+        y_ref[channel] = jnp.concatenate(
+            [total[part * blocks : (part + 1) * blocks] for part in range(parts)], axis=1
+        )
+
+    def one_group(group, carry):
+        for slot in range(GROUP):
+            one_channel(slot, group * GROUP + slot)
+        return carry
+
+    lax.fori_loop(0, channels // GROUP, one_group, 0)
+
+
+VMEM = pl.BlockSpec(memory_space=pltpu.VMEM)
+SMEM = pl.BlockSpec(memory_space=pltpu.SMEM)
+
+
+def convolve(product, filters):
+    channels, blocks, width = product.shape
+    return pl.pallas_call(
+        conv_kernel,
+        out_shape=jax.ShapeDtypeStruct(product.shape, jnp.float32),
+        in_specs=[VMEM, VMEM],
+        out_specs=VMEM,
+        scratch_shapes=[pltpu.VMEM((GROUP, width // BAND, 2 * blocks + 8, width), jnp.float32)],
+        compiler_params=pltpu.CompilerParams(vmem_limit_bytes=VMEM_LIMIT),
+        cost_estimate=pl.CostEstimate(
+            flops=16 * channels * width * width * blocks * blocks,
+            bytes_accessed=10 * channels * blocks * width,
+            transcendentals=0,
+        ),
+    )(product, filters)
+
+
 def delayed(value, steps, lane, row):
     rolled = pltpu.roll(value, steps, 1)
     above = jnp.where(row >= 1, pltpu.roll(rolled, 1, 0), 0.0)
     return jnp.where(lane >= steps, rolled, above)
 
 
-def conv_kernel(place_ref, taps_ref, x_ref, h_ref, q_ref, *rest):
-    outs, (xpad, gated) = rest[:-2], rest[-2:]
-    channels, blocks, width = x_ref.shape
-    keep = lax.broadcasted_iota(jnp.int32, (width, width), 1) >= lax.broadcasted_iota(
-        jnp.int32, (width, width), 0
-    )
+def gate_kernel(place_ref, taps_ref, q_ref, y_ref, *rest):
+    outs, gated = rest[:-1], rest[-1]
+    channels, blocks, width = y_ref.shape
     lane = lax.broadcasted_iota(jnp.int32, (blocks, width), 1)
     row = lax.broadcasted_iota(jnp.int32, (blocks, width), 0)
-    xpad[:blocks] = jnp.zeros((blocks, width), jnp.float32)
 
     def one_channel(channel, carry):
-        xpad[blocks:] = x_ref[channel].astype(jnp.float32)
-        earlier = jnp.zeros((width, width), jnp.float32)
-        total = jnp.zeros((blocks, width), jnp.float32)
-        bands, shifts = [], []
-        for lag in range(blocks):
-            rolled = pltpu.roll(
-                jnp.broadcast_to(h_ref[channel, lag : lag + 1, :], (width, width)),
-                0,
-                1,
-                stride=1,
-                stride_axis=0,
-            )
-            bands.append(jnp.where(keep, rolled, earlier).astype(jnp.bfloat16))
-            earlier = rolled
-            shifts.append(xpad[pl.ds(blocks - lag, blocks), :].astype(jnp.bfloat16))
-            if len(bands) == 2:
-                total += jnp.dot(
-                    jnp.concatenate(shifts, axis=1),
-                    jnp.concatenate(bands, axis=0),
-                    preferred_element_type=jnp.float32,
-                )
-                bands, shifts = [], []
         query = q_ref[channel].astype(jnp.float32)
         query_short = (
             taps_ref[0, channel] * query
             + taps_ref[1, channel] * delayed(query, 1, lane, row)
             + taps_ref[2, channel] * delayed(query, 2, lane, row)
         )
-        gated[pl.ds(pl.multiple_of(channel * blocks, blocks), blocks), :] = query_short * total
+        gated[pl.ds(pl.multiple_of(channel * blocks, blocks), blocks), :] = query_short * y_ref[channel]
         return carry
 
-    lax.fori_loop(0, channels, one_channel, 0, unroll=4)
+    lax.fori_loop(0, channels, one_channel, 0, unroll=8)
     inner = len(outs)
     for offset, out in enumerate(outs):
         for outer in range(blocks // inner):
@@ -92,52 +150,47 @@
             out[outer] = tile.T.astype(jnp.bfloat16)
 
 
-def convolve_and_gate(place, taps, product, filters, query, inner):
-    channels, blocks, width = product.shape
-    vmem = pl.BlockSpec(memory_space=pltpu.VMEM)
-    smem = pl.BlockSpec(memory_space=pltpu.SMEM)
+def gate(place, taps, query, mixed, inner):
+    channels, blocks, width = mixed.shape
     return pl.pallas_call(
-        conv_kernel,
+        gate_kernel,
         out_shape=[jax.ShapeDtypeStruct((blocks // inner, width, channels), jnp.bfloat16)] * inner,
-        in_specs=[smem, smem, vmem, vmem, vmem],
-        out_specs=[vmem] * inner,
-        scratch_shapes=[
-            pltpu.VMEM((2 * blocks, width), jnp.float32),
-            pltpu.VMEM((channels * blocks, width), jnp.float32),
-        ],
+        in_specs=[SMEM, SMEM, VMEM, VMEM],
+        out_specs=[VMEM] * inner,
+        scratch_shapes=[pltpu.VMEM((channels * blocks, width), jnp.float32)],
         compiler_params=pltpu.CompilerParams(vmem_limit_bytes=VMEM_LIMIT),
         cost_estimate=pl.CostEstimate(
-            flops=2 * channels * width * width * blocks * blocks,
-            bytes_accessed=12 * channels * blocks * width,
+            flops=40 * channels * width * blocks,
+            bytes_accessed=8 * channels * blocks * width,
             transcendentals=0,
         ),
-    )(place, taps, product, filters, query)
+    )(place, taps, query, mixed)
 
 
 def project_kernel(pieces, place_ref, *refs):
     gates, weights, outs = refs[: 8 * pieces], refs[8 * pieces : -pieces], refs[-pieces:]
-    tiles = [ref[...] for ref in weights[:3]] + [
-        jnp.concatenate([weights[3][...], weights[4][...]], axis=0)
-    ]
-    depth = tiles[0].shape[0] // 2
+    depth = gates[0].shape[-1]
     for piece in range(pieces):
         mine = [ref[...].reshape(-1, depth) for ref in gates[8 * piece : 8 * piece + 8]]
-        total = None
-        for index, tile in enumerate(tiles):
-            left = jnp.concatenate([mine[2 * index], mine[2 * index + 1]], axis=1)
-            term = jnp.dot(left, tile, preferred_element_type=jnp.float32)
+        total, taken = None, 0
+        for weight in weights:
+            count = weight.shape[0] // depth
+            left = jnp.concatenate(mine[taken : taken + count], axis=1)
+            term = jnp.dot(left, weight[...], preferred_element_type=jnp.float32)
             total = term if total is None else total + term
+            taken += count
         outs[piece][...] = total.astype(outs[piece].dtype)
 
 
 def project(place, gates, weights, steps, dtype, tile=512):
     _, _, planes, rows, depth = gates.shape
     columns = weights[0].shape[1]
+    ordered = len(weights) == 1
 
     def gate_spec(step, offset, half):
         def index(column, place_ref):
             inner, outer, core = place_ref[0], place_ref[1], place_ref[2]
-            owner = inner ^ offset
+            owner = offset if ordered else inner ^ offset
             source = 2 * (owner % 2) + half
             return ((owner // 2) ^ core, source ^ inner, (outer + step) % planes, 0, 0)
 
@@ -176,8 +229,6 @@
     place = jnp.stack([inner, outer, core]).astype(jnp.int32)
     channels, width = long_filters.shape[0], query_proj.shape[1]
 
-    across = [(source, source ^ 1) for source in range(seq_count)]
-    along = [(source, source ^ 2) for source in range(seq_count)]
     up = [(source, (source + PLANE) % seq_count) for source in range(seq_count)]
     down = [(target, source) for source, target in up]
 
@@ -187,19 +238,23 @@
         )
         return parts.transpose(1, 0, 2)
 
-    weight_x = lax.ppermute(out_weight, "seq", across)
-    weight_y = lax.ppermute(out_weight, "seq", along)
-    half_rows = out_weight.shape[0] // 2
-    weight_top = lax.ppermute(weight_y[:half_rows], "seq", across)
-    weight_end = lax.ppermute(weight_x[half_rows:], "seq", along)
-    weights = [out_weight, weight_x, weight_y, weight_top, weight_end]
-
+    in_plane = [
+        [(source, source ^ offset) for source in range(seq_count)] for offset in range(PLANE)
+    ]
+    groups = [list(range(first, first + PLANE)) for first in range(0, seq_count, PLANE)]
+    tails = last_positions((key_proj, value_proj))
+    tails, out_weight = lax.optimization_barrier((tails, out_weight))
+    early = out_weight.shape[1] * EARLY_EIGHTHS // 8
+    weight_early = lax.all_gather(
+        out_weight[:, :early], "seq", axis=0, tiled=True, axis_index_groups=groups
+    )
+    key_short, value_short = filtered_streams((key_proj, value_proj), tails, short_taps[1:])
+    product = spread((key_short * value_short).astype(jnp.bfloat16))
+    query_proj, product = lax.optimization_barrier((query_proj, product))
     query = spread(query_proj)
-    key_short, value_short = filtered_streams((key_proj, value_proj), short_taps[1:])
-    product = spread((key_short * value_short).astype(jnp.bfloat16))
     taps = lax.dynamic_slice_in_dim(short_taps[0], place_seq * channels, channels, axis=1)
-    filters = long_filters.reshape(channels, seq_count, width)
-    gated = convolve_and_gate(place, taps, product, filters, query, PLANE)
+    filters = long_filters[:, ::-1].reshape(channels, seq_count, width)
+    gated = gate(place, taps, query, convolve(product, filters), PLANE)
 
     landed = []
     for offset, message in enumerate(gated):
@@ -210,27 +265,53 @@
                 target = (planes // tp_count * tp + z // tp_count) * PLANE + (q ^ offset)
                 pairs.append((source * tp_count + tp, target * tp_count + z % tp_count))
         landed.append(lax.ppermute(message, ("seq", "tp"), pairs))
+    landed, out_weight = lax.optimization_barrier((landed, out_weight))
     own = jnp.stack(landed)
     other = lax.ppermute(own, "tp", [(0, 1), (1, 0)])
     gates = jnp.stack([own, other])
 
-    (far,) = project(place, gates, weights, (2,), jnp.bfloat16)
-    half = far.shape[1] // 2
-    far_left = lax.ppermute(far[:, :half], "seq", up)
-    far_right = lax.ppermute(far[:, half:], "seq", down)
-    ahead, behind = project(place, gates, weights, (1, planes - 1), jnp.bfloat16)
-    near_right = lax.ppermute(ahead[:, half:], "seq", up)
-    near_left = lax.ppermute(behind[:, :half], "seq", down)
-    (mine,) = project(place, gates, weights, (0,), jnp.float32)
+    late = out_weight[:, early:]
+    weights_late = [late] + [lax.ppermute(late, "seq", pairs) for pairs in in_plane[1:]]
 
     def added(first, second):
         return (first.astype(jnp.float32) + second.astype(jnp.float32)).astype(jnp.bfloat16)
 
-    sum_left = lax.ppermute(added(ahead[:, :half], far_left), "seq", up)
-    sum_right = lax.ppermute(added(behind[:, half:], far_right), "seq", down)
-    left = mine[:, :half] + near_left.astype(jnp.float32) + sum_left.astype(jnp.float32)
-    right = mine[:, half:] + near_right.astype(jnp.float32) + sum_right.astype(jnp.float32)
-    return jnp.concatenate([left, right], axis=1).astype(jnp.bfloat16)
+    def far_sends(gates, weights):
+        (far,) = project(place, gates, weights, (2,), jnp.bfloat16)
+        half = far.shape[1] // 2
+        return lax.ppermute(far[:, :half], "seq", up), lax.ppermute(far[:, half:], "seq", down)
+
+    def near_sends(gates, weights, far_left, far_right):
+        ahead, behind = project(place, gates, weights, (1, planes - 1), jnp.bfloat16)
+        half = ahead.shape[1] // 2
+        near_right = lax.ppermute(ahead[:, half:], "seq", up)
+        near_left = lax.ppermute(behind[:, :half], "seq", down)
+        up_sum, down_sum = added(ahead[:, :half], far_left), added(behind[:, half:], far_right)
+        return (near_left, near_right), (up_sum, down_sum)
+
+    def sum_sends(sums):
+        return lax.ppermute(sums[0], "seq", up), lax.ppermute(sums[1], "seq", down)
+
+    def own_and_near(gates, weights, near):
+        (mine,) = project(place, gates, weights, (0,), jnp.float32)
+        half = mine.shape[1] // 2
+        return mine[:, :half] + near[0].astype(jnp.float32), mine[:, half:] + near[1].astype(jnp.float32)
+
+    weights_early = [weight_early]
+    near_early, sums = near_sends(gates, weights_early, *far_sends(gates, weights_early))
+    sum_early = sum_sends(sums)
+    part_early = own_and_near(gates, weights_early, near_early)
+    gates_late, sums, part_early = lax.optimization_barrier((gates, sums, part_early))
+    far_late = far_sends(gates_late, weights_late)
+    gates_late, sum_early = lax.optimization_barrier((gates_late, sum_early))
+    near_late, sums = near_sends(gates_late, weights_late, *far_late)
+    sum_late = sum_sends(sums)
+    part_late = own_and_near(gates_late, weights_late, near_late)
+    columns = [
+        part + summed.astype(jnp.float32)
+        for part, summed in zip(part_early + part_late, sum_early + sum_late)
+    ]
+    return jnp.concatenate(columns, axis=1).astype(jnp.bfloat16)
 
 
 PRECISE = lax.Precision.HIGHEST
@@ -296,8 +377,9 @@
 
 def by_whole_rows(query_proj, key_proj, value_proj, short_taps, long_filters, out_weight):
     inner_size = query_proj.shape[1] // 2
+    streams = (query_proj, key_proj, value_proj)
     query_short, key_short, value_short = filtered_streams(
-        (query_proj, key_proj, value_proj), short_taps
+        streams, last_positions(streams), short_taps
     )
     product = (key_short * value_short).astype(jnp.bfloat16)
     spread = lax.all_to_all(product, "seq", split_axis=0, concat_axis=1, tiled=True)

time: 226 us -> 178 us (0.79)
  waiting for transfers between devices: 123 us -> 64.7 us
  starting transfers between devices: 32.8 us -> 50.3 us
  between operations: 0.29 us -> 13.8 us
  Pallas kernels: 44.3 us -> 31.2 us
  local copies, waits for them, and re-layouts: 16.5 us -> 11.2 us
    ppermute x1, waiting for transfers between devices: 34 us -> 1.37 us  [shifted(): lax.ppermute(value, axis, [(source, source + steps) for source in range(i...]
    ppermute x10 -> x15, waiting for transfers between devices: 50.5 us -> 30.2 us  [the longest x2 9.57 us: near_sends(): near_right = lax.ppermute(ahead[:, half:], 'seq', up)]
    ppermute x10 -> x15, starting transfers between devices: 12.1 us -> 29.5 us  [the longest x2 8.73 us: sum_sends(): lax.ppermute(sums[0], 'seq', up)]
    ppermute x4, waiting for transfers between devices: 26.9 us -> 13 us  [by_planes(): landed.append(lax.ppermute(message, ('seq', 'tp'), pairs))]
    pallas_call x1 -> x2, Pallas kernels: 24.8 us -> 16.8 us  [the longest x1 14.2 us: convolve(): pl.pallas_call(conv_kernel, out_shape=jax.ShapeDtypeStruct(product.shape,...]
    all_gather x0 -> x1, waiting for transfers between devices: none -> 5.84 us  [by_planes(): lax.all_gather(out_weight[:, :early], 'seq', axis=0, tiled=True, axis_ind...]
    pallas_call x3 -> x6, Pallas kernels: 19.5 us -> 14.4 us  [project(): pl.pallas_call(functools.partial(project_kernel, len(steps)), out_shape=[...]
    unnamed x15 -> x17, local copies, waits for them, and re-layouts: 7.16 us -> 3.77 us
  transfers between devices with their start and end apart: 18 -> 24, of which waited for: 10 -> 18; matrix products, arithmetic and copies ran while one was open for 10% -> 5% of each run, Pallas kernels for 17% -> 16%
where the time goes in v3:
time: 178 us
  waiting for transfers between devices  64.7 us (36%)
  starting transfers between devices  50.3 us (28%)
  Pallas kernels  31.2 us (18%)
  between operations  13.8 us (8%)
  local copies, waits for them, and re-layouts  11.2 us (6%)
  other arithmetic  6.5 us (4%)
    pallas_call x6, Pallas kernels, project(): pl.pallas_call(functools.partial(project_kernel, len(steps)), out_shape=[...  14.4 us
    pallas_call x1, Pallas kernels, convolve(): pl.pallas_call(conv_kernel, out_shape=jax.ShapeDtypeStruct(product.shape,...  14.2 us
    ppermute x4, waiting for transfers between devices, by_planes(): landed.append(lax.ppermute(message, ('seq', 'tp'), pairs))  13 us
    all_to_all x2, waiting for transfers between devices, spread(): lax.all_to_all(stream.reshape(seq_count, channels, width), 'seq', split_a...  12.4 us
    all_to_all x2, starting transfers between devices, spread(): lax.all_to_all(stream.reshape(seq_count, channels, width), 'seq', split_a...  11.6 us
    ppermute x2, waiting for transfers between devices, near_sends(): near_right = lax.ppermute(ahead[:, half:], 'seq', up)  9.57 us
    ppermute x2, waiting for transfers between devices, sum_sends(): lax.ppermute(sums[1], 'seq', down)  9.21 us
    ppermute x2, starting transfers between devices, sum_sends(): lax.ppermute(sums[0], 'seq', up)  8.73 us
  transfers between devices with their start and end apart: 24, of which 18 were waited for; matrix products, arithmetic and copies ran while one was open for 5% of the time, Pallas kernels for 16%

profile of v3, /device:TPU:0, one launch (start us, length us, event | category | flops | bytes accessed | tf_op | source)
XLA Modules:
  0.0 177.6 jit_solution(5802972382540236954)
XLA Ops:
  6.5 1.4 slice.123
  8.2 1.3 slice.122
  9.7 1.2 slice.137
  10.9 4.8 %collective-permute-start = (bf16[2,2048,2]{1,2,0:T(2,128)(2,1)S(1)}, bf16[2,2048,2]{1,2,0:T(2,128)(2,1)S(1)}, u32[]{:S(2)}, u32[]{:S(2)}) collective-permute-start(bf16[2,2048,2]{1,2,0:T(2,128)(2,1)S(1)} %pad_maximum_fusion.3), channel_id=1, source_target_pairs={{0,2},{2,4},{4,6},{6,8},{8,10},{10,12},{12,14},{14,16},{16,18},{18... | collective-permute-start | bytes 49160 | tf_op jit(solution)/shard_map/ppermute | solution.py:19
  15.8 1.4 collective-permute-done
  18.7 3.7 %fusion.2 = bf16[2048,128]{1,0:T(8,128)(2,1)} fusion(f32[2048,130]{1,0:T(8,128)S(1)} %get-tuple-element.70, f32[2048,130]{1,0:T(8,128)S(1)} %get-tuple-element.69, f32[2048]{0:T(1024)S(1)} %bitcast.48, f32[2048]{0:T(1024)S(1)} %bitcast.49, f32[2048]{0:T(1024)S(1)} %bitcast.45, f32[2048]{0:T(1024)S(1)} %bitcast.46, f32[2048]{0:T(1024)S(1)} %bitcast.47, ...), kind=kLoop, calls=%fused_computation.3 | loop fusion | flops 3145728 | bytes 6864896 | tf_op jit(solution)/shard_map/convert_element_type | solution.py:252
  22.4 7.7 %all-to-all-start = ((bf16[16,128,128]{2,1,0:T(8,128)(2,1)}), bf16[16,128,128]{2,1,0:T(8,128)(2,1)S(1)}, u32[]{:S(2)}, u32[]{:S(2)}) async-start(bf16[16,128,128]{2,1,0:T(8,128)(2,1)} %bitcast.14), calls=%async_computation | async-start | bytes 1048576 | tf_op jit(solution)/shard_map/all_to_all | solution.py:236
  30.1 1.5 rev.3
  31.8 12.4 %all-to-all-done = bf16[16,128,128]{2,1,0:T(8,128)(2,1)S(1)} async-done(((bf16[16,128,128]{2,1,0:T(8,128)(2,1)}), bf16[16,128,128]{2,1,0:T(8,128)(2,1)S(1)}, u32[]{:S(2)}, u32[]{:S(2)}) %all-to-all-start) | async-done | bytes 524320 | tf_op jit(solution)/shard_map/all_to_all | solution.py:236
  44.6 3.9 %all-to-all-start.1 = ((bf16[16,128,128]{2,1,0:T(8,128)(2,1)}), bf16[16,128,128]{2,1,0:T(8,128)(2,1)S(1)}, u32[]{:S(2)}, u32[]{:S(2)}) async-start(bf16[16,128,128]{2,1,0:T(8,128)(2,1)} %bitcast.38), calls=%async_computation.1 | async-start | bytes 1048576 | tf_op jit(solution)/shard_map/all_to_all | solution.py:236
  48.6 14.2 %shard_map.64.y_ref = f32[128,16,128]{2,1,0:T(8,128)S(1)} custom-call(bf16[128,16,128]{2,1,0:T(8,128)(2,1)S(1)} %bitcast.34, f32[128,16,128]{2,1,0:T(8,128)S(1)} %bitcast.33), custom_call_target="tpu_custom_call" | custom-call | flops 8589934592 | bytes 2621440 | tf_op jit(solution)/shard_map/pallas_call | solution.py:107
  63.1 2.6 %shard_map.65 = (bf16[4,128,128]{2,1,0:T(8,128)(2,1)S(1)}, bf16[4,128,128]{2,1,0:T(8,128)(2,1)S(1)}, bf16[4,128,128]{2,1,0:T(8,128)(2,1)S(1)}, bf16[4,128,128]{2,1,0:T(8,128)(2,1)S(1)}) custom-call(s32[3]{0:T(128)S(1)} %pad_add_fusion.place_ref, f32[3,128]{1,0:T(4,128)S(1)} %dynamic-slice_bitcast_fusion.taps_ref, bf16[128,16,128]{2,1,0:T(8,128)(2,1)S(1)} %bitcast.32, ...), custom_call_target="tpu_custom_call" | custom-call | flops 10485760 | bytes 2097152 | tf_op jit(solution)/shard_map/pallas_call | solution.py:155
  66.4 2.0 %collective-permute-start.2 = (bf16[4,128,128]{2,1,0:T(8,128)(2,1)S(1)}, bf16[4,128,128]{2,1,0:T(8,128)(2,1)S(1)}, u32[]{:S(2)}, u32[]{:S(2)}) collective-permute-start(bf16[4,128,128]{2,1,0:T(8,128)(2,1)S(1)} %get-tuple-element.32), channel_id=1, source_target_pairs={{0,2},{1,18},{2,0},{3,16},{4,6},{5,22},{6,4},{7,20},{8,3},{9,19},{... | collective-permute-start | bytes 393224 | tf_op jit(solution)/shard_map/ppermute | solution.py:267
  68.4 1.5 collective-permute-start.3
  70.0 4.3 %collective-permute-done.2 = bf16[4,128,128]{2,1,0:T(8,128)(2,1)S(1)} collective-permute-done((bf16[4,128,128]{2,1,0:T(8,128)(2,1)S(1)}, bf16[4,128,128]{2,1,0:T(8,128)(2,1)S(1)}, u32[]{:S(2)}, u32[]{:S(2)}) %collective-permute-start.2) | collective-permute-done | bytes 131104 | tf_op jit(solution)/shard_map/ppermute | solution.py:267
  74.2 2.0 %collective-permute-done.3 = bf16[4,128,128]{2,1,0:T(8,128)(2,1)S(1)} collective-permute-done((bf16[4,128,128]{2,1,0:T(8,128)(2,1)S(1)}, bf16[4,128,128]{2,1,0:T(8,128)(2,1)S(1)}, u32[]{:S(2)}, u32[]{:S(2)}) %collective-permute-start.3) | collective-permute-done | bytes 131104 | tf_op jit(solution)/shard_map/ppermute | solution.py:267
  76.2 6.8 %collective-permute-done.4 = bf16[4,128,128]{2,1,0:T(8,128)(2,1)S(1)} collective-permute-done((bf16[4,128,128]{2,1,0:T(8,128)(2,1)S(1)}, bf16[4,128,128]{2,1,0:T(8,128)(2,1)S(1)}, u32[]{:S(2)}, u32[]{:S(2)}) %collective-permute-start.4) | collective-permute-done | bytes 131104 | tf_op jit(solution)/shard_map/ppermute | solution.py:267
  83.2 1.9 %collective-permute-done.5 = bf16[4,4,128,128]{3,2,1,0:T(8,128)(2,1)S(1)} collective-permute-done((bf16[4,4,128,128]{3,2,1,0:T(8,128)(2,1)S(1)}, bf16[4,4,128,128]{3,2,1,0:T(8,128)(2,1)S(1)}, u32[]{:S(2)}, u32[]{:S(2)}) %collective-permute-start.5) | collective-permute-done | bytes 524320 | tf_op jit(solution)/shard_map/ppermute | solution.py:270
  85.2 5.8 %all-gather.2.cloned.1.call-done.refs_16_.refs_8_ = bf16[1024,2560]{1,0:T(8,128)(2,1)} async-done(((bf16[256,2560]{1,0:T(8,128)(2,1)}), bf16[1024,2560]{1,0:T(8,128)(2,1)}) %all-gather.2.cloned.1.call-update) | async-done | bytes 5242896 | tf_op jit(solution)/shard_map/all_gather | solution.py:248
  91.0 2.5 %copy-done = bf16[1024,2560]{1,0:T(8,128)(2,1)S(1)} copy-done((bf16[1024,2560]{1,0:T(8,128)(2,1)S(1)}, bf16[1024,2560]{1,0:T(8,128)(2,1)}, u32[]{:S(2)}) %copy-start) | copy-done | bytes 5242904
  93.5 2.6 %shard_map.67 = bf16[128,2560]{1,0:T(8,128)(2,1)S(1)} custom-call(s32[3]{0:T(128)S(1)} %pad_add_fusion.place_ref, bf16[2,4,4,128,128]{4,3,2,1,0:T(8,128)(2,1)S(1)} %pad_maximum_fusion.refs_0_.refs_1_.refs_2_.refs_3_.refs_4_.refs_5_.refs_6_.refs_7_.refs_8_.refs_9_.refs_10_.refs_11_.refs_12_.refs_13_.refs_14_.refs_15_, ...), custom_call_target="tpu_custom_call" | custom-call | flops 671088640 | bytes 6553600 | tf_op jit(solution)/shard_map/pallas_call | solution.py:206
  97.0 1.2 slice.146.refs_8_.refs_16_
  98.2 1.3 collective-permute-start.12
  100.3 1.4 collective-permute-start.14
  101.8 3.0 %collective-permute-start.7 = (bf16[128,1280]{1,0:T(8,128)(2,1)S(1)}, bf16[128,1280]{1,0:T(8,128)(2,1)S(1)}, u32[]{:S(2)}, u32[]{:S(2)}) collective-permute-start(bf16[128,1280]{1,0:T(8,128)(2,1)S(1)} %get-tuple-element.55), channel_id=1, source_target_pairs={{8,0},{10,2},{12,4},{14,6},{16,8},{18,10},{20,12},{22,14},{24,16},... | collective-permute-start | bytes 983048 | tf_op jit(solution)/shard_map/ppermute | solution.py:282
  104.7 3.3 %shard_map.66 = (bf16[128,2560]{1,0:T(8,128)(2,1)S(1)}, bf16[128,2560]{1,0:T(8,128)(2,1)S(1)}) custom-call(s32[3]{0:T(128)S(1)} %pad_add_fusion.place_ref, bf16[2,4,4,128,128]{4,3,2,1,0:T(8,128)(2,1)S(1)} %pad_maximum_fusion.refs_0_.refs_1_.refs_2_.refs_3_.refs_4_.refs_5_.refs_6_.refs_7_.refs_8_.refs_9_.refs_10_.refs_11_.refs_12_.refs_13_.refs_14_.refs_15_, ...), custom_call_target="tpu_custom_call" | custom-call | flops 1342177280 | bytes 7864320 | tf_op jit(solution)/shard_map/pallas_call | solution.py:206
  108.1 2.6 %shard_map.68 = f32[128,2560]{1,0:T(8,128)S(1)} custom-call(s32[3]{0:T(128)S(1)} %pad_add_fusion.place_ref, bf16[2,4,4,128,128]{4,3,2,1,0:T(8,128)(2,1)S(1)} %pad_maximum_fusion.refs_0_.refs_1_.refs_2_.refs_3_.refs_4_.refs_5_.refs_6_.refs_7_.refs_8_.refs_9_.refs_10_.refs_11_.refs_12_.refs_13_.refs_14_.refs_15_, ...), custom_call_target="tpu_custom_call" | custom-call | flops 671088640 | bytes 6553600 | tf_op jit(solution)/shard_map/pallas_call | solution.py:206
  110.7 2.3 %collective-permute-start.9 = (bf16[128,1280]{1,0:T(8,128)(2,1)S(1)}, bf16[128,1280]{1,0:T(8,128)(2,1)S(1)}, u32[]{:S(2)}, u32[]{:S(2)}) collective-permute-start(bf16[128,1280]{1,0:T(8,128)(2,1)S(1)} %slice.145), channel_id=1, source_target_pairs={{0,8},{2,10},{4,12},{6,14},{8,16},{10,18},{12,20},{14,22},{16,24},... | collective-permute-start | bytes 983048 | tf_op jit(solution)/shard_map/ppermute | solution.py:287
  113.1 2.3 %collective-permute-done.7 = bf16[128,1280]{1,0:T(8,128)(2,1)S(1)} collective-permute-done((bf16[128,1280]{1,0:T(8,128)(2,1)S(1)}, bf16[128,1280]{1,0:T(8,128)(2,1)S(1)}, u32[]{:S(2)}, u32[]{:S(2)}) %collective-permute-start.7) | collective-permute-done | bytes 327712 | tf_op jit(solution)/shard_map/ppermute | solution.py:282
  115.4 1.5 collective-permute-start.8
  117.0 6.2 %collective-permute-done.9 = bf16[128,1280]{1,0:T(8,128)(2,1)S(1)} collective-permute-done((bf16[128,1280]{1,0:T(8,128)(2,1)S(1)}, bf16[128,1280]{1,0:T(8,128)(2,1)S(1)}, u32[]{:S(2)}, u32[]{:S(2)}) %collective-permute-start.9) | collective-permute-done | bytes 327712 | tf_op jit(solution)/shard_map/ppermute | solution.py:287
  123.3 6.4 %collective-permute-start.10 = (bf16[128,1280]{1,0:T(8,128)(2,1)S(1)}, bf16[128,1280]{1,0:T(8,128)(2,1)S(1)}, u32[]{:S(2)}, u32[]{:S(2)}) collective-permute-start(bf16[128,1280]{1,0:T(8,128)(2,1)S(1)} %add_convert_fusion.3), channel_id=1, source_target_pairs={{0,8},{2,10},{4,12},{6,14},{8,16},{10,18},{12,20},{14,22},{16,24},... | collective-permute-start | bytes 983048 | tf_op jit(solution)/shard_map/ppermute | solution.py:293
  130.2 2.0 %collective-permute-start.11 = (bf16[128,1280]{1,0:T(8,128)(2,1)S(1)}, bf16[128,1280]{1,0:T(8,128)(2,1)S(1)}, u32[]{:S(2)}, u32[]{:S(2)}) collective-permute-start(bf16[128,1280]{1,0:T(8,128)(2,1)S(1)} %add_convert_fusion.2), channel_id=1, source_target_pairs={{8,0},{10,2},{12,4},{14,6},{16,8},{18,10},{20,12},{22,14},{24,16},... | collective-permute-start | bytes 983048 | tf_op jit(solution)/shard_map/ppermute | solution.py:293
  132.3 1.4 collective-permute-done.13.refs_10_.refs_18_
  133.7 1.6 collective-permute-done.14.refs_11_.refs_19_
  135.3 1.8 %shard_map.71 = bf16[128,1536]{1,0:T(8,128)(2,1)S(1)} custom-call(s32[3]{0:T(128)S(1)} %pad_add_fusion.place_ref, bf16[2,4,4,128,128]{4,3,2,1,0:T(8,128)(2,1)S(1)} %pad_maximum_fusion.refs_0_.refs_1_.refs_2_.refs_3_.refs_4_.refs_5_.refs_6_.refs_7_.refs_8_.refs_9_.refs_10_.refs_11_.refs_12_.refs_13_.refs_14_.refs_15_, ...), custom_call_target="tpu_custom_call" | custom-call | flops 402653184 | bytes 3932160 | tf_op jit(solution)/shard_map/pallas_call | solution.py:206
  137.1 1.8 %collective-permute-start.16 = (bf16[128,768]{1,0:T(8,128)(2,1)S(1)}, bf16[128,768]{1,0:T(8,128)(2,1)S(1)}, u32[]{:S(2)}, u32[]{:S(2)}) collective-permute-start(bf16[128,768]{1,0:T(8,128)(2,1)S(1)} %get-tuple-element.59), channel_id=1, source_target_pairs={{0,8},{2,10},{4,12},{6,14},{8,16},{10,18},{12,20},{14,22},{16,24},... | collective-permute-start | bytes 589832 | tf_op jit(solution)/shard_map/ppermute | solution.py:282
  139.0 2.0 %collective-permute-start.19 = (bf16[128,768]{1,0:T(8,128)(2,1)S(1)}, bf16[128,768]{1,0:T(8,128)(2,1)S(1)}, u32[]{:S(2)}, u32[]{:S(2)}) collective-permute-start(bf16[128,768]{1,0:T(8,128)(2,1)S(1)} %get-tuple-element.60), channel_id=1, source_target_pairs={{8,0},{10,2},{12,4},{14,6},{16,8},{18,10},{20,12},{22,14},{24,16},... | collective-permute-start | bytes 589832 | tf_op jit(solution)/shard_map/ppermute | solution.py:282
  141.0 4.3 %collective-permute-done.11 = bf16[128,1280]{1,0:T(8,128)(2,1)S(1)} collective-permute-done((bf16[128,1280]{1,0:T(8,128)(2,1)S(1)}, bf16[128,1280]{1,0:T(8,128)(2,1)S(1)}, u32[]{:S(2)}, u32[]{:S(2)}) %collective-permute-start.11) | collective-permute-done | bytes 327712 | tf_op jit(solution)/shard_map/ppermute | solution.py:293
  145.3 2.3 %shard_map.70 = (bf16[128,1536]{1,0:T(8,128)(2,1)S(1)}, bf16[128,1536]{1,0:T(8,128)(2,1)S(1)}) custom-call(s32[3]{0:T(128)S(1)} %pad_add_fusion.place_ref, bf16[2,4,4,128,128]{4,3,2,1,0:T(8,128)(2,1)S(1)} %pad_maximum_fusion.refs_0_.refs_1_.refs_2_.refs_3_.refs_4_.refs_5_.refs_6_.refs_7_.refs_8_.refs_9_.refs_10_.refs_11_.refs_12_.refs_13_.refs_14_.refs_15_, ...), custom_call_target="tpu_custom_call" | custom-call | flops 805306368 | bytes 4718592 | tf_op jit(solution)/shard_map/pallas_call | solution.py:206
  147.6 1.6 collective-permute-done.16
  149.3 2.3 %collective-permute-start.17 = (bf16[128,768]{1,0:T(8,128)(2,1)S(1)}, bf16[128,768]{1,0:T(8,128)(2,1)S(1)}, u32[]{:S(2)}, u32[]{:S(2)}) collective-permute-start(bf16[128,768]{1,0:T(8,128)(2,1)S(1)} %add_convert_fusion.5), channel_id=1, source_target_pairs={{0,8},{2,10},{4,12},{6,14},{8,16},{10,18},{12,20},{14,22},{16,24},... | collective-permute-start | bytes 589832 | tf_op jit(solution)/shard_map/ppermute | solution.py:293
  151.7 1.6 collective-permute-start.15
  153.3 1.9 %collective-permute-start.20 = (bf16[128,768]{1,0:T(8,128)(2,1)S(1)}, bf16[128,768]{1,0:T(8,128)(2,1)S(1)}, u32[]{:S(2)}, u32[]{:S(2)}) collective-permute-start(bf16[128,768]{1,0:T(8,128)(2,1)S(1)} %add_convert_fusion.4), channel_id=1, source_target_pairs={{8,0},{10,2},{12,4},{14,6},{16,8},{18,10},{20,12},{22,14},{24,16},... | collective-permute-start | bytes 589832 | tf_op jit(solution)/shard_map/ppermute | solution.py:293
  155.5 1.8 %shard_map.69 = f32[128,1536]{1,0:T(8,128)S(1)} custom-call(s32[3]{0:T(128)S(1)} %pad_add_fusion.place_ref, bf16[2,4,4,128,128]{4,3,2,1,0:T(8,128)(2,1)S(1)} %pad_maximum_fusion.refs_0_.refs_1_.refs_2_.refs_3_.refs_4_.refs_5_.refs_6_.refs_7_.refs_8_.refs_9_.refs_10_.refs_11_.refs_12_.refs_13_.refs_14_.refs_15_, ...), custom_call_target="tpu_custom_call" | custom-call | flops 402653184 | bytes 3932160 | tf_op jit(solution)/shard_map/pallas_call | solution.py:206
  158.4 2.9 %collective-permute-done.15 = bf16[128,768]{1,0:T(8,128)(2,1)S(1)} collective-permute-done((bf16[128,768]{1,0:T(8,128)(2,1)S(1)}, bf16[128,768]{1,0:T(8,128)(2,1)S(1)}, u32[]{:S(2)}, u32[]{:S(2)}) %collective-permute-start.15) | collective-permute-done | bytes 196640 | tf_op jit(solution)/shard_map/ppermute | solution.py:288
  161.3 4.9 %collective-permute-done.20 = bf16[128,768]{1,0:T(8,128)(2,1)S(1)} collective-permute-done((bf16[128,768]{1,0:T(8,128)(2,1)S(1)}, bf16[128,768]{1,0:T(8,128)(2,1)S(1)}, u32[]{:S(2)}, u32[]{:S(2)}) %collective-permute-start.20) | collective-permute-done | bytes 196640 | tf_op jit(solution)/shard_map/ppermute | solution.py:293
  166.2 3.4 %collective-permute-done.18 = bf16[128,768]{1,0:T(8,128)(2,1)S(1)} collective-permute-done((bf16[128,768]{1,0:T(8,128)(2,1)S(1)}, bf16[128,768]{1,0:T(8,128)(2,1)S(1)}, u32[]{:S(2)}, u32[]{:S(2)}) %collective-permute-start.18) | collective-permute-done | bytes 196640 | tf_op jit(solution)/shard_map/ppermute | solution.py:287
  (59 shorter events, 9.4 us)
Async XLA Ops:
  6.5 3.1 %copy-start.3 = (bf16[256,4096]{1,0:T(8,128)(2,1)S(1)}, bf16[256,4096]{1,0:T(8,128)(2,1)}, u32[]{:S(2)}) copy-start(bf16[256,4096]{1,0:T(8,128)(2,1)} %param.11) | copy-start | bytes 6291460
  6.5 84.5 %all-gather.2.cloned.1.call-start = ((), (), s32[]{:S(2)}) async-start(), calls=%async_computation.2 | async-start | bytes 6553600 | tf_op jit(solution)/shard_map/all_gather | solution.py:248
  9.6 6.2 %copy-start.5 = (f32[3,3,2048]{2,1,0:T(4,128)S(1)}, f32[3,3,2048]{2,1,0:T(4,128)}, u32[]{:S(2)}) copy-start(f32[3,3,2048]{2,1,0:T(4,128)} %param.9) | copy-start | bytes 221188
  9.7 8.2 %copy-start.1 = (bf16[2048,128]{1,0:T(8,128)(2,1)S(1)}, bf16[2048,128]{1,0:T(8,128)(2,1)}, u32[]{:S(2)}) copy-start(bf16[2048,128]{1,0:T(8,128)(2,1)} %param.7) | copy-start | bytes 1572868
  9.7 8.2 %copy-start.2 = (bf16[2048,128]{1,0:T(8,128)(2,1)S(1)}, bf16[2048,128]{1,0:T(8,128)(2,1)}, u32[]{:S(2)}) copy-start(bf16[2048,128]{1,0:T(8,128)(2,1)} %param.8) | copy-start | bytes 1572868
  10.9 6.3 %collective-permute-start = (bf16[2,2048,2]{1,2,0:T(2,128)(2,1)S(1)}, bf16[2,2048,2]{1,2,0:T(2,128)(2,1)S(1)}, u32[]{:S(2)}, u32[]{:S(2)}) collective-permute-start(bf16[2,2048,2]{1,2,0:T(2,128)(2,1)S(1)} %pad_maximum_fusion.3), channel_id=1, source_target_pairs={{0,2},{2,4},{4,6},{6,8},{8,10},{10,12},{12,14},{14,16},{16,18},{18... | collective-permute-start | bytes 49160 | tf_op jit(solution)/shard_map/ppermute | solution.py:19
  18.7 11.4 %copy-start.4 = (f32[128,2048]{1,0:T(8,128)S(1)}, f32[128,2048]{1,0:T(8,128)}, u32[]{:S(2)}) copy-start(f32[128,2048]{1,0:T(8,128)} %param.10) | copy-start | bytes 3145732
  22.4 21.8 %all-to-all-start = ((bf16[16,128,128]{2,1,0:T(8,128)(2,1)}), bf16[16,128,128]{2,1,0:T(8,128)(2,1)S(1)}, u32[]{:S(2)}, u32[]{:S(2)}) async-start(bf16[16,128,128]{2,1,0:T(8,128)(2,1)} %bitcast.14), calls=%async_computation | async-start | bytes 1048576 | tf_op jit(solution)/shard_map/all_to_all | solution.py:236
  31.6 17.0 %slice-start = ((f32[3,3,2048]{2,1,0:T(4,128)}), f32[1,3,2048]{2,1,0:T(4,128)S(1)}, s32[]{:S(2)}) async-start(f32[3,3,2048]{2,1,0:T(4,128)} %param.9), calls=%async_computation.3 | async-start | bytes 65536 | tf_op jit(solution)/shard_map/slice | solution.py:255
  44.6 18.2 %all-to-all-start.1 = ((bf16[16,128,128]{2,1,0:T(8,128)(2,1)}), bf16[16,128,128]{2,1,0:T(8,128)(2,1)S(1)}, u32[]{:S(2)}, u32[]{:S(2)}) async-start(bf16[16,128,128]{2,1,0:T(8,128)(2,1)} %bitcast.38), calls=%async_computation.1 | async-start | bytes 1048576 | tf_op jit(solution)/shard_map/all_to_all | solution.py:236
  65.7 4.2 %collective-permute-start.1 = (bf16[4,128,128]{2,1,0:T(8,128)(2,1)S(1)}, bf16[4,128,128]{2,1,0:T(8,128)(2,1)S(1)}, u32[]{:S(2)}, u32[]{:S(2)}) collective-permute-start(bf16[4,128,128]{2,1,0:T(8,128)(2,1)S(1)} %get-tuple-element.31), channel_id=1, source_target_pairs={{0,0},{1,16},{2,2},{3,18},{4,4},{5,20},{6,6},{7,22},{8,1},{9,17},{... | collective-permute-start | bytes 393224 | tf_op jit(solution)/shard_map/ppermute | solution.py:267
  66.4 7.8 %collective-permute-start.2 = (bf16[4,128,128]{2,1,0:T(8,128)(2,1)S(1)}, bf16[4,128,128]{2,1,0:T(8,128)(2,1)S(1)}, u32[]{:S(2)}, u32[]{:S(2)}) collective-permute-start(bf16[4,128,128]{2,1,0:T(8,128)(2,1)S(1)} %get-tuple-element.32), channel_id=1, source_target_pairs={{0,2},{1,18},{2,0},{3,16},{4,6},{5,22},{6,4},{7,20},{8,3},{9,19},{... | collective-permute-start | bytes 393224 | tf_op jit(solution)/shard_map/ppermute | solution.py:267
  68.4 7.8 %collective-permute-start.3 = (bf16[4,128,128]{2,1,0:T(8,128)(2,1)S(1)}, bf16[4,128,128]{2,1,0:T(8,128)(2,1)S(1)}, u32[]{:S(2)}, u32[]{:S(2)}) collective-permute-start(bf16[4,128,128]{2,1,0:T(8,128)(2,1)S(1)} %get-tuple-element.33), channel_id=1, source_target_pairs={{0,4},{1,20},{2,6},{3,22},{4,0},{5,16},{6,2},{7,18},{8,5},{9,21},{... | collective-permute-start | bytes 393224 | tf_op jit(solution)/shard_map/ppermute | solution.py:267
  69.9 13.1 %collective-permute-start.4 = (bf16[4,128,128]{2,1,0:T(8,128)(2,1)S(1)}, bf16[4,128,128]{2,1,0:T(8,128)(2,1)S(1)}, u32[]{:S(2)}, u32[]{:S(2)}) collective-permute-start(bf16[4,128,128]{2,1,0:T(8,128)(2,1)S(1)} %get-tuple-element.34), channel_id=1, source_target_pairs={{0,6},{1,22},{2,4},{3,20},{4,2},{5,18},{6,0},{7,16},{8,7},{9,23},{... | collective-permute-start | bytes 393224 | tf_op jit(solution)/shard_map/ppermute | solution.py:267
  83.1 2.0 %collective-permute-start.5 = (bf16[4,4,128,128]{3,2,1,0:T(8,128)(2,1)S(1)}, bf16[4,4,128,128]{3,2,1,0:T(8,128)(2,1)S(1)}, u32[]{:S(2)}, u32[]{:S(2)}) collective-permute-start(bf16[4,4,128,128]{3,2,1,0:T(8,128)(2,1)S(1)} %get-tuple-element.58), channel_id=1, source_target_pairs={{0,1},{1,0},{2,3},{3,2},{4,5},{5,4},{6,7},{7,6},{8,9},{9,8},{10,11... | collective-permute-start | bytes 1572872 | tf_op jit(solution)/shard_map/ppermute | solution.py:270
  91.0 2.5 %copy-start = (bf16[1024,2560]{1,0:T(8,128)(2,1)S(1)}, bf16[1024,2560]{1,0:T(8,128)(2,1)}, u32[]{:S(2)}) copy-start(bf16[1024,2560]{1,0:T(8,128)(2,1)} %all-gather.2.cloned.1.call-done.refs_16_.refs_8_) | copy-start | bytes 15728644
  96.1 14.6 %collective-permute-start.6 = (bf16[128,1280]{1,0:T(8,128)(2,1)S(1)}, bf16[128,1280]{1,0:T(8,128)(2,1)S(1)}, u32[]{:S(2)}, u32[]{:S(2)}) collective-permute-start(bf16[128,1280]{1,0:T(8,128)(2,1)S(1)} %get-tuple-element.56), channel_id=1, source_target_pairs={{0,8},{2,10},{4,12},{6,14},{8,16},{10,18},{12,20},{14,22},{16,24},... | collective-permute-start | bytes 983048 | tf_op jit(solution)/shard_map/ppermute | solution.py:282
  98.2 34.1 %collective-permute-start.12 = (bf16[256,1536]{1,0:T(8,128)(2,1)S(1)}, bf16[256,1536]{1,0:T(8,128)(2,1)S(1)}, u32[]{:S(2)}, u32[]{:S(2)}) collective-permute-start(bf16[256,1536]{1,0:T(8,128)(2,1)S(1)} %slice.146.refs_8_.refs_16_), channel_id=1, source_target_pairs={{0,2},{2,0},{4,6},{6,4},{8,10},{10,8},{12,14},{14,12},{16,18},{18,... | collective-permute-start | bytes 2359304 | tf_op jit(solution)/shard_map/ppermute | solution.py:274
  99.5 34.2 %collective-permute-start.13 = (bf16[256,1536]{1,0:T(8,128)(2,1)S(1)}, bf16[256,1536]{1,0:T(8,128)(2,1)S(1)}, u32[]{:S(2)}, u32[]{:S(2)}) collective-permute-start(bf16[256,1536]{1,0:T(8,128)(2,1)S(1)} %slice.146.refs_8_.refs_16_), channel_id=1, source_target_pairs={{0,4},{2,6},{4,0},{6,2},{8,12},{10,14},{12,8},{14,10},{16,20},{18,... | collective-permute-start | bytes 2359304 | tf_op jit(solution)/shard_map/ppermute | solution.py:274
  100.3 34.9 %collective-permute-start.14 = (bf16[256,1536]{1,0:T(8,128)(2,1)S(1)}, bf16[256,1536]{1,0:T(8,128)(2,1)S(1)}, u32[]{:S(2)}, u32[]{:S(2)}) collective-permute-start(bf16[256,1536]{1,0:T(8,128)(2,1)S(1)} %slice.146.refs_8_.refs_16_), channel_id=1, source_target_pairs={{0,6},{2,4},{4,2},{6,0},{8,14},{10,12},{12,10},{14,8},{16,22},{18,... | collective-permute-start | bytes 2359304 | tf_op jit(solution)/shard_map/ppermute | solution.py:274
  101.8 13.6 %collective-permute-start.7 = (bf16[128,1280]{1,0:T(8,128)(2,1)S(1)}, bf16[128,1280]{1,0:T(8,128)(2,1)S(1)}, u32[]{:S(2)}, u32[]{:S(2)}) collective-permute-start(bf16[128,1280]{1,0:T(8,128)(2,1)S(1)} %get-tuple-element.55), channel_id=1, source_target_pairs={{8,0},{10,2},{12,4},{14,6},{16,8},{18,10},{20,12},{22,14},{24,16},... | collective-permute-start | bytes 983048 | tf_op jit(solution)/shard_map/ppermute | solution.py:282
  110.7 12.5 %collective-permute-start.9 = (bf16[128,1280]{1,0:T(8,128)(2,1)S(1)}, bf16[128,1280]{1,0:T(8,128)(2,1)S(1)}, u32[]{:S(2)}, u32[]{:S(2)}) collective-permute-start(bf16[128,1280]{1,0:T(8,128)(2,1)S(1)} %slice.145), channel_id=1, source_target_pairs={{0,8},{2,10},{4,12},{6,14},{8,16},{10,18},{12,20},{14,22},{16,24},... | collective-permute-start | bytes 983048 | tf_op jit(solution)/shard_map/ppermute | solution.py:287
  115.4 14.8 %collective-permute-start.8 = (bf16[128,1280]{1,0:T(8,128)(2,1)S(1)}, bf16[128,1280]{1,0:T(8,128)(2,1)S(1)}, u32[]{:S(2)}, u32[]{:S(2)}) collective-permute-start(bf16[128,1280]{1,0:T(8,128)(2,1)S(1)} %slice.143), channel_id=1, source_target_pairs={{8,0},{10,2},{12,4},{14,6},{16,8},{18,10},{20,12},{22,14},{24,16},... | collective-permute-start | bytes 983048 | tf_op jit(solution)/shard_map/ppermute | solution.py:288
  123.3 17.7 %collective-permute-start.10 = (bf16[128,1280]{1,0:T(8,128)(2,1)S(1)}, bf16[128,1280]{1,0:T(8,128)(2,1)S(1)}, u32[]{:S(2)}, u32[]{:S(2)}) collective-permute-start(bf16[128,1280]{1,0:T(8,128)(2,1)S(1)} %add_convert_fusion.3), channel_id=1, source_target_pairs={{0,8},{2,10},{4,12},{6,14},{8,16},{10,18},{12,20},{14,22},{16,24},... | collective-permute-start | bytes 983048 | tf_op jit(solution)/shard_map/ppermute | solution.py:293
  130.2 15.1 %collective-permute-start.11 = (bf16[128,1280]{1,0:T(8,128)(2,1)S(1)}, bf16[128,1280]{1,0:T(8,128)(2,1)S(1)}, u32[]{:S(2)}, u32[]{:S(2)}) collective-permute-start(bf16[128,1280]{1,0:T(8,128)(2,1)S(1)} %add_convert_fusion.2), channel_id=1, source_target_pairs={{8,0},{10,2},{12,4},{14,6},{16,8},{18,10},{20,12},{22,14},{24,16},... | collective-permute-start | bytes 983048 | tf_op jit(solution)/shard_map/ppermute | solution.py:293
  137.1 12.1 %collective-permute-start.16 = (bf16[128,768]{1,0:T(8,128)(2,1)S(1)}, bf16[128,768]{1,0:T(8,128)(2,1)S(1)}, u32[]{:S(2)}, u32[]{:S(2)}) collective-permute-start(bf16[128,768]{1,0:T(8,128)(2,1)S(1)} %get-tuple-element.59), channel_id=1, source_target_pairs={{0,8},{2,10},{4,12},{6,14},{8,16},{10,18},{12,20},{14,22},{16,24},... | collective-permute-start | bytes 589832 | tf_op jit(solution)/shard_map/ppermute | solution.py:282
  139.0 14.3 %collective-permute-start.19 = (bf16[128,768]{1,0:T(8,128)(2,1)S(1)}, bf16[128,768]{1,0:T(8,128)(2,1)S(1)}, u32[]{:S(2)}, u32[]{:S(2)}) collective-permute-start(bf16[128,768]{1,0:T(8,128)(2,1)S(1)} %get-tuple-element.60), channel_id=1, source_target_pairs={{8,0},{10,2},{12,4},{14,6},{16,8},{18,10},{20,12},{22,14},{24,16},... | collective-permute-start | bytes 589832 | tf_op jit(solution)/shard_map/ppermute | solution.py:282
  149.3 9.1 %collective-permute-start.17 = (bf16[128,768]{1,0:T(8,128)(2,1)S(1)}, bf16[128,768]{1,0:T(8,128)(2,1)S(1)}, u32[]{:S(2)}, u32[]{:S(2)}) collective-permute-start(bf16[128,768]{1,0:T(8,128)(2,1)S(1)} %add_convert_fusion.5), channel_id=1, source_target_pairs={{0,8},{2,10},{4,12},{6,14},{8,16},{10,18},{12,20},{14,22},{16,24},... | collective-permute-start | bytes 589832 | tf_op jit(solution)/shard_map/ppermute | solution.py:293
  151.7 9.6 %collective-permute-start.15 = (bf16[128,768]{1,0:T(8,128)(2,1)S(1)}, bf16[128,768]{1,0:T(8,128)(2,1)S(1)}, u32[]{:S(2)}, u32[]{:S(2)}) collective-permute-start(bf16[128,768]{1,0:T(8,128)(2,1)S(1)} %slice.148), channel_id=1, source_target_pairs={{8,0},{10,2},{12,4},{14,6},{16,8},{18,10},{20,12},{22,14},{24,16},... | collective-permute-start | bytes 589832 | tf_op jit(solution)/shard_map/ppermute | solution.py:288
  153.3 12.9 %collective-permute-start.20 = (bf16[128,768]{1,0:T(8,128)(2,1)S(1)}, bf16[128,768]{1,0:T(8,128)(2,1)S(1)}, u32[]{:S(2)}, u32[]{:S(2)}) collective-permute-start(bf16[128,768]{1,0:T(8,128)(2,1)S(1)} %add_convert_fusion.4), channel_id=1, source_target_pairs={{8,0},{10,2},{12,4},{14,6},{16,8},{18,10},{20,12},{22,14},{24,16},... | collective-permute-start | bytes 589832 | tf_op jit(solution)/shard_map/ppermute | solution.py:293
  155.2 14.4 %collective-permute-start.18 = (bf16[128,768]{1,0:T(8,128)(2,1)S(1)}, bf16[128,768]{1,0:T(8,128)(2,1)S(1)}, u32[]{:S(2)}, u32[]{:S(2)}) collective-permute-start(bf16[128,768]{1,0:T(8,128)(2,1)S(1)} %slice.152), channel_id=1, source_target_pairs={{0,8},{2,10},{4,12},{6,14},{8,16},{10,18},{12,20},{14,22},{16,24},... | collective-permute-start | bytes 589832 | tf_op jit(solution)/shard_map/ppermute | solution.py:287
Sparse Core Ops, SparseCore 0:
  11.1 79.9 all-gather.1

commit v4 on v0

--- a/solution.py
+++ b/solution.py
@@ -1,11 +1,16 @@
+import functools
 import math
 
 import jax
 import jax.numpy as jnp
 from jax import lax
+from jax.experimental import pallas as pl
+from jax.experimental.pallas import tpu as pltpu
 from jax.sharding import PartitionSpec as P
 
-precise = lax.Precision.HIGHEST
+COLUMN_SHARES = (16, 16)
+PLANE = 4
+VMEM_LIMIT = 16 * 2**20
 
 
 def shifted(value, axis, steps):
@@ -22,6 +27,377 @@
     )
 
 
+def filtered_streams(streams, taps):
+    before = shifted(jnp.stack([stream[:, -2:] for stream in streams]), "seq", 1)
+    extended = [
+        jnp.concatenate([before[index], stream], axis=1).astype(jnp.float32)
+        for index, stream in enumerate(streams)
+    ]
+    return [short_filter(value, tap) for value, tap in zip(extended, taps)]
+
+
+VMEM = pl.BlockSpec(memory_space=pltpu.VMEM)
+SMEM = pl.BlockSpec(memory_space=pltpu.SMEM)
+TAIL_ROWS = 16
+
+
+def tails_kernel(query_ref, key_ref, value_ref, out_ref):
+    width = key_ref.shape[1]
+    row = lax.broadcasted_iota(jnp.int32, (TAIL_ROWS, width), 0)
+    lane = lax.broadcasted_iota(jnp.int32, (TAIL_ROWS, width), 1)
+    total = None
+    for index, stream in enumerate((query_ref, key_ref, value_ref)):
+        picked = (row // 2 == index) & (lane == width - 2 + row % 2)
+        term = lax.dot_general(
+            jnp.where(picked, 1.0, 0.0).astype(jnp.bfloat16),
+            stream[...],
+            (((1,), (1,)), ((), ())),
+            preferred_element_type=jnp.float32,
+        )
+        total = term if total is None else total + term
+    out_ref[...] = total.astype(out_ref.dtype)
+
+
+def last_rows(query, key, value):
+    return pl.pallas_call(
+        tails_kernel,
+        out_shape=jax.ShapeDtypeStruct((TAIL_ROWS, key.shape[0]), key.dtype),
+        in_specs=[VMEM] * 3,
+        out_specs=VMEM,
+        compiler_params=pltpu.CompilerParams(vmem_limit_bytes=VMEM_LIMIT),
+    )(query, key, value)
+
+
+def moved_rows(stream):
+    width = stream.shape[1]
+    row = lax.broadcasted_iota(jnp.int32, (3 * width, width), 0)
+    lane = lax.broadcasted_iota(jnp.int32, (3 * width, width), 1)
+    picked = jnp.where(lane == row % width - row // width, 1.0, 0.0).astype(stream.dtype)
+    moved = lax.dot_general(
+        picked, stream, (((1,), (1,)), ((), ())), preferred_element_type=jnp.float32
+    )
+    return moved[:width], moved[width : 2 * width], moved[2 * width :]
+
+
+def short_filtered(stream, index, taps_ref, before_ref, spot):
+    now, once, twice = moved_rows(stream)
+    tap = lambda place: taps_ref[3 * index + place : 3 * index + place + 1, spot]
+    second, first = (
+        before_ref[:, spot].astype(jnp.float32)[2 * index + place : 2 * index + place + 1]
+        for place in range(2)
+    )
+    row = lax.broadcasted_iota(jnp.int32, now.shape, 0)
+    once = jnp.where(row == 0, first, once)
+    twice = jnp.where(row == 0, second, jnp.where(row == 1, first, twice))
+    return tap(0) * now + tap(1) * once + tap(2) * twice
+
+
+def product_kernel(taps_ref, before_ref, key_ref, value_ref, out_ref):
+    width = key_ref.shape[1]
+    for start in range(0, key_ref.shape[0], width):
+        spot = pl.ds(start, width)
+        key = short_filtered(key_ref[spot], 1, taps_ref, before_ref, spot)
+        value = short_filtered(value_ref[spot], 2, taps_ref, before_ref, spot)
+        out_ref[spot] = (key * value).T.astype(out_ref.dtype)
+
+
+def gated_product(taps, before, key, value):
+    return pl.pallas_call(
+        product_kernel,
+        out_shape=jax.ShapeDtypeStruct(key.shape, key.dtype),
+        in_specs=[VMEM] * 4,
+        out_specs=VMEM,
+        compiler_params=pltpu.CompilerParams(vmem_limit_bytes=VMEM_LIMIT),
+    )(taps, before, key, value)
+
+
+def query_kernel(place_ref, taps_ref, before_ref, query_ref, *outs):
+    width = query_ref.shape[1]
+    for offset, out in enumerate(outs):
+        share = jnp.bitwise_xor(place_ref[1], offset)
+        for step in range(out.shape[0]):
+            spot = pl.ds(pl.multiple_of((share * out.shape[0] + step) * width, width), width)
+            query = short_filtered(query_ref[spot], 0, taps_ref, before_ref, spot)
+            out[step] = query.astype(out.dtype)
+
+
+def query_shares(place, taps, before, query, count):
+    channels, width = query.shape
+    shape = (channels // count // width, width, width)
+    return pl.pallas_call(
+        query_kernel,
+        out_shape=[jax.ShapeDtypeStruct(shape, query.dtype)] * count,
+        in_specs=[SMEM] + [VMEM] * 3,
+        out_specs=[VMEM] * count,
+        compiler_params=pltpu.CompilerParams(vmem_limit_bytes=VMEM_LIMIT),
+    )(place, taps, before, query)
+
+
+BAND = 32
+GROUP = 8
+
+
+def conv_kernel(place_ref, x_ref, h_ref, *rest):
+    outs, (signals_f32, turned_filters, shifted_x, result) = rest[:-4], rest[-4:]
+    blocks, channels, width = x_ref.shape
+    parts = width // BAND
+    band_lane = lax.broadcasted_iota(jnp.int32, (BAND, width), 1)
+    keep = band_lane > lax.broadcasted_iota(jnp.int32, (BAND, width), 0)
+    lane = lax.broadcasted_iota(jnp.int32, (blocks, width), 1)
+    row = lax.broadcasted_iota(jnp.int32, (blocks, width), 0)
+    square_row = lax.broadcasted_iota(jnp.int32, (width, width), 0)
+    square_lane = lax.broadcasted_iota(jnp.int32, (width, width), 1)
+    exchange = jnp.where(square_row + square_lane == width - 1, 1.0, 0.0).astype(jnp.bfloat16)
+    shifted_x[...] = jnp.zeros(shifted_x.shape, jnp.float32)
+    for block in range(blocks):
+        signals_f32[block * channels : (block + 1) * channels] = x_ref[block].astype(jnp.float32)
+        turned_filters[blocks - 1 - block] = jnp.dot(
+            h_ref[:, block * width : (block + 1) * width].astype(jnp.bfloat16),
+            exchange,
+            preferred_element_type=jnp.float32,
+        )
+
+    def one_channel(slot, channel):
+        signal = signals_f32[pl.ds(channel, blocks, stride=channels), :]
+        shifted_x[slot, 0, blocks : 2 * blocks] = signal
+        for part in range(1, parts):
+            left = width - BAND * part
+            turned = pltpu.roll(signal, left, 1)
+            following = jnp.where(row == blocks - 1, 0.0, pltpu.roll(turned, blocks - 1, 0))
+            shifted_x[slot, part, blocks : 2 * blocks] = jnp.where(lane < left, turned, following)
+            shifted_x[slot, part, blocks - 8 : blocks] = jnp.where(
+                (lane[:8] >= left) & (row[:8] == 7), jnp.broadcast_to(turned[:1], (8, width)), 0.0
+            )
+        earlier = jnp.zeros((BAND, width), jnp.float32)
+        bands, signals = [], []
+        for lag in range(blocks + 1):
+            delayed_filter = jnp.zeros((BAND, width), jnp.float32)
+            if lag < blocks:
+                delayed_filter = pltpu.roll(
+                    jnp.broadcast_to(turned_filters[lag, pl.ds(channel, 1), :], (BAND, width)),
+                    1,
+                    1,
+                    stride=1,
+                    stride_axis=0,
+                )
+            bands.append(jnp.where(keep, delayed_filter, earlier).astype(jnp.bfloat16))
+            earlier = delayed_filter
+            ahead = [shifted_x[slot, part, lag : lag + blocks, :] for part in range(parts)]
+            signals.append(jnp.concatenate(ahead, axis=0).astype(jnp.bfloat16))
+        total = lax.dot_general(
+            jnp.concatenate(signals, axis=1),
+            jnp.concatenate(bands, axis=1),
+            (((1,), (1,)), ((), ())),
+            preferred_element_type=jnp.float32,
+        )
+        result[pl.ds(pl.multiple_of(channel * blocks, blocks), blocks), :] = jnp.concatenate(
+            [total[part * blocks : (part + 1) * blocks] for part in range(parts)], axis=1
+        )
+
+    def one_group(group, carry):
+        for slot in range(GROUP):
+            one_channel(slot, group * GROUP + slot)
+        return carry
+
+    lax.fori_loop(0, channels // GROUP, one_group, 0)
+    inner = len(outs)
+    for offset, out in enumerate(outs):
+        for outer in range(blocks // inner):
+            block = outer * inner + jnp.bitwise_xor(place_ref[0], offset)
+            out[outer] = result[pl.ds(block, channels, stride=blocks), :].astype(out.dtype)
+
+
+def convolve(place, product, filters, inner):
+    blocks, channels, width = product.shape
+    return pl.pallas_call(
+        conv_kernel,
+        out_shape=[jax.ShapeDtypeStruct((blocks // inner, channels, width), jnp.bfloat16)] * inner,
+        in_specs=[SMEM, VMEM, VMEM],
+        out_specs=[VMEM] * inner,
+        scratch_shapes=[
+            pltpu.VMEM((blocks * channels, width), jnp.float32),
+            pltpu.VMEM((blocks, channels, width), jnp.float32),
+            pltpu.VMEM((GROUP, width // BAND, 2 * blocks + 8, width), jnp.float32),
+            pltpu.VMEM((channels * blocks, width), jnp.float32),
+        ],
+        compiler_params=pltpu.CompilerParams(vmem_limit_bytes=VMEM_LIMIT),
+        cost_estimate=pl.CostEstimate(
+            flops=16 * channels * width * width * blocks * blocks,
+            bytes_accessed=10 * channels * blocks * width,
+            transcendentals=0,
+        ),
+    )(place, product, filters)
+
+
+def gate_kernel(place_ref, *refs):
+    inner = (len(refs) - 1) // 2
+    landed, queries, out_ref = refs[:inner], refs[inner:-1], refs[-1]
+    share = 2 * (place_ref[1] % 2) + place_ref[2]
+    for source, query in enumerate(queries):
+        plane = jnp.bitwise_xor(share, source)
+        for offset, mixed in enumerate(landed):
+            gated = mixed[plane].astype(jnp.float32).T * query[
+                jnp.bitwise_xor(place_ref[0], offset)
+            ].astype(jnp.float32)
+            out_ref[offset, plane] = gated.astype(out_ref.dtype)
+
+
+def gate(place, landed, queries):
+    planes, channels, width = landed[0].shape
+    return pl.pallas_call(
+        gate_kernel,
+        out_shape=jax.ShapeDtypeStruct((len(landed), planes, width, channels), jnp.bfloat16),
+        in_specs=[SMEM] + [VMEM] * (len(landed) + len(queries)),
+        out_specs=VMEM,
+        compiler_params=pltpu.CompilerParams(vmem_limit_bytes=VMEM_LIMIT),
+    )(place, *landed, *queries)
+
+
+def project_kernel(place_ref, own_ref, other_ref, *refs):
+    weights, outs = refs[:-4], refs[-4:]
+    planes, depth = own_ref.shape[1], own_ref.shape[3]
+    inner, outer, core = place_ref[0], place_ref[1], place_ref[2]
+    for out, step in zip(outs, STEPS):
+        plane = (outer + step) % planes
+        total = None
+        for index in range(PLANE):
+            if len(weights) == 1:
+                owner, weight = index, weights[0][2 * depth * index : 2 * depth * (index + 1)]
+            elif index + 1 < PLANE:
+                owner, weight = jnp.bitwise_xor(inner, index), weights[index][...]
+            else:
+                owner = jnp.bitwise_xor(inner, index)
+                weight = jnp.concatenate([ref[...] for ref in weights[index:]], axis=0)
+            mine = jnp.bitwise_xor(owner // 2, core) == 0
+            halves = []
+            for half in range(2):
+                source = jnp.bitwise_xor(2 * (owner % 2) + half, inner)
+                halves.append(jnp.where(mine, own_ref[source, plane], other_ref[source, plane]))
+            term = jnp.dot(
+                jnp.concatenate(halves, axis=1), weight, preferred_element_type=jnp.float32
+            )
+            total = term if total is None else total + term
+        out[...] = total.astype(out.dtype)
+
+
+STEPS = (2, 1, 3, 0)
+
+
+def project(place, gates, weights, first, columns):
+    _, _, rows, _ = gates[0].shape
+    specs = [
+        pl.BlockSpec((weight.shape[0], columns), lambda step, place_ref: (0, first // columns))
+        for weight in weights
+    ]
+    whole = pl.BlockSpec(gates[0].shape, lambda step, place_ref: (0,) * 4)
+    kinds = [jnp.bfloat16] * 3 + [jnp.float32]
+    return pl.pallas_call(
+        project_kernel,
+        out_shape=[jax.ShapeDtypeStruct((rows, columns), kind) for kind in kinds],
+        grid_spec=pltpu.PrefetchScalarGridSpec(
+            num_scalar_prefetch=1,
+            grid=(1,),
+            in_specs=[whole] * 2 + specs,
+            out_specs=[pl.BlockSpec((rows, columns), lambda step, place_ref: (0, 0))] * 4,
+        ),
+        compiler_params=pltpu.CompilerParams(vmem_limit_bytes=VMEM_LIMIT),
+        cost_estimate=pl.CostEstimate(flops=rows * columns, bytes_accessed=0, transcendentals=0),
+    )(place, *gates, *weights)
+
+
+def by_planes(query_proj, key_proj, value_proj, short_taps, long_filters, out_weight):
+    seq_count, tp_count = lax.axis_size("seq"), lax.axis_size("tp")
+    planes = seq_count // PLANE
+    place_seq, core = lax.axis_index("seq"), lax.axis_index("tp")
+    place = jnp.stack([place_seq % PLANE, place_seq // PLANE, core]).astype(jnp.int32)
+    channels, width = long_filters.shape[0], query_proj.shape[1]
+
+    across = [(source, source ^ 1) for source in range(seq_count)]
+    along = [(source, source ^ 2) for source in range(seq_count)]
+    up = [(source, (source + PLANE) % seq_count) for source in range(seq_count)]
+    down = [(target, source) for source, target in up]
+
+    def to_plane_of_rows(message, target_of):
+        pairs = []
+        for source in range(seq_count):
+            z, q = divmod(source, PLANE)
+            for tp in range(tp_count):
+                share, target_q = target_of(z, q)
+                target = (planes // tp_count * tp + share // tp_count) * PLANE + target_q
+                pairs.append((source * tp_count + tp, target * tp_count + share % tp_count))
+        return lax.ppermute(message, ("seq", "tp"), pairs)
+
+    def from_neighbours(first, count):
+        part = out_weight[:, first : first + count]
+        return [part, lax.ppermute(part, "seq", across), lax.ppermute(part, "seq", along)]
+
+    def from_corner(part, from_x, from_y):
+        half = part.shape[0] // 2
+        top = lax.ppermute(from_y[:half], "seq", across)
+        end = lax.ppermute(from_x[half:], "seq", along)
+        return [part, from_x, from_y, top, end]
+
+    spans, first = [], 0
+    for share in COLUMN_SHARES:
+        count = out_weight.shape[1] * share // sum(COLUMN_SHARES)
+        spans.append((first, count))
+        first += count
+
+    groups = [list(range(first, first + PLANE)) for first in range(0, seq_count, PLANE)]
+    early = out_weight[:, : spans[0][1]]
+    early = lax.all_gather(early, "seq", axis=0, tiled=True, axis_index_groups=groups)
+    rows = [[early]]
+    taps = jnp.pad(
+        short_taps.reshape(-1, short_taps.shape[2]),
+        ((0, TAIL_ROWS - short_taps.shape[0] * short_taps.shape[1]), (0, 0)),
+    )
+    before = shifted(last_rows(query_proj, key_proj, value_proj), "seq", 1)
+    product = gated_product(taps, before, key_proj, value_proj)
+    product, before = lax.optimization_barrier((product, before))
+    spread = lax.all_to_all(
+        product.reshape(seq_count, channels, width), "seq", split_axis=0, concat_axis=0, tiled=True
+    )
+    queries = [
+        to_plane_of_rows(message, lambda z, q: (z ^ offset, q))
+        for offset, message in enumerate(query_shares(place, taps, before, query_proj, planes))
+    ]
+    mixed = convolve(place, spread, long_filters, PLANE)
+    mixed, queries = lax.optimization_barrier((mixed, queries))
+    landed = [
+        to_plane_of_rows(message, lambda z, q: (z, q ^ offset))
+        for offset, message in enumerate(mixed)
+    ]
+    landed[0], out_weight = lax.optimization_barrier((landed[0], out_weight))
+    rows.append(from_neighbours(*spans[1]))
+    own = gate(place, landed, queries)
+    gates = [own, lax.ppermute(own, "tp", [(0, 1), (1, 0)])]
+
+    parts, sums, sent = [], [], []
+    for index in range(2 * len(spans)):
+        if index == 2:
+            sent += [lax.ppermute(sums[0], "seq", up), lax.ppermute(sums[1], "seq", down)]
+            rows[1], sums = lax.optimization_barrier((rows[1], sums))
+            rows[1] = from_corner(*rows[1])
+            gates, parts, sums = lax.optimization_barrier((gates, parts, sums))
+        elif index == 3:
+            gates, sent = lax.optimization_barrier((gates, sent))
+        weights, count = rows[index // 2], spans[index // 2][1] // 2
+        forth, back = (up, down) if index % 2 == 0 else (down, up)
+        far, ahead, behind, mine = project(place, gates, weights, count * (index % 2), count)
+        if index % 2 == 1:
+            ahead, behind = behind, ahead
+        far = lax.ppermute(far, "seq", forth)
+        near = lax.ppermute(behind, "seq", back)
+        sums.append((ahead.astype(jnp.float32) + far.astype(jnp.float32)).astype(jnp.bfloat16))
+        parts.append(mine + near.astype(jnp.float32))
+    sent += [lax.ppermute(sums[-2], "seq", up), lax.ppermute(sums[-1], "seq", down)]
+    columns = [part + value.astype(jnp.float32) for part, value in zip(parts, sent)]
+    return jnp.concatenate(columns, axis=1).astype(jnp.bfloat16)
+
+
+PRECISE = lax.Precision.HIGHEST
+
+
 def phase_table(period, out_size, in_size, direction):
     out_index = lax.broadcasted_iota(jnp.int32, (out_size, in_size), 0)
     in_index = lax.broadcasted_iota(jnp.int32, (out_size, in_size), 1)
@@ -32,11 +408,11 @@
 
 
 def left_apply(phase, signal):
-    return jnp.einsum("kn,cnm->ckm", phase, signal, precision=precise)
+    return jnp.einsum("kn,cnm->ckm", phase, signal, precision=PRECISE)
 
 
 def right_apply(signal, phase):
-    return jnp.einsum("ckn,nm->ckm", signal, phase, precision=precise)
+    return jnp.einsum("ckn,nm->ckm", signal, phase, precision=PRECISE)
 
 
 def forward_spectrum(signal, inner_size):
@@ -80,24 +456,18 @@
     return inverse_signal(prod_re, prod_im, length, inner_size)
 
 
-def shards(query_proj, key_proj, value_proj, short_taps, long_filters, out_weight):
-    tok_rows = query_proj.shape[1]
-    inner_size = tok_rows // 2
-    tail_cols = jnp.stack([query_proj[:, -2:], key_proj[:, -2:], value_proj[:, -2:]])
-    before = shifted(tail_cols, "seq", 1)
-    shorts = []
-    for stream_index, stream in enumerate((query_proj, key_proj, value_proj)):
-        extended = jnp.concatenate([before[stream_index], stream], axis=1).astype(jnp.float32)
-        shorts.append(short_filter(extended, short_taps[stream_index]))
-    query_short, key_short, value_short = shorts
+def by_whole_rows(query_proj, key_proj, value_proj, short_taps, long_filters, out_weight):
+    inner_size = query_proj.shape[1] // 2
+    query_short, key_short, value_short = filtered_streams(
+        (query_proj, key_proj, value_proj), short_taps
+    )
     product = (key_short * value_short).astype(jnp.bfloat16)
     spread = lax.all_to_all(product, "seq", split_axis=0, concat_axis=1, tiled=True)
     mixed_conv = long_convolve(spread.astype(jnp.float32), long_filters, inner_size)
     returned = lax.all_to_all(mixed_conv, "seq", split_axis=1, concat_axis=0, tiled=True)
     gated_out = (query_short * returned).astype(jnp.bfloat16)
-    full_rows = lax.all_gather(gated_out, "tp", axis=0, tiled=True)
     result = lax.dot_general(
-        full_rows,
+        lax.all_gather(gated_out, "tp", axis=0, tiled=True),
         lax.all_gather(out_weight, "seq", axis=0, tiled=True),
         (((0,), (0,)), ((), ())),
         preferred_element_type=jnp.float32,
@@ -106,8 +476,10 @@
 
 
 def solution(mesh):
+    planes, cores = mesh.shape["seq"] // PLANE, mesh.shape["tp"]
+    plan = by_planes if planes == PLANE and cores == 2 else by_whole_rows
     return jax.shard_map(
-        shards,
+        plan,
         mesh=mesh,
         in_specs=(
             P("tp", "seq"),

time: 522 us -> 169 us (0.32); the launches traced: 512 us -> 169 us
  waiting for transfers between devices: 385 us -> 60.7 us
  matrix products: 73.6 us -> 0 us
  starting transfers between devices: 18.4 us -> 57.2 us
  Pallas kernels: 0 us -> 29.4 us
  other arithmetic: 11 us -> 1.84 us
    all_gather x2 -> x1, waiting for transfers between devices: 363 us -> 0.01 us  [by_planes(): lax.all_gather(early, 'seq', axis=0, tiled=True, axis_index_groups=groups)]
    dot_general x19 -> x0, matrix products: 73.6 us -> none  [the longest x12 42.7 us: right_apply(): return jnp.einsum('ckn,nm->ckm', signal, phase, precision=precise)]
    ppermute x0 -> x25, waiting for transfers between devices: none -> 54 us  [the longest x4 19.2 us: by_planes(): far = lax.ppermute(far, 'seq', forth)]
    ppermute x0 -> x25, starting transfers between devices: none -> 44.5 us  [the longest x8 12.2 us: to_plane_of_rows(): return lax.ppermute(message, ('seq', 'tp'), pairs)]
    pallas_call x0 -> x9, Pallas kernels: none -> 29.4 us  [the longest x1 15.4 us: convolve(): pl.pallas_call(conv_kernel, out_shape=[jax.ShapeDtypeStruct((blocks // in...]
    all_to_all x2 -> x1, waiting for transfers between devices: 20.9 us -> 4.88 us  [by_planes(): lax.all_to_all(product.reshape(seq_count, channels, width), 'seq', split_...]
    convert_element_type x4, other arithmetic: 10.5 us -> 0.26 us  [by_planes(): (ahead.astype(jnp.float32) + far.astype(jnp.float32)).astype(jnp.bfloat16)]
    all_to_all x2 -> x1, starting transfers between devices: 13.3 us -> 7.73 us  [by_planes(): lax.all_to_all(product.reshape(seq_count, channels, width), 'seq', split_...]
  transfers between devices with their start and end apart: 5 -> 28, of which waited for: 3 -> 13; matrix products, arithmetic and copies ran while one was open for 6% -> 1% of each run, Pallas kernels for 0% -> 17%
where the time goes in v4:
time: 169 us
  waiting for transfers between devices  60.7 us (36%)
  starting transfers between devices  57.2 us (34%)
  Pallas kernels  29.4 us (17%)
  between operations  13.7 us (8%)
  local copies, waits for them, and re-layouts  5.87 us (3%)
  other arithmetic  1.84 us (1%)
    ppermute x4, waiting for transfers between devices, by_planes(): far = lax.ppermute(far, 'seq', forth)  19.2 us
    pallas_call x1, Pallas kernels, convolve(): pl.pallas_call(conv_kernel, out_shape=[jax.ShapeDtypeStruct((blocks // in...  15.4 us
    ppermute x4, waiting for transfers between devices, by_planes(): near = lax.ppermute(behind, 'seq', back)  15 us
    ppermute x8, starting transfers between devices, to_plane_of_rows(): return lax.ppermute(message, ('seq', 'tp'), pairs)  12.2 us
    ppermute x8, waiting for transfers between devices, to_plane_of_rows(): return lax.ppermute(message, ('seq', 'tp'), pairs)  10.2 us
    ppermute x4, starting transfers between devices, by_planes(): far = lax.ppermute(far, 'seq', forth)  9.72 us
    pallas_call x4, Pallas kernels, project(): pl.pallas_call(project_kernel, out_shape=[jax.ShapeDtypeStruct((rows, col...  9.66 us
    all_to_all x1, starting transfers between devices, by_planes(): lax.all_to_all(product.reshape(seq_count, channels, width), 'seq', split_...  7.73 us
  transfers between devices with their start and end apart: 28, of which 13 were waited for; matrix products, arithmetic and copies ran while one was open for 1% of the time, Pallas kernels for 17%

profile of v4, /device:TPU:0, one launch (start us, length us, event | category | flops | bytes accessed | tf_op | source)
XLA Modules:
  0.0 168.8 jit_solution(6557909741264518264)
XLA Ops:
  6.6 2.4 %slice.12 = bf16[256,2048]{1,0:T(8,128)(2,1)} slice(bf16[256,4096]{1,0:T(8,128)(2,1)} %param.11), slice={[0:256], [0:2048]} | slice | bytes 2097152 | tf_op jit(solution)/shard_map/slice | solution.py:347
  9.1 0.5 shard_map.64
  9.6 5.0 %collective-permute-start = (bf16[16,2048]{1,0:T(8,128)(2,1)S(1)}, bf16[16,2048]{1,0:T(8,128)(2,1)S(1)}, u32[]{:S(2)}, u32[]{:S(2)}) collective-permute-start(bf16[16,2048]{1,0:T(8,128)(2,1)S(1)} %shard_map.64), channel_id=1, source_target_pairs={{0,2},{2,4},{4,6},{6,8},{8,10},{10,12},{12,14},{14,16},{16,18},{18... | collective-permute-start | bytes 196616 | tf_op jit(solution)/shard_map/ppermute | solution.py:19
  14.6 1.8 %collective-permute-done.before_ref = bf16[16,2048]{1,0:T(8,128)(2,1)S(1)} collective-permute-done((bf16[16,2048]{1,0:T(8,128)(2,1)S(1)}, bf16[16,2048]{1,0:T(8,128)(2,1)S(1)}, u32[]{:S(2)}, u32[]{:S(2)}) %collective-permute-start) | collective-permute-done | bytes 65568 | tf_op jit(solution)/shard_map/ppermute | solution.py:19
  16.4 1.9 %shard_map.65 = bf16[2048,128]{1,0:T(8,128)(2,1)} custom-call(f32[16,2048]{1,0:T(8,128)S(1)} %pad.4.taps_ref, bf16[16,2048]{1,0:T(8,128)(2,1)S(1)} %collective-permute-done.before_ref, bf16[2048,128]{1,0:T(8,128)(2,1)S(1)} %copy-done.1, bf16[2048,128]{1,0:T(8,128)(2,1)S(1)} %copy-done.2), custom_call_target="tpu_custom_call" | custom-call | tf_op jit(solution)/shard_map/pallas_call | solution.py:105
  18.3 7.7 %all-to-all-start = ((bf16[16,128,128]{2,1,0:T(8,128)(2,1)}), bf16[16,128,128]{2,1,0:T(8,128)(2,1)S(1)}, u32[]{:S(2)}, u32[]{:S(2)}) async-start(bf16[16,128,128]{2,1,0:T(8,128)(2,1)} %bitcast.3), calls=%async_computation | async-start | bytes 1048576 | tf_op jit(solution)/shard_map/all_to_all | solution.py:357
  26.2 1.1 shard_map.67
  27.3 0.7 collective-permute-start.1
  28.0 4.2 %collective-permute-start.2 = (bf16[4,128,128]{2,1,0:T(8,128)(2,1)S(1)}, bf16[4,128,128]{2,1,0:T(8,128)(2,1)S(1)}, u32[]{:S(2)}, u32[]{:S(2)}) collective-permute-start(bf16[4,128,128]{2,1,0:T(8,128)(2,1)S(1)} %get-tuple-element.59), channel_id=1, source_target_pairs={{0,1},{1,17},{2,3},{3,19},{4,5},{5,21},{6,7},{7,23},{8,0},{9,16},{... | collective-permute-start | bytes 393224 | tf_op jit(solution)/shard_map/ppermute | solution.py:328
  32.2 3.1 %collective-permute-start.4 = (bf16[4,128,128]{2,1,0:T(8,128)(2,1)S(1)}, bf16[4,128,128]{2,1,0:T(8,128)(2,1)S(1)}, u32[]{:S(2)}, u32[]{:S(2)}) collective-permute-start(bf16[4,128,128]{2,1,0:T(8,128)(2,1)S(1)} %get-tuple-element.61), channel_id=1, source_target_pairs={{0,9},{1,25},{2,11},{3,27},{4,13},{5,29},{6,15},{7,31},{8,8},{9,24... | collective-permute-start | bytes 393224 | tf_op jit(solution)/shard_map/ppermute | solution.py:328
  35.3 4.9 %all-to-all-done.x_ref = bf16[16,128,128]{2,1,0:T(8,128)(2,1)S(1)} async-done(((bf16[16,128,128]{2,1,0:T(8,128)(2,1)}), bf16[16,128,128]{2,1,0:T(8,128)(2,1)S(1)}, u32[]{:S(2)}, u32[]{:S(2)}) %all-to-all-start) | async-done | bytes 524320 | tf_op jit(solution)/shard_map/all_to_all | solution.py:357
  40.2 15.4 %shard_map.66 = (bf16[4,128,128]{2,1,0:T(8,128)(2,1)S(1)}, bf16[4,128,128]{2,1,0:T(8,128)(2,1)S(1)}, bf16[4,128,128]{2,1,0:T(8,128)(2,1)S(1)}, bf16[4,128,128]{2,1,0:T(8,128)(2,1)S(1)}) custom-call(s32[3]{0:T(128)S(1)} %pad_add_fusion.place_ref, bf16[16,128,128]{2,1,0:T(8,128)(2,1)S(1)} %all-to-all-done.x_ref, f32[128,2048]{1,0:T(8,128)S(1)} %copy-done.4), custom_call_target="tpu_custom_call" | custom-call | flops 8589934592 | bytes 2621440 | tf_op jit(solution)/shard_map/pallas_call | solution.py:212
  55.7 0.7 collective-permute-start.5
  56.3 1.3 collective-permute-start.6
  57.6 0.3 collective-permute-start.7
  57.9 2.0 %collective-permute-start.8 = (bf16[4,128,128]{2,1,0:T(8,128)(2,1)S(1)}, bf16[4,128,128]{2,1,0:T(8,128)(2,1)S(1)}, u32[]{:S(2)}, u32[]{:S(2)}) collective-permute-start(bf16[4,128,128]{2,1,0:T(8,128)(2,1)S(1)} %get-tuple-element.66), channel_id=1, source_target_pairs={{0,6},{1,22},{2,4},{3,20},{4,2},{5,18},{6,0},{7,16},{8,7},{9,23},{... | collective-permute-start | bytes 393224 | tf_op jit(solution)/shard_map/ppermute | solution.py:328
  59.9 4.3 %collective-permute-done.6.refs_1_ = bf16[4,128,128]{2,1,0:T(8,128)(2,1)S(1)} collective-permute-done((bf16[4,128,128]{2,1,0:T(8,128)(2,1)S(1)}, bf16[4,128,128]{2,1,0:T(8,128)(2,1)S(1)}, u32[]{:S(2)}, u32[]{:S(2)}) %collective-permute-start.6) | collective-permute-done | bytes 131104 | tf_op jit(solution)/shard_map/ppermute | solution.py:328
  64.1 1.7 %collective-permute-done.7.refs_2_ = bf16[4,128,128]{2,1,0:T(8,128)(2,1)S(1)} collective-permute-done((bf16[4,128,128]{2,1,0:T(8,128)(2,1)S(1)}, bf16[4,128,128]{2,1,0:T(8,128)(2,1)S(1)}, u32[]{:S(2)}, u32[]{:S(2)}) %collective-permute-start.7) | collective-permute-done | bytes 131104 | tf_op jit(solution)/shard_map/ppermute | solution.py:328
  65.8 4.2 %collective-permute-done.8.refs_3_ = bf16[4,128,128]{2,1,0:T(8,128)(2,1)S(1)} collective-permute-done((bf16[4,128,128]{2,1,0:T(8,128)(2,1)S(1)}, bf16[4,128,128]{2,1,0:T(8,128)(2,1)S(1)}, u32[]{:S(2)}, u32[]{:S(2)}) %collective-permute-start.8) | collective-permute-done | bytes 131104 | tf_op jit(solution)/shard_map/ppermute | solution.py:328
  70.0 0.8 shard_map.68.own_ref
  70.8 3.1 %collective-permute-start.9 = (bf16[4,4,128,128]{3,2,1,0:T(8,128)(2,1)S(1)}, bf16[4,4,128,128]{3,2,1,0:T(8,128)(2,1)S(1)}, u32[]{:S(2)}, u32[]{:S(2)}) collective-permute-start(bf16[4,4,128,128]{3,2,1,0:T(8,128)(2,1)S(1)} %shard_map.68.own_ref), channel_id=1, source_target_pairs={{0,1},{1,0},{2,3},{3,2},{4,5},{5,4},{6,7},{7,6},{8,9},{9,8},{10,11... | collective-permute-start | bytes 1572872 | tf_op jit(solution)/shard_map/ppermute | solution.py:373
  74.0 1.5 collective-permute-start.16
  75.4 2.0 %collective-permute-start.17 = (bf16[256,2048]{1,0:T(8,128)(2,1)S(1)}, bf16[256,2048]{1,0:T(8,128)(2,1)}, u32[]{:S(2)}, u32[]{:S(2)}) collective-permute-start(bf16[256,2048]{1,0:T(8,128)(2,1)S(1)} %slice.13.refs_0_), channel_id=1, source_target_pairs={{0,4},{2,6},{4,0},{6,2},{8,12},{10,14},{12,8},{14,10},{16,20},{18,... | collective-permute-start | bytes 3145736 | tf_op jit(solution)/shard_map/ppermute | solution.py:332
  77.4 2.2 %copy-done = bf16[1024,2048]{1,0:T(8,128)(2,1)S(1)} copy-done((bf16[1024,2048]{1,0:T(8,128)(2,1)S(1)}, bf16[1024,2048]{1,0:T(8,128)(2,1)}, u32[]{:S(2)}) %copy-start) | copy-done | bytes 4194328
  79.6 1.9 %shard_map.70 = (bf16[128,1024]{1,0:T(8,128)(2,1)S(1)}, bf16[128,1024]{1,0:T(8,128)(2,1)S(1)}, bf16[128,1024]{1,0:T(8,128)(2,1)S(1)}, f32[128,1024]{1,0:T(8,128)S(1)}) custom-call(s32[3]{0:T(128)S(1)} %pad_add_fusion.place_ref, bf16[4,4,128,128]{3,2,1,0:T(8,128)(2,1)S(1)} %shard_map.68.own_ref, ...), custom_call_target="tpu_custom_call" | custom-call | flops 131072 | tf_op jit(solution)/shard_map/pallas_call | solution.py:294
  81.5 1.5 collective-permute-start.14
  83.0 1.9 %shard_map.69 = (bf16[128,1024]{1,0:T(8,128)(2,1)S(1)}, bf16[128,1024]{1,0:T(8,128)(2,1)S(1)}, bf16[128,1024]{1,0:T(8,128)(2,1)S(1)}, f32[128,1024]{1,0:T(8,128)S(1)}) custom-call(s32[3]{0:T(128)S(1)} %pad_add_fusion.place_ref, bf16[4,4,128,128]{3,2,1,0:T(8,128)(2,1)S(1)} %shard_map.68.own_ref, ...), custom_call_target="tpu_custom_call" | custom-call | flops 131072 | tf_op jit(solution)/shard_map/pallas_call | solution.py:294
  84.9 3.6 %collective-permute-start.12 = (bf16[128,1024]{1,0:T(8,128)(2,1)S(1)}, bf16[128,1024]{1,0:T(8,128)(2,1)S(1)}, u32[]{:S(2)}, u32[]{:S(2)}) collective-permute-start(bf16[128,1024]{1,0:T(8,128)(2,1)S(1)} %get-tuple-element.79), channel_id=1, source_target_pairs={{0,8},{2,10},{4,12},{6,14},{8,16},{10,18},{12,20},{14,22},{16,24},... | collective-permute-start | bytes 786440 | tf_op jit(solution)/shard_map/ppermute | solution.py:389
  88.4 2.0 %collective-permute-start.11 = (bf16[128,1024]{1,0:T(8,128)(2,1)S(1)}, bf16[128,1024]{1,0:T(8,128)(2,1)S(1)}, u32[]{:S(2)}, u32[]{:S(2)}) collective-permute-start(bf16[128,1024]{1,0:T(8,128)(2,1)S(1)} %get-tuple-element.74), channel_id=1, source_target_pairs={{0,8},{2,10},{4,12},{6,14},{8,16},{10,18},{12,20},{14,22},{16,24},... | collective-permute-start | bytes 786440 | tf_op jit(solution)/shard_map/ppermute | solution.py:390
  90.5 3.1 %collective-permute-done.14 = bf16[128,1024]{1,0:T(8,128)(2,1)S(1)} collective-permute-done((bf16[128,1024]{1,0:T(8,128)(2,1)S(1)}, bf16[128,1024]{1,0:T(8,128)(2,1)S(1)}, u32[]{:S(2)}, u32[]{:S(2)}) %collective-permute-start.14) | collective-permute-done | bytes 262176 | tf_op jit(solution)/shard_map/ppermute | solution.py:389
  93.6 7.4 %collective-permute-done.12 = bf16[128,1024]{1,0:T(8,128)(2,1)S(1)} collective-permute-done((bf16[128,1024]{1,0:T(8,128)(2,1)S(1)}, bf16[128,1024]{1,0:T(8,128)(2,1)S(1)}, u32[]{:S(2)}, u32[]{:S(2)}) %collective-permute-start.12) | collective-permute-done | bytes 262176 | tf_op jit(solution)/shard_map/ppermute | solution.py:389
  101.2 1.1 slice.14
  102.3 1.0 collective-permute-start.18
  103.3 0.9 collective-permute-start.19
  104.2 1.9 %collective-permute-start.10 = (bf16[128,1024]{1,0:T(8,128)(2,1)S(1)}, bf16[128,1024]{1,0:T(8,128)(2,1)S(1)}, u32[]{:S(2)}, u32[]{:S(2)}) collective-permute-start(bf16[128,1024]{1,0:T(8,128)(2,1)S(1)} %get-tuple-element.72), channel_id=1, source_target_pairs={{8,0},{10,2},{12,4},{14,6},{16,8},{18,10},{20,12},{22,14},{24,16},... | collective-permute-start | bytes 786440 | tf_op jit(solution)/shard_map/ppermute | solution.py:390
  106.1 5.1 %collective-permute-start.15 = (bf16[128,1024]{1,0:T(8,128)(2,1)S(1)}, bf16[128,1024]{1,0:T(8,128)(2,1)S(1)}, u32[]{:S(2)}, u32[]{:S(2)}) collective-permute-start(bf16[128,1024]{1,0:T(8,128)(2,1)S(1)} %add_convert_fusion.6), channel_id=1, source_target_pairs={{8,0},{10,2},{12,4},{14,6},{16,8},{18,10},{20,12},{22,14},{24,16},... | collective-permute-start | bytes 786440 | tf_op jit(solution)/shard_map/ppermute | solution.py:378
  111.3 5.6 %collective-permute-done.10 = bf16[128,1024]{1,0:T(8,128)(2,1)S(1)} collective-permute-done((bf16[128,1024]{1,0:T(8,128)(2,1)S(1)}, bf16[128,1024]{1,0:T(8,128)(2,1)S(1)}, u32[]{:S(2)}, u32[]{:S(2)}) %collective-permute-start.10) | collective-permute-done | bytes 262176 | tf_op jit(solution)/shard_map/ppermute | solution.py:390
  117.0 3.0 %shard_map.71 = (bf16[128,1024]{1,0:T(8,128)(2,1)S(1)}, bf16[128,1024]{1,0:T(8,128)(2,1)S(1)}, bf16[128,1024]{1,0:T(8,128)(2,1)S(1)}, f32[128,1024]{1,0:T(8,128)S(1)}) custom-call(s32[3]{0:T(128)S(1)} %pad_add_fusion.place_ref, bf16[4,4,128,128]{3,2,1,0:T(8,128)(2,1)S(1)} %shard_map.68.own_ref, ...), custom_call_target="tpu_custom_call" | custom-call | flops 131072 | tf_op jit(solution)/shard_map/pallas_call | solution.py:294
  120.0 4.6 %collective-permute-start.21 = (bf16[128,1024]{1,0:T(8,128)(2,1)S(1)}, bf16[128,1024]{1,0:T(8,128)(2,1)S(1)}, u32[]{:S(2)}, u32[]{:S(2)}) collective-permute-start(bf16[128,1024]{1,0:T(8,128)(2,1)S(1)} %get-tuple-element.92), channel_id=1, source_target_pairs={{0,8},{2,10},{4,12},{6,14},{8,16},{10,18},{12,20},{14,22},{16,24},... | collective-permute-start | bytes 786440 | tf_op jit(solution)/shard_map/ppermute | solution.py:389
  124.6 5.2 %collective-permute-done.13 = bf16[128,1024]{1,0:T(8,128)(2,1)S(1)} collective-permute-done((bf16[128,1024]{1,0:T(8,128)(2,1)S(1)}, bf16[128,1024]{1,0:T(8,128)(2,1)S(1)}, u32[]{:S(2)}, u32[]{:S(2)}) %collective-permute-start.13) | collective-permute-done | bytes 262176 | tf_op jit(solution)/shard_map/ppermute | solution.py:378
  129.8 3.0 %shard_map.72 = (bf16[128,1024]{1,0:T(8,128)(2,1)S(1)}, bf16[128,1024]{1,0:T(8,128)(2,1)S(1)}, bf16[128,1024]{1,0:T(8,128)(2,1)S(1)}, f32[128,1024]{1,0:T(8,128)S(1)}) custom-call(s32[3]{0:T(128)S(1)} %pad_add_fusion.place_ref, bf16[4,4,128,128]{3,2,1,0:T(8,128)(2,1)S(1)} %shard_map.68.own_ref, ...), custom_call_target="tpu_custom_call" | custom-call | flops 131072 | tf_op jit(solution)/shard_map/pallas_call | solution.py:294
  132.8 2.8 %collective-permute-start.20 = (bf16[128,1024]{1,0:T(8,128)(2,1)S(1)}, bf16[128,1024]{1,0:T(8,128)(2,1)S(1)}, u32[]{:S(2)}, u32[]{:S(2)}) collective-permute-start(bf16[128,1024]{1,0:T(8,128)(2,1)S(1)} %get-tuple-element.90), channel_id=1, source_target_pairs={{8,0},{10,2},{12,4},{14,6},{16,8},{18,10},{20,12},{22,14},{24,16},... | collective-permute-start | bytes 786440 | tf_op jit(solution)/shard_map/ppermute | solution.py:390
  135.9 2.0 %collective-permute-start.22 = (bf16[128,1024]{1,0:T(8,128)(2,1)S(1)}, bf16[128,1024]{1,0:T(8,128)(2,1)S(1)}, u32[]{:S(2)}, u32[]{:S(2)}) collective-permute-start(bf16[128,1024]{1,0:T(8,128)(2,1)S(1)} %add_convert_fusion.3), channel_id=1, source_target_pairs={{0,8},{2,10},{4,12},{6,14},{8,16},{10,18},{12,20},{14,22},{16,24},... | collective-permute-start | bytes 786440 | tf_op jit(solution)/shard_map/ppermute | solution.py:393
  137.9 8.7 %collective-permute-done.24 = bf16[128,1024]{1,0:T(8,128)(2,1)S(1)} collective-permute-done((bf16[128,1024]{1,0:T(8,128)(2,1)S(1)}, bf16[128,1024]{1,0:T(8,128)(2,1)S(1)}, u32[]{:S(2)}, u32[]{:S(2)}) %collective-permute-start.24) | collective-permute-done | bytes 262176 | tf_op jit(solution)/shard_map/ppermute | solution.py:389
  146.9 9.3 %collective-permute-done.20 = bf16[128,1024]{1,0:T(8,128)(2,1)S(1)} collective-permute-done((bf16[128,1024]{1,0:T(8,128)(2,1)S(1)}, bf16[128,1024]{1,0:T(8,128)(2,1)S(1)}, u32[]{:S(2)}, u32[]{:S(2)}) %collective-permute-start.20) | collective-permute-done | bytes 262176 | tf_op jit(solution)/shard_map/ppermute | solution.py:390
  156.2 1.8 %collective-permute-done.22 = bf16[128,1024]{1,0:T(8,128)(2,1)S(1)} collective-permute-done((bf16[128,1024]{1,0:T(8,128)(2,1)S(1)}, bf16[128,1024]{1,0:T(8,128)(2,1)S(1)}, u32[]{:S(2)}, u32[]{:S(2)}) %collective-permute-start.22) | collective-permute-done | bytes 262176 | tf_op jit(solution)/shard_map/ppermute | solution.py:393
  158.2 2.6 %collective-permute-done.25 = bf16[128,1024]{1,0:T(8,128)(2,1)S(1)} collective-permute-done((bf16[128,1024]{1,0:T(8,128)(2,1)S(1)}, bf16[128,1024]{1,0:T(8,128)(2,1)S(1)}, u32[]{:S(2)}, u32[]{:S(2)}) %collective-permute-start.25) | collective-permute-done | bytes 262176 | tf_op jit(solution)/shard_map/ppermute | solution.py:393
  160.9 1.0 pad_maximum_fusion
  (49 shorter events, 1.4 us)
Async XLA Ops:
  6.5 2.5 %copy-start.3 = (bf16[2048,128]{1,0:T(8,128)(2,1)S(1)}, bf16[2048,128]{1,0:T(8,128)(2,1)}, u32[]{:S(2)}) copy-start(bf16[2048,128]{1,0:T(8,128)(2,1)} %query_ref.3) | copy-start | bytes 1572868
  6.5 2.5 %copy-start.1 = (bf16[2048,128]{1,0:T(8,128)(2,1)S(1)}, bf16[2048,128]{1,0:T(8,128)(2,1)}, u32[]{:S(2)}) copy-start(bf16[2048,128]{1,0:T(8,128)(2,1)} %key_ref.3) | copy-start | bytes 1572868
  6.5 2.5 %copy-start.2 = (bf16[2048,128]{1,0:T(8,128)(2,1)S(1)}, bf16[2048,128]{1,0:T(8,128)(2,1)}, u32[]{:S(2)}) copy-start(bf16[2048,128]{1,0:T(8,128)(2,1)} %value_ref.3) | copy-start | bytes 1572868
  6.5 8.0 %copy-start.6 = (f32[3,3,2048]{2,1,0:T(4,128)S(1)}, f32[3,3,2048]{2,1,0:T(4,128)}, u32[]{:S(2)}) copy-start(f32[3,3,2048]{2,1,0:T(4,128)} %param.9) | copy-start | bytes 221188
  6.5 70.9 %all-gather.2.cloned.1.call-start = ((), (), s32[]{:S(2)}) async-start(), calls=%async_computation.1 | async-start | bytes 5242880 | tf_op jit(solution)/shard_map/all_gather | solution.py:348
  9.6 30.6 %copy-start.4 = (f32[128,2048]{1,0:T(8,128)S(1)}, f32[128,2048]{1,0:T(8,128)}, u32[]{:S(2)}) copy-start(f32[128,2048]{1,0:T(8,128)} %h_ref.1) | copy-start | bytes 3145732
  9.6 6.9 %collective-permute-start = (bf16[16,2048]{1,0:T(8,128)(2,1)S(1)}, bf16[16,2048]{1,0:T(8,128)(2,1)S(1)}, u32[]{:S(2)}, u32[]{:S(2)}) collective-permute-start(bf16[16,2048]{1,0:T(8,128)(2,1)S(1)} %shard_map.64), channel_id=1, source_target_pairs={{0,2},{2,4},{4,6},{6,8},{8,10},{10,12},{12,14},{14,16},{16,18},{18... | collective-permute-start | bytes 196616 | tf_op jit(solution)/shard_map/ppermute | solution.py:19
  18.3 21.8 %all-to-all-start = ((bf16[16,128,128]{2,1,0:T(8,128)(2,1)}), bf16[16,128,128]{2,1,0:T(8,128)(2,1)S(1)}, u32[]{:S(2)}, u32[]{:S(2)}) async-start(bf16[16,128,128]{2,1,0:T(8,128)(2,1)} %bitcast.3), calls=%async_computation | async-start | bytes 1048576 | tf_op jit(solution)/shard_map/all_to_all | solution.py:357
  27.3 28.3 %collective-permute-start.1 = (bf16[4,128,128]{2,1,0:T(8,128)(2,1)S(1)}, bf16[4,128,128]{2,1,0:T(8,128)(2,1)S(1)}, u32[]{:S(2)}, u32[]{:S(2)}) collective-permute-start(bf16[4,128,128]{2,1,0:T(8,128)(2,1)S(1)} %get-tuple-element.58), channel_id=1, source_target_pairs={{0,0},{1,16},{2,2},{3,18},{4,4},{5,20},{6,6},{7,22},{8,1},{9,17},{... | collective-permute-start | bytes 393224 | tf_op jit(solution)/shard_map/ppermute | solution.py:328
  28.0 27.7 %collective-permute-start.2 = (bf16[4,128,128]{2,1,0:T(8,128)(2,1)S(1)}, bf16[4,128,128]{2,1,0:T(8,128)(2,1)S(1)}, u32[]{:S(2)}, u32[]{:S(2)}) collective-permute-start(bf16[4,128,128]{2,1,0:T(8,128)(2,1)S(1)} %get-tuple-element.59), channel_id=1, source_target_pairs={{0,1},{1,17},{2,3},{3,19},{4,5},{5,21},{6,7},{7,23},{8,0},{9,16},{... | collective-permute-start | bytes 393224 | tf_op jit(solution)/shard_map/ppermute | solution.py:328
  32.2 23.4 %collective-permute-start.3 = (bf16[4,128,128]{2,1,0:T(8,128)(2,1)S(1)}, bf16[4,128,128]{2,1,0:T(8,128)(2,1)S(1)}, u32[]{:S(2)}, u32[]{:S(2)}) collective-permute-start(bf16[4,128,128]{2,1,0:T(8,128)(2,1)S(1)} %get-tuple-element.60), channel_id=1, source_target_pairs={{0,8},{1,24},{2,10},{3,26},{4,12},{5,28},{6,14},{7,30},{8,9},{9,25... | collective-permute-start | bytes 393224 | tf_op jit(solution)/shard_map/ppermute | solution.py:328
  32.2 23.5 %collective-permute-start.4 = (bf16[4,128,128]{2,1,0:T(8,128)(2,1)S(1)}, bf16[4,128,128]{2,1,0:T(8,128)(2,1)S(1)}, u32[]{:S(2)}, u32[]{:S(2)}) collective-permute-start(bf16[4,128,128]{2,1,0:T(8,128)(2,1)S(1)} %get-tuple-element.61), channel_id=1, source_target_pairs={{0,9},{1,25},{2,11},{3,27},{4,13},{5,29},{6,15},{7,31},{8,8},{9,24... | collective-permute-start | bytes 393224 | tf_op jit(solution)/shard_map/ppermute | solution.py:328
  40.2 33.7 %copy-start.5 = (bf16[256,4096]{1,0:T(8,128)(2,1)S(1)}, bf16[256,4096]{1,0:T(8,128)(2,1)}, u32[]{:S(2)}) copy-start(bf16[256,4096]{1,0:T(8,128)(2,1)} %param.11) | copy-start | bytes 6291460
  55.7 4.2 %collective-permute-start.5 = (bf16[4,128,128]{2,1,0:T(8,128)(2,1)S(1)}, bf16[4,128,128]{2,1,0:T(8,128)(2,1)S(1)}, u32[]{:S(2)}, u32[]{:S(2)}) collective-permute-start(bf16[4,128,128]{2,1,0:T(8,128)(2,1)S(1)} %get-tuple-element.62), channel_id=1, source_target_pairs={{0,0},{1,16},{2,2},{3,18},{4,4},{5,20},{6,6},{7,22},{8,1},{9,17},{... | collective-permute-start | bytes 393224 | tf_op jit(solution)/shard_map/ppermute | solution.py:328
  56.3 7.8 %collective-permute-start.6 = (bf16[4,128,128]{2,1,0:T(8,128)(2,1)S(1)}, bf16[4,128,128]{2,1,0:T(8,128)(2,1)S(1)}, u32[]{:S(2)}, u32[]{:S(2)}) collective-permute-start(bf16[4,128,128]{2,1,0:T(8,128)(2,1)S(1)} %get-tuple-element.64), channel_id=1, source_target_pairs={{0,2},{1,18},{2,0},{3,16},{4,6},{5,22},{6,4},{7,20},{8,3},{9,19},{... | collective-permute-start | bytes 393224 | tf_op jit(solution)/shard_map/ppermute | solution.py:328
  57.6 8.2 %collective-permute-start.7 = (bf16[4,128,128]{2,1,0:T(8,128)(2,1)S(1)}, bf16[4,128,128]{2,1,0:T(8,128)(2,1)S(1)}, u32[]{:S(2)}, u32[]{:S(2)}) collective-permute-start(bf16[4,128,128]{2,1,0:T(8,128)(2,1)S(1)} %get-tuple-element.65), channel_id=1, source_target_pairs={{0,4},{1,20},{2,6},{3,22},{4,0},{5,16},{6,2},{7,18},{8,5},{9,21},{... | collective-permute-start | bytes 393224 | tf_op jit(solution)/shard_map/ppermute | solution.py:328
  57.9 12.1 %collective-permute-start.8 = (bf16[4,128,128]{2,1,0:T(8,128)(2,1)S(1)}, bf16[4,128,128]{2,1,0:T(8,128)(2,1)S(1)}, u32[]{:S(2)}, u32[]{:S(2)}) collective-permute-start(bf16[4,128,128]{2,1,0:T(8,128)(2,1)S(1)} %get-tuple-element.66), channel_id=1, source_target_pairs={{0,6},{1,22},{2,4},{3,20},{4,2},{5,18},{6,0},{7,16},{8,7},{9,23},{... | collective-permute-start | bytes 393224 | tf_op jit(solution)/shard_map/ppermute | solution.py:328
  70.8 6.6 %collective-permute-start.9 = (bf16[4,4,128,128]{3,2,1,0:T(8,128)(2,1)S(1)}, bf16[4,4,128,128]{3,2,1,0:T(8,128)(2,1)S(1)}, u32[]{:S(2)}, u32[]{:S(2)}) collective-permute-start(bf16[4,4,128,128]{3,2,1,0:T(8,128)(2,1)S(1)} %shard_map.68.own_ref), channel_id=1, source_target_pairs={{0,1},{1,0},{2,3},{3,2},{4,5},{5,4},{6,7},{7,6},{8,9},{9,8},{10,11... | collective-permute-start | bytes 1572872 | tf_op jit(solution)/shard_map/ppermute | solution.py:373
  74.0 27.2 %collective-permute-start.16 = (bf16[256,2048]{1,0:T(8,128)(2,1)S(1)}, bf16[256,2048]{1,0:T(8,128)(2,1)S(1)}, u32[]{:S(2)}, u32[]{:S(2)}) collective-permute-start(bf16[256,2048]{1,0:T(8,128)(2,1)S(1)} %slice.13.refs_0_), channel_id=1, source_target_pairs={{0,2},{2,0},{4,6},{6,4},{8,10},{10,8},{12,14},{14,12},{16,18},{18,... | collective-permute-start | bytes 3145736 | tf_op jit(solution)/shard_map/ppermute | solution.py:332
  75.4 25.7 %collective-permute-start.17 = (bf16[256,2048]{1,0:T(8,128)(2,1)S(1)}, bf16[256,2048]{1,0:T(8,128)(2,1)}, u32[]{:S(2)}, u32[]{:S(2)}) collective-permute-start(bf16[256,2048]{1,0:T(8,128)(2,1)S(1)} %slice.13.refs_0_), channel_id=1, source_target_pairs={{0,4},{2,6},{4,0},{6,2},{8,12},{10,14},{12,8},{14,10},{16,20},{18,... | collective-permute-start | bytes 3145736 | tf_op jit(solution)/shard_map/ppermute | solution.py:332
  77.4 2.2 %copy-start = (bf16[1024,2048]{1,0:T(8,128)(2,1)S(1)}, bf16[1024,2048]{1,0:T(8,128)(2,1)}, u32[]{:S(2)}) copy-start(bf16[1024,2048]{1,0:T(8,128)(2,1)} %all-gather.2.cloned.1.call-done.refs_0_) | copy-start | bytes 12582916
  81.5 12.1 %collective-permute-start.14 = (bf16[128,1024]{1,0:T(8,128)(2,1)S(1)}, bf16[128,1024]{1,0:T(8,128)(2,1)S(1)}, u32[]{:S(2)}, u32[]{:S(2)}) collective-permute-start(bf16[128,1024]{1,0:T(8,128)(2,1)S(1)} %get-tuple-element.81), channel_id=1, source_target_pairs={{8,0},{10,2},{12,4},{14,6},{16,8},{18,10},{20,12},{22,14},{24,16},... | collective-permute-start | bytes 786440 | tf_op jit(solution)/shard_map/ppermute | solution.py:389
  84.9 16.2 %collective-permute-start.12 = (bf16[128,1024]{1,0:T(8,128)(2,1)S(1)}, bf16[128,1024]{1,0:T(8,128)(2,1)S(1)}, u32[]{:S(2)}, u32[]{:S(2)}) collective-permute-start(bf16[128,1024]{1,0:T(8,128)(2,1)S(1)} %get-tuple-element.79), channel_id=1, source_target_pairs={{0,8},{2,10},{4,12},{6,14},{8,16},{10,18},{12,20},{14,22},{16,24},... | collective-permute-start | bytes 786440 | tf_op jit(solution)/shard_map/ppermute | solution.py:389
  88.4 22.8 %collective-permute-start.11 = (bf16[128,1024]{1,0:T(8,128)(2,1)S(1)}, bf16[128,1024]{1,0:T(8,128)(2,1)S(1)}, u32[]{:S(2)}, u32[]{:S(2)}) collective-permute-start(bf16[128,1024]{1,0:T(8,128)(2,1)S(1)} %get-tuple-element.74), channel_id=1, source_target_pairs={{0,8},{2,10},{4,12},{6,14},{8,16},{10,18},{12,20},{14,22},{16,24},... | collective-permute-start | bytes 786440 | tf_op jit(solution)/shard_map/ppermute | solution.py:390
  102.3 14.7 %collective-permute-start.18 = (bf16[128,2048]{1,0:T(8,128)(2,1)S(1)}, bf16[128,2048]{1,0:T(8,128)(2,1)S(1)}, u32[]{:S(2)}, u32[]{:S(2)}) collective-permute-start(bf16[128,2048]{1,0:T(8,128)(2,1)S(1)} %slice.14), channel_id=1, source_target_pairs={{0,2},{2,0},{4,6},{6,4},{8,10},{10,8},{12,14},{14,12},{16,18},{18,... | collective-permute-start | bytes 1572872 | tf_op jit(solution)/shard_map/ppermute | solution.py:336
  103.3 13.7 %collective-permute-start.19 = (bf16[128,2048]{1,0:T(8,128)(2,1)S(1)}, bf16[128,2048]{1,0:T(8,128)(2,1)S(1)}, u32[]{:S(2)}, u32[]{:S(2)}) collective-permute-start(bf16[128,2048]{1,0:T(8,128)(2,1)S(1)} %slice.15), channel_id=1, source_target_pairs={{0,4},{2,6},{4,0},{6,2},{8,12},{10,14},{12,8},{14,10},{16,20},{18,... | collective-permute-start | bytes 1572872 | tf_op jit(solution)/shard_map/ppermute | solution.py:337
  104.2 12.8 %collective-permute-start.10 = (bf16[128,1024]{1,0:T(8,128)(2,1)S(1)}, bf16[128,1024]{1,0:T(8,128)(2,1)S(1)}, u32[]{:S(2)}, u32[]{:S(2)}) collective-permute-start(bf16[128,1024]{1,0:T(8,128)(2,1)S(1)} %get-tuple-element.72), channel_id=1, source_target_pairs={{8,0},{10,2},{12,4},{14,6},{16,8},{18,10},{20,12},{22,14},{24,16},... | collective-permute-start | bytes 786440 | tf_op jit(solution)/shard_map/ppermute | solution.py:390
  106.1 18.5 %collective-permute-start.15 = (bf16[128,1024]{1,0:T(8,128)(2,1)S(1)}, bf16[128,1024]{1,0:T(8,128)(2,1)S(1)}, u32[]{:S(2)}, u32[]{:S(2)}) collective-permute-start(bf16[128,1024]{1,0:T(8,128)(2,1)S(1)} %add_convert_fusion.6), channel_id=1, source_target_pairs={{8,0},{10,2},{12,4},{14,6},{16,8},{18,10},{20,12},{22,14},{24,16},... | collective-permute-start | bytes 786440 | tf_op jit(solution)/shard_map/ppermute | solution.py:378
  111.2 18.5 %collective-permute-start.13 = (bf16[128,1024]{1,0:T(8,128)(2,1)S(1)}, bf16[128,1024]{1,0:T(8,128)(2,1)S(1)}, u32[]{:S(2)}, u32[]{:S(2)}) collective-permute-start(bf16[128,1024]{1,0:T(8,128)(2,1)S(1)} %add_convert_fusion.7), channel_id=1, source_target_pairs={{0,8},{2,10},{4,12},{6,14},{8,16},{10,18},{12,20},{14,22},{16,24},... | collective-permute-start | bytes 786440 | tf_op jit(solution)/shard_map/ppermute | solution.py:378
  120.0 15.8 %collective-permute-start.21 = (bf16[128,1024]{1,0:T(8,128)(2,1)S(1)}, bf16[128,1024]{1,0:T(8,128)(2,1)S(1)}, u32[]{:S(2)}, u32[]{:S(2)}) collective-permute-start(bf16[128,1024]{1,0:T(8,128)(2,1)S(1)} %get-tuple-element.92), channel_id=1, source_target_pairs={{0,8},{2,10},{4,12},{6,14},{8,16},{10,18},{12,20},{14,22},{16,24},... | collective-permute-start | bytes 786440 | tf_op jit(solution)/shard_map/ppermute | solution.py:389
  132.8 13.8 %collective-permute-start.24 = (bf16[128,1024]{1,0:T(8,128)(2,1)S(1)}, bf16[128,1024]{1,0:T(8,128)(2,1)S(1)}, u32[]{:S(2)}, u32[]{:S(2)}) collective-permute-start(bf16[128,1024]{1,0:T(8,128)(2,1)S(1)} %get-tuple-element.98), channel_id=1, source_target_pairs={{8,0},{10,2},{12,4},{14,6},{16,8},{18,10},{20,12},{22,14},{24,16},... | collective-permute-start | bytes 786440 | tf_op jit(solution)/shard_map/ppermute | solution.py:389
  132.8 23.4 %collective-permute-start.20 = (bf16[128,1024]{1,0:T(8,128)(2,1)S(1)}, bf16[128,1024]{1,0:T(8,128)(2,1)S(1)}, u32[]{:S(2)}, u32[]{:S(2)}) collective-permute-start(bf16[128,1024]{1,0:T(8,128)(2,1)S(1)} %get-tuple-element.90), channel_id=1, source_target_pairs={{8,0},{10,2},{12,4},{14,6},{16,8},{18,10},{20,12},{22,14},{24,16},... | collective-permute-start | bytes 786440 | tf_op jit(solution)/shard_map/ppermute | solution.py:390
  135.6 22.5 %collective-permute-start.23 = (bf16[128,1024]{1,0:T(8,128)(2,1)S(1)}, bf16[128,1024]{1,0:T(8,128)(2,1)S(1)}, u32[]{:S(2)}, u32[]{:S(2)}) collective-permute-start(bf16[128,1024]{1,0:T(8,128)(2,1)S(1)} %get-tuple-element.96), channel_id=1, source_target_pairs={{0,8},{2,10},{4,12},{6,14},{8,16},{10,18},{12,20},{14,22},{16,24},... | collective-permute-start | bytes 786440 | tf_op jit(solution)/shard_map/ppermute | solution.py:390
  135.9 22.2 %collective-permute-start.22 = (bf16[128,1024]{1,0:T(8,128)(2,1)S(1)}, bf16[128,1024]{1,0:T(8,128)(2,1)S(1)}, u32[]{:S(2)}, u32[]{:S(2)}) collective-permute-start(bf16[128,1024]{1,0:T(8,128)(2,1)S(1)} %add_convert_fusion.3), channel_id=1, source_target_pairs={{0,8},{2,10},{4,12},{6,14},{8,16},{10,18},{12,20},{14,22},{16,24},... | collective-permute-start | bytes 786440 | tf_op jit(solution)/shard_map/ppermute | solution.py:393
  146.7 14.1 %collective-permute-start.25 = (bf16[128,1024]{1,0:T(8,128)(2,1)S(1)}, bf16[128,1024]{1,0:T(8,128)(2,1)S(1)}, u32[]{:S(2)}, u32[]{:S(2)}) collective-permute-start(bf16[128,1024]{1,0:T(8,128)(2,1)S(1)} %add_convert_fusion.1), channel_id=1, source_target_pairs={{8,0},{10,2},{12,4},{14,6},{16,8},{18,10},{20,12},{22,14},{24,16},... | collective-permute-start | bytes 786440 | tf_op jit(solution)/shard_map/ppermute | solution.py:393
Sparse Core Ops, SparseCore 0:
  9.2 66.3 all-gather.1

commit v5 on v4

--- a/solution.py
+++ b/solution.py
@@ -8,7 +8,7 @@
 from jax.experimental.pallas import tpu as pltpu
 from jax.sharding import PartitionSpec as P
 
-COLUMN_SHARES = (16, 16)
+COLUMN_SHARES = (14, 18)
 PLANE = 4
 VMEM_LIMIT = 16 * 2**20
 
@@ -38,34 +38,22 @@
 
 VMEM = pl.BlockSpec(memory_space=pltpu.VMEM)
 SMEM = pl.BlockSpec(memory_space=pltpu.SMEM)
-TAIL_ROWS = 16
-
-
-def tails_kernel(query_ref, key_ref, value_ref, out_ref):
-    width = key_ref.shape[1]
-    row = lax.broadcasted_iota(jnp.int32, (TAIL_ROWS, width), 0)
-    lane = lax.broadcasted_iota(jnp.int32, (TAIL_ROWS, width), 1)
-    total = None
-    for index, stream in enumerate((query_ref, key_ref, value_ref)):
-        picked = (row // 2 == index) & (lane == width - 2 + row % 2)
-        term = lax.dot_general(
-            jnp.where(picked, 1.0, 0.0).astype(jnp.bfloat16),
-            stream[...],
-            (((1,), (1,)), ((), ())),
-            preferred_element_type=jnp.float32,
-        )
-        total = term if total is None else total + term
-    out_ref[...] = total.astype(out_ref.dtype)
-
-
-def last_rows(query, key, value):
-    return pl.pallas_call(
-        tails_kernel,
-        out_shape=jax.ShapeDtypeStruct((TAIL_ROWS, key.shape[0]), key.dtype),
-        in_specs=[VMEM] * 3,
-        out_specs=VMEM,
-        compiler_params=pltpu.CompilerParams(vmem_limit_bytes=VMEM_LIMIT),
-    )(query, key, value)
+EDGE_ROWS = 16
+
+
+def picked_rows(stream, pairs):
+    width = stream.shape[1]
+    row = lax.broadcasted_iota(jnp.int32, (EDGE_ROWS, width), 0)
+    lane = lax.broadcasted_iota(jnp.int32, (EDGE_ROWS, width), 1)
+    picked = functools.reduce(
+        jnp.logical_or, [(row == out) & (lane == position) for out, position in pairs]
+    )
+    return lax.dot_general(
+        jnp.where(picked, 1.0, 0.0).astype(stream.dtype),
+        stream,
+        (((1,), (1,)), ((), ())),
+        preferred_element_type=jnp.float32,
+    )
 
 
 def moved_rows(stream):
@@ -79,67 +67,59 @@
     return moved[:width], moved[width : 2 * width], moved[2 * width :]
 
 
-def short_filtered(stream, index, taps_ref, before_ref, spot):
+def short_filtered(stream, index, taps_ref, spot):
     now, once, twice = moved_rows(stream)
     tap = lambda place: taps_ref[3 * index + place : 3 * index + place + 1, spot]
-    second, first = (
-        before_ref[:, spot].astype(jnp.float32)[2 * index + place : 2 * index + place + 1]
-        for place in range(2)
-    )
-    row = lax.broadcasted_iota(jnp.int32, now.shape, 0)
-    once = jnp.where(row == 0, first, once)
-    twice = jnp.where(row == 0, second, jnp.where(row == 1, first, twice))
     return tap(0) * now + tap(1) * once + tap(2) * twice
 
 
-def product_kernel(taps_ref, before_ref, key_ref, value_ref, out_ref):
-    width = key_ref.shape[1]
-    for start in range(0, key_ref.shape[0], width):
-        spot = pl.ds(start, width)
-        key = short_filtered(key_ref[spot], 1, taps_ref, before_ref, spot)
-        value = short_filtered(value_ref[spot], 2, taps_ref, before_ref, spot)
-        out_ref[spot] = (key * value).T.astype(out_ref.dtype)
-
-
-def gated_product(taps, before, key, value):
+def product_kernel(taps_ref, key_ref, value_ref, out_ref):
+    blocks, rows, width = out_ref.shape
+    for block in range(blocks):
+        spot = pl.ds(block * width, width)
+        key, value = key_ref[spot], value_ref[spot]
+        product = short_filtered(key, 1, taps_ref, spot)
+        product = product * short_filtered(value, 2, taps_ref, spot)
+        out_ref[block, :width] = product.T.astype(out_ref.dtype)
+        places = (0, 1, width - 2, width - 1)
+        edges = picked_rows(key, list(enumerate(places)))
+        edges = edges + picked_rows(value, [(4 + out, place) for out, place in enumerate(places)])
+        out_ref[block, width:] = edges.astype(out_ref.dtype)
+
+
+def gated_product(taps, key, value):
+    channels, width = key.shape
     return pl.pallas_call(
         product_kernel,
-        out_shape=jax.ShapeDtypeStruct(key.shape, key.dtype),
-        in_specs=[VMEM] * 4,
+        out_shape=jax.ShapeDtypeStruct((channels // width, width + EDGE_ROWS, width), key.dtype),
+        in_specs=[VMEM] * 3,
         out_specs=VMEM,
         compiler_params=pltpu.CompilerParams(vmem_limit_bytes=VMEM_LIMIT),
-    )(taps, before, key, value)
-
-
-def query_kernel(place_ref, taps_ref, before_ref, query_ref, *outs):
-    width = query_ref.shape[1]
-    for offset, out in enumerate(outs):
-        share = jnp.bitwise_xor(place_ref[1], offset)
-        for step in range(out.shape[0]):
-            spot = pl.ds(pl.multiple_of((share * out.shape[0] + step) * width, width), width)
-            query = short_filtered(query_ref[spot], 0, taps_ref, before_ref, spot)
-            out[step] = query.astype(out.dtype)
-
-
-def query_shares(place, taps, before, query, count):
-    channels, width = query.shape
-    shape = (channels // count // width, width, width)
-    return pl.pallas_call(
-        query_kernel,
-        out_shape=[jax.ShapeDtypeStruct(shape, query.dtype)] * count,
-        in_specs=[SMEM] + [VMEM] * 3,
-        out_specs=[VMEM] * count,
-        compiler_params=pltpu.CompilerParams(vmem_limit_bytes=VMEM_LIMIT),
-    )(place, taps, before, query)
+    )(taps, key, value)
+
+
+def first_products(taps, edges, earlier):
+    short = []
+    for stream in range(2):
+        tap = [taps[3 * (stream + 1) + place : 3 * (stream + 1) + place + 1] for place in range(3)]
+        start, then = (edges[4 * stream + place : 4 * stream + place + 1] for place in range(2))
+        second, first = (earlier[4 * stream + place : 4 * stream + place + 1] for place in (2, 3))
+        short.append(
+            (
+                tap[0] * start + tap[1] * first + tap[2] * second,
+                tap[0] * then + tap[1] * start + tap[2] * first,
+            )
+        )
+    return [(key * value).astype(jnp.bfloat16).astype(jnp.float32) for key, value in zip(*short)]
 
 
 BAND = 32
-GROUP = 8
-
-
-def conv_kernel(place_ref, x_ref, h_ref, *rest):
-    outs, (signals_f32, turned_filters, shifted_x, result) = rest[:-4], rest[-4:]
-    blocks, channels, width = x_ref.shape
+GROUP = 16
+
+
+def conv_kernel(taps_ref, x_ref, h_ref, result, signals_f32, turned_filters, shifted_x):
+    blocks, width = x_ref.shape[0], x_ref.shape[2]
+    channels = h_ref.shape[0]
     parts = width // BAND
     band_lane = lax.broadcasted_iota(jnp.int32, (BAND, width), 1)
     keep = band_lane > lax.broadcasted_iota(jnp.int32, (BAND, width), 0)
@@ -149,8 +129,18 @@
     square_lane = lax.broadcasted_iota(jnp.int32, (width, width), 1)
     exchange = jnp.where(square_row + square_lane == width - 1, 1.0, 0.0).astype(jnp.bfloat16)
     shifted_x[...] = jnp.zeros(shifted_x.shape, jnp.float32)
+    tile_lane = lax.broadcasted_iota(jnp.int32, (channels, width), 1)
+    taps = taps_ref[...]
+    earlier_edges = jnp.zeros((EDGE_ROWS, channels), jnp.float32)
     for block in range(blocks):
-        signals_f32[block * channels : (block + 1) * channels] = x_ref[block].astype(jnp.float32)
+        edges = x_ref[block, channels:].astype(jnp.float32)
+        pair = first_products(taps, edges, earlier_edges)
+        earlier_edges = edges
+        pair_row = lax.broadcasted_iota(jnp.int32, (8, channels), 0)
+        pair = jnp.where(pair_row == 0, pair[0], jnp.where(pair_row == 1, pair[1], 0.0)).T
+        tile = x_ref[block, :channels].astype(jnp.float32)
+        tile = jnp.where(tile_lane == 0, pair[:, :1], jnp.where(tile_lane == 1, pair[:, 1:2], tile))
+        signals_f32[block * channels : (block + 1) * channels] = tile
         turned_filters[blocks - 1 - block] = jnp.dot(
             h_ref[:, block * width : (block + 1) * width].astype(jnp.bfloat16),
             exchange,
@@ -200,25 +190,20 @@
         return carry
 
     lax.fori_loop(0, channels // GROUP, one_group, 0)
-    inner = len(outs)
-    for offset, out in enumerate(outs):
-        for outer in range(blocks // inner):
-            block = outer * inner + jnp.bitwise_xor(place_ref[0], offset)
-            out[outer] = result[pl.ds(block, channels, stride=blocks), :].astype(out.dtype)
-
-
-def convolve(place, product, filters, inner):
-    blocks, channels, width = product.shape
+
+
+def convolve(taps, product, filters):
+    blocks, _, width = product.shape
+    channels = filters.shape[0]
     return pl.pallas_call(
         conv_kernel,
-        out_shape=[jax.ShapeDtypeStruct((blocks // inner, channels, width), jnp.bfloat16)] * inner,
-        in_specs=[SMEM, VMEM, VMEM],
-        out_specs=[VMEM] * inner,
+        out_shape=jax.ShapeDtypeStruct((channels * blocks, width), jnp.float32),
+        in_specs=[VMEM] * 3,
+        out_specs=VMEM,
         scratch_shapes=[
             pltpu.VMEM((blocks * channels, width), jnp.float32),
             pltpu.VMEM((blocks, channels, width), jnp.float32),
             pltpu.VMEM((GROUP, width // BAND, 2 * blocks + 8, width), jnp.float32),
-            pltpu.VMEM((channels * blocks, width), jnp.float32),
         ],
         compiler_params=pltpu.CompilerParams(vmem_limit_bytes=VMEM_LIMIT),
         cost_estimate=pl.CostEstimate(
@@ -226,31 +211,39 @@
             bytes_accessed=10 * channels * blocks * width,
             transcendentals=0,
         ),
-    )(place, product, filters)
-
-
-def gate_kernel(place_ref, *refs):
-    inner = (len(refs) - 1) // 2
-    landed, queries, out_ref = refs[:inner], refs[inner:-1], refs[-1]
-    share = 2 * (place_ref[1] % 2) + place_ref[2]
-    for source, query in enumerate(queries):
-        plane = jnp.bitwise_xor(share, source)
-        for offset, mixed in enumerate(landed):
-            gated = mixed[plane].astype(jnp.float32).T * query[
-                jnp.bitwise_xor(place_ref[0], offset)
-            ].astype(jnp.float32)
-            out_ref[offset, plane] = gated.astype(out_ref.dtype)
-
-
-def gate(place, landed, queries):
-    planes, channels, width = landed[0].shape
+    )(taps, product, filters)
+
+
+def gate_kernel(place_ref, taps_ref, q_ref, y_ref, *outs):
+    blocks, channels, width = q_ref.shape
+    lane = lax.broadcasted_iota(jnp.int32, (channels, width), 1)
+    columns = taps_ref[...].T
+    taps = [jnp.broadcast_to(columns[:, place : place + 1], lane.shape) for place in range(3)]
+    inner = len(outs)
+    for offset, out in enumerate(outs):
+        for outer in range(blocks // inner):
+            block = outer * inner + jnp.bitwise_xor(place_ref[0], offset)
+            query = q_ref[block].astype(jnp.float32)
+            earlier = q_ref[jnp.maximum(block - 1, 0)].astype(jnp.float32)
+            earlier = jnp.where(block > 0, earlier, 0.0)
+            once, twice = (
+                jnp.where(lane >= steps, pltpu.roll(query, steps, 1), pltpu.roll(earlier, steps, 1))
+                for steps in (1, 2)
+            )
+            query_short = taps[0] * query + taps[1] * once + taps[2] * twice
+            gated = query_short * y_ref[pl.ds(block, channels, stride=blocks), :]
+            out[outer] = gated.T.astype(out.dtype)
+
+
+def gate(place, taps, query, mixed, inner):
+    blocks, channels, width = query.shape
     return pl.pallas_call(
         gate_kernel,
-        out_shape=jax.ShapeDtypeStruct((len(landed), planes, width, channels), jnp.bfloat16),
-        in_specs=[SMEM] + [VMEM] * (len(landed) + len(queries)),
-        out_specs=VMEM,
+        out_shape=[jax.ShapeDtypeStruct((blocks // inner, width, channels), jnp.bfloat16)] * inner,
+        in_specs=[SMEM] + [VMEM] * 3,
+        out_specs=[VMEM] * inner,
         compiler_params=pltpu.CompilerParams(vmem_limit_bytes=VMEM_LIMIT),
-    )(place, *landed, *queries)
+    )(place, taps, query, mixed)
 
 
 def project_kernel(place_ref, own_ref, other_ref, *refs):
@@ -283,11 +276,14 @@
 STEPS = (2, 1, 3, 0)
 
 
-def project(place, gates, weights, first, columns):
+def project(place, gates, weights, columns):
     _, _, rows, _ = gates[0].shape
     specs = [
-        pl.BlockSpec((weight.shape[0], columns), lambda step, place_ref: (0, first // columns))
-        for weight in weights
+        pl.BlockSpec(
+            (weight.shape[0], columns),
+            functools.partial(lambda block, step, place_ref: (0, block), first // columns),
+        )
+        for weight, first in weights
     ]
     whole = pl.BlockSpec(gates[0].shape, lambda step, place_ref: (0,) * 4)
     kinds = [jnp.bfloat16] * 3 + [jnp.float32]
@@ -302,7 +298,7 @@
         ),
         compiler_params=pltpu.CompilerParams(vmem_limit_bytes=VMEM_LIMIT),
         cost_estimate=pl.CostEstimate(flops=rows * columns, bytes_accessed=0, transcendentals=0),
-    )(place, *gates, *weights)
+    )(place, *gates, *[weight for weight, _ in weights])
 
 
 def by_planes(query_proj, key_proj, value_proj, short_taps, long_filters, out_weight):
@@ -317,25 +313,24 @@
     up = [(source, (source + PLANE) % seq_count) for source in range(seq_count)]
     down = [(target, source) for source, target in up]
 
-    def to_plane_of_rows(message, target_of):
+    def to_plane_of_rows(message, offset):
         pairs = []
         for source in range(seq_count):
             z, q = divmod(source, PLANE)
             for tp in range(tp_count):
-                share, target_q = target_of(z, q)
-                target = (planes // tp_count * tp + share // tp_count) * PLANE + target_q
-                pairs.append((source * tp_count + tp, target * tp_count + share % tp_count))
+                target = (planes // tp_count * tp + z // tp_count) * PLANE + (q ^ offset)
+                pairs.append((source * tp_count + tp, target * tp_count + z % tp_count))
         return lax.ppermute(message, ("seq", "tp"), pairs)
 
     def from_neighbours(first, count):
         part = out_weight[:, first : first + count]
         return [part, lax.ppermute(part, "seq", across), lax.ppermute(part, "seq", along)]
 
-    def from_corner(part, from_x, from_y):
+    def from_corner(part, from_x, from_y, first, count):
         half = part.shape[0] // 2
-        top = lax.ppermute(from_y[:half], "seq", across)
-        end = lax.ppermute(from_x[half:], "seq", along)
-        return [part, from_x, from_y, top, end]
+        top = lax.ppermute(from_y[:half, first : first + count], "seq", across)
+        end = lax.ppermute(from_x[half:, first : first + count], "seq", along)
+        return [(part, first), (from_x, first), (from_y, first), (top, 0), (end, 0)]
 
     spans, first = [], 0
     for share in COLUMN_SHARES:
@@ -346,44 +341,42 @@
     groups = [list(range(first, first + PLANE)) for first in range(0, seq_count, PLANE)]
     early = out_weight[:, : spans[0][1]]
     early = lax.all_gather(early, "seq", axis=0, tiled=True, axis_index_groups=groups)
-    rows = [[early]]
+    half = spans[0][1] // 2
+    halves = [([(early, 0)], half), ([(early, half)], half)]
     taps = jnp.pad(
         short_taps.reshape(-1, short_taps.shape[2]),
-        ((0, TAIL_ROWS - short_taps.shape[0] * short_taps.shape[1]), (0, 0)),
-    )
-    before = shifted(last_rows(query_proj, key_proj, value_proj), "seq", 1)
-    product = gated_product(taps, before, key_proj, value_proj)
-    product, before = lax.optimization_barrier((product, before))
-    spread = lax.all_to_all(
-        product.reshape(seq_count, channels, width), "seq", split_axis=0, concat_axis=0, tiled=True
-    )
-    queries = [
-        to_plane_of_rows(message, lambda z, q: (z ^ offset, q))
-        for offset, message in enumerate(query_shares(place, taps, before, query_proj, planes))
-    ]
-    mixed = convolve(place, spread, long_filters, PLANE)
-    mixed, queries = lax.optimization_barrier((mixed, queries))
+        ((0, EDGE_ROWS - short_taps.shape[0] * short_taps.shape[1]), (0, 0)),
+    )
+    product = gated_product(taps, key_proj, value_proj)
+    spread = lax.all_to_all(product, "seq", split_axis=0, concat_axis=0, tiled=True)
+    taps_here = lax.dynamic_slice_in_dim(taps, place_seq * channels, channels, axis=1)
+    spread, query_proj = lax.optimization_barrier((spread, query_proj))
+    query = lax.all_to_all(
+        query_proj.reshape(seq_count, channels, width), "seq", split_axis=0, concat_axis=0, tiled=True
+    )
+    mixed = convolve(taps_here, spread, long_filters)
     landed = [
-        to_plane_of_rows(message, lambda z, q: (z, q ^ offset))
-        for offset, message in enumerate(mixed)
+        to_plane_of_rows(message, offset)
+        for offset, message in enumerate(gate(place, taps_here, query, mixed, PLANE))
     ]
     landed[0], out_weight = lax.optimization_barrier((landed[0], out_weight))
-    rows.append(from_neighbours(*spans[1]))
-    own = gate(place, landed, queries)
+    late = from_neighbours(*spans[1])
+    own = jnp.stack(landed)
     gates = [own, lax.ppermute(own, "tp", [(0, 1), (1, 0)])]
 
     parts, sums, sent = [], [], []
-    for index in range(2 * len(spans)):
+    for index in range(4):
         if index == 2:
             sent += [lax.ppermute(sums[0], "seq", up), lax.ppermute(sums[1], "seq", down)]
-            rows[1], sums = lax.optimization_barrier((rows[1], sums))
-            rows[1] = from_corner(*rows[1])
+            late, sums = lax.optimization_barrier((late, sums))
+            half = spans[1][1] // 2
+            halves += [(from_corner(*late, first, half), half) for first in (0, half)]
             gates, parts, sums = lax.optimization_barrier((gates, parts, sums))
         elif index == 3:
             gates, sent = lax.optimization_barrier((gates, sent))
-        weights, count = rows[index // 2], spans[index // 2][1] // 2
+        weights, count = halves[index]
         forth, back = (up, down) if index % 2 == 0 else (down, up)
-        far, ahead, behind, mine = project(place, gates, weights, count * (index % 2), count)
+        far, ahead, behind, mine = project(place, gates, weights, count)
         if index % 2 == 1:
             ahead, behind = behind, ahead
         far = lax.ppermute(far, "seq", forth)

time: 169 us -> 166 us (0.982)
  starting transfers between devices: 57.2 us -> 48.4 us
  waiting for transfers between devices: 60.7 us -> 68.7 us
  Pallas kernels: 29.4 us -> 27.6 us
    ppermute x4, waiting for transfers between devices: 15 us -> 0.01 us  [by_planes(): near = lax.ppermute(behind, 'seq', back)]
    all_to_all x1 -> x2, waiting for transfers between devices: 4.88 us -> 17.3 us  [the longest x1 16.3 us: by_planes(): lax.all_to_all(product, 'seq', split_axis=0, concat_axis=0, tiled=True)]
    ppermute x1, waiting for transfers between devices: 1.82 us -> 10.9 us  [by_planes(): lax.ppermute(sums[-2], 'seq', up)]
    ppermute x8 -> x4, starting transfers between devices: 12.2 us -> 4.21 us  [to_plane_of_rows(): return lax.ppermute(message, ('seq', 'tp'), pairs)]
    ppermute x3 -> x4, waiting for transfers between devices: 1.81 us -> 7.07 us  [the longest x2 7.07 us: from_corner(): top = lax.ppermute(from_y[:half, first:first + count], 'seq', across)]
    ppermute x1, waiting for transfers between devices: 5.22 us -> 0.01 us  [by_planes(): lax.ppermute(sums[0], 'seq', up)]
    all_to_all x1 -> x2, starting transfers between devices: 7.73 us -> 12.7 us  [the longest x1 8.32 us: by_planes(): lax.all_to_all(product, 'seq', split_axis=0, concat_axis=0, tiled=True)]
    ppermute x4, starting transfers between devices: 9.72 us -> 5.04 us  [by_planes(): far = lax.ppermute(far, 'seq', forth)]
  transfers between devices with their start and end apart: 28 -> 26, of which waited for: 13 -> 14; matrix products, arithmetic and copies ran while one was open for 1% -> 1% of each run, Pallas kernels for 17% -> 17%
where the time goes in v5:
time: 166 us
  waiting for transfers between devices  68.7 us (41%)
  starting transfers between devices  48.4 us (29%)
  Pallas kernels  27.6 us (17%)
  between operations  13.6 us (8%)
  local copies, waits for them, and re-layouts  5.61 us (3%)
  other arithmetic  1.83 us (1%)
    all_to_all x1, waiting for transfers between devices, by_planes(): lax.all_to_all(product, 'seq', split_axis=0, concat_axis=0, tiled=True)  16.3 us
    ppermute x4, waiting for transfers between devices, by_planes(): far = lax.ppermute(far, 'seq', forth)  14.6 us
    pallas_call x1, Pallas kernels, convolve(): pl.pallas_call(conv_kernel, out_shape=jax.ShapeDtypeStruct((channels * bl...  13.1 us
    ppermute x4, waiting for transfers between devices, to_plane_of_rows(): return lax.ppermute(message, ('seq', 'tp'), pairs)  12.1 us
    ppermute x1, waiting for transfers between devices, by_planes(): lax.ppermute(sums[-2], 'seq', up)  10.9 us
    pallas_call x4, Pallas kernels, project(): pl.pallas_call(project_kernel, out_shape=[jax.ShapeDtypeStruct((rows, col...  10.3 us
    ppermute x4, starting transfers between devices, by_planes(): near = lax.ppermute(behind, 'seq', back)  10.2 us
    all_to_all x1, starting transfers between devices, by_planes(): lax.all_to_all(product, 'seq', split_axis=0, concat_axis=0, tiled=True)  8.32 us
  transfers between devices with their start and end apart: 26, of which 14 were waited for; matrix products, arithmetic and copies ran while one was open for 1% of the time, Pallas kernels for 17%

profile of v5, /device:TPU:0, one launch (start us, length us, event | category | flops | bytes accessed | tf_op | source)
XLA Modules:
  0.0 165.8 jit_solution(5350648366450210480)
XLA Ops:
  6.5 2.3 %slice.18 = bf16[256,1792]{1,0:T(8,128)(2,1)} slice(bf16[256,4096]{1,0:T(8,128)(2,1)} %param.11), slice={[0:256], [0:1792]} | slice | bytes 1835008 | tf_op jit(solution)/shard_map/slice | solution.py:342
  8.9 2.5 %shard_map.64 = bf16[16,144,128]{2,1,0:T(8,128)(2,1)} custom-call(f32[16,2048]{1,0:T(8,128)S(1)} %pad.4.taps_ref, bf16[2048,128]{1,0:T(8,128)(2,1)S(1)} %copy-done.1, bf16[2048,128]{1,0:T(8,128)(2,1)S(1)} %copy-done.2), custom_call_target="tpu_custom_call" | custom-call | tf_op jit(solution)/shard_map/pallas_call | solution.py:92
  11.4 8.3 %all-to-all-start = ((bf16[16,144,128]{2,1,0:T(8,128)(2,1)}), bf16[16,144,128]{2,1,0:T(8,128)(2,1)S(1)}, u32[]{:S(2)}, u32[]{:S(2)}) async-start(bf16[16,144,128]{2,1,0:T(8,128)(2,1)} %shard_map.64), calls=%async_computation | async-start | bytes 1179648 | tf_op jit(solution)/shard_map/all_to_all | solution.py:351
  19.7 16.3 %all-to-all-done.x_ref = bf16[16,144,128]{2,1,0:T(8,128)(2,1)S(1)} async-done(((bf16[16,144,128]{2,1,0:T(8,128)(2,1)}), bf16[16,144,128]{2,1,0:T(8,128)(2,1)S(1)}, u32[]{:S(2)}, u32[]{:S(2)}) %all-to-all-start) | async-done | bytes 589856 | tf_op jit(solution)/shard_map/all_to_all | solution.py:351
  36.0 4.4 %all-to-all-start.1 = ((bf16[16,128,128]{2,1,0:T(8,128)(2,1)}), bf16[16,128,128]{2,1,0:T(8,128)(2,1)S(1)}, u32[]{:S(2)}, u32[]{:S(2)}) async-start(bf16[16,128,128]{2,1,0:T(8,128)(2,1)} %bitcast.3), calls=%async_computation.1 | async-start | bytes 1048576 | tf_op jit(solution)/shard_map/all_to_all | solution.py:354
  40.5 13.1 %shard_map.65.y_ref = f32[2048,128]{1,0:T(8,128)S(1)} custom-call(f32[16,128]{1,0:T(8,128)S(1)} %constant_dynamic-slice_fusion.taps_ref, bf16[16,144,128]{2,1,0:T(8,128)(2,1)S(1)} %all-to-all-done.x_ref, f32[128,2048]{1,0:T(8,128)S(1)} %copy-done.3), custom_call_target="tpu_custom_call" | custom-call | flops 8589934592 | bytes 2621440 | tf_op jit(solution)/shard_map/pallas_call | solution.py:198
  53.6 1.1 all-to-all-done.1.q_ref
  54.6 1.8 %shard_map.66 = (bf16[4,128,128]{2,1,0:T(8,128)(2,1)S(1)}, bf16[4,128,128]{2,1,0:T(8,128)(2,1)S(1)}, bf16[4,128,128]{2,1,0:T(8,128)(2,1)S(1)}, bf16[4,128,128]{2,1,0:T(8,128)(2,1)S(1)}) custom-call(s32[3]{0:T(128)S(1)} %pad_add_fusion.place_ref, f32[16,128]{1,0:T(8,128)S(1)} %constant_dynamic-slice_fusion.taps_ref, ...), custom_call_target="tpu_custom_call" | custom-call | tf_op jit(solution)/shard_map/pallas_call | solution.py:240
  56.4 0.7 collective-permute-start
  57.1 0.9 collective-permute-start.1
  58.0 1.5 collective-permute-start.2
  59.5 1.2 collective-permute-start.3
  60.7 5.7 %collective-permute-done.1 = bf16[4,128,128]{2,1,0:T(8,128)(2,1)S(1)} collective-permute-done((bf16[4,128,128]{2,1,0:T(8,128)(2,1)S(1)}, bf16[4,128,128]{2,1,0:T(8,128)(2,1)S(1)}, u32[]{:S(2)}, u32[]{:S(2)}) %collective-permute-start.1) | collective-permute-done | bytes 131104 | tf_op jit(solution)/shard_map/ppermute | solution.py:323
  66.3 6.4 %collective-permute-done.3 = bf16[4,128,128]{2,1,0:T(8,128)(2,1)S(1)} collective-permute-done((bf16[4,128,128]{2,1,0:T(8,128)(2,1)S(1)}, bf16[4,128,128]{2,1,0:T(8,128)(2,1)S(1)}, u32[]{:S(2)}, u32[]{:S(2)}) %collective-permute-start.3) | collective-permute-done | bytes 131104 | tf_op jit(solution)/shard_map/ppermute | solution.py:323
  72.9 0.1 slice.19.refs_0_
  73.0 1.0 collective-permute-start.11
  74.0 0.6 collective-permute-start.12
  74.6 0.2 collective-permute-done.4.other_ref
  74.8 0.3 all-gather.2.cloned.1.call-done.refs_0_
  75.1 2.0 %copy-done = bf16[1024,1792]{1,0:T(8,128)(2,1)S(1)} copy-done((bf16[1024,1792]{1,0:T(8,128)(2,1)S(1)}, bf16[1024,1792]{1,0:T(8,128)(2,1)}, u32[]{:S(2)}) %copy-start) | copy-done | bytes 3670040
  77.2 1.9 %shard_map.68 = (bf16[128,896]{1,0:T(8,128)(2,1)S(1)}, bf16[128,896]{1,0:T(8,128)(2,1)S(1)}, bf16[128,896]{1,0:T(8,128)(2,1)S(1)}, f32[128,896]{1,0:T(8,128)S(1)}) custom-call(s32[3]{0:T(128)S(1)} %pad_add_fusion.place_ref, bf16[4,4,128,128]{3,2,1,0:T(8,128)(2,1)S(1)} %pad_maximum_fusion.1.own_ref, ...), custom_call_target="tpu_custom_call" | custom-call | flops 114688 | tf_op jit(solution)/shard_map/pallas_call | solution.py:290
  79.1 4.1 %collective-permute-start.9 = (bf16[128,896]{1,0:T(8,128)(2,1)S(1)}, bf16[128,896]{1,0:T(8,128)(2,1)S(1)}, u32[]{:S(2)}, u32[]{:S(2)}) collective-permute-start(bf16[128,896]{1,0:T(8,128)(2,1)S(1)} %get-tuple-element.57), channel_id=1, source_target_pairs={{8,0},{10,2},{12,4},{14,6},{16,8},{18,10},{20,12},{22,14},{24,16},... | collective-permute-start | bytes 688136 | tf_op jit(solution)/shard_map/ppermute | solution.py:382
  83.2 1.9 %shard_map.67 = (bf16[128,896]{1,0:T(8,128)(2,1)S(1)}, bf16[128,896]{1,0:T(8,128)(2,1)S(1)}, bf16[128,896]{1,0:T(8,128)(2,1)S(1)}, f32[128,896]{1,0:T(8,128)S(1)}) custom-call(s32[3]{0:T(128)S(1)} %pad_add_fusion.place_ref, bf16[4,4,128,128]{3,2,1,0:T(8,128)(2,1)S(1)} %pad_maximum_fusion.1.own_ref, ...), custom_call_target="tpu_custom_call" | custom-call | flops 114688 | tf_op jit(solution)/shard_map/pallas_call | solution.py:290
  85.1 0.8 collective-permute-start.6
  85.9 3.3 %collective-permute-done.9 = bf16[128,896]{1,0:T(8,128)(2,1)S(1)} collective-permute-done((bf16[128,896]{1,0:T(8,128)(2,1)S(1)}, bf16[128,896]{1,0:T(8,128)(2,1)S(1)}, u32[]{:S(2)}, u32[]{:S(2)}) %collective-permute-start.9) | collective-permute-done | bytes 229408 | tf_op jit(solution)/shard_map/ppermute | solution.py:382
  89.2 4.3 %collective-permute-start.5 = (bf16[128,896]{1,0:T(8,128)(2,1)S(1)}, bf16[128,896]{1,0:T(8,128)(2,1)S(1)}, u32[]{:S(2)}, u32[]{:S(2)}) collective-permute-start(bf16[128,896]{1,0:T(8,128)(2,1)S(1)} %get-tuple-element.48), channel_id=1, source_target_pairs={{8,0},{10,2},{12,4},{14,6},{16,8},{18,10},{20,12},{22,14},{24,16},... | collective-permute-start | bytes 688136 | tf_op jit(solution)/shard_map/ppermute | solution.py:383
  93.6 2.0 %collective-permute-done.7 = bf16[128,896]{1,0:T(8,128)(2,1)S(1)} collective-permute-done((bf16[128,896]{1,0:T(8,128)(2,1)S(1)}, bf16[128,896]{1,0:T(8,128)(2,1)S(1)}, u32[]{:S(2)}, u32[]{:S(2)}) %collective-permute-start.7) | collective-permute-done | bytes 229408 | tf_op jit(solution)/shard_map/ppermute | solution.py:382
  95.6 1.6 collective-permute-start.10
  97.2 4.2 %collective-permute-done.11.refs_1_ = bf16[256,2304]{1,0:T(8,128)(2,1)S(1)} collective-permute-done((bf16[256,2304]{1,0:T(8,128)(2,1)S(1)}, bf16[256,2304]{1,0:T(8,128)(2,1)S(1)}, u32[]{:S(2)}, u32[]{:S(2)}) %collective-permute-start.11) | collective-permute-done | bytes 1179680 | tf_op jit(solution)/shard_map/ppermute | solution.py:327
  101.4 3.2 %collective-permute-start.8 = (bf16[128,896]{1,0:T(8,128)(2,1)S(1)}, bf16[128,896]{1,0:T(8,128)(2,1)S(1)}, u32[]{:S(2)}, u32[]{:S(2)}) collective-permute-start(bf16[128,896]{1,0:T(8,128)(2,1)S(1)} %add_convert_fusion.7), channel_id=1, source_target_pairs={{0,8},{2,10},{4,12},{6,14},{8,16},{10,18},{12,20},{14,22},{16,24},... | collective-permute-start | bytes 688136 | tf_op jit(solution)/shard_map/ppermute | solution.py:370
  104.6 1.1 fusion.1
  105.7 0.7 collective-permute-start.13
  106.5 0.9 collective-permute-start.14
  107.5 1.2 collective-permute-start.18
  108.7 7.1 %collective-permute-done.13.refs_3_ = bf16[128,1152]{1,0:T(8,128)(2,1)S(1)} collective-permute-done((bf16[128,1152]{1,0:T(8,128)(2,1)S(1)}, bf16[128,1152]{1,0:T(8,128)(2,1)S(1)}, u32[]{:S(2)}, u32[]{:S(2)}) %collective-permute-start.13) | collective-permute-done | bytes 294944 | tf_op jit(solution)/shard_map/ppermute | solution.py:331
  115.7 0.6 collective-permute-start.19
  116.3 3.2 %shard_map.69 = (bf16[128,1152]{1,0:T(8,128)(2,1)S(1)}, bf16[128,1152]{1,0:T(8,128)(2,1)S(1)}, bf16[128,1152]{1,0:T(8,128)(2,1)S(1)}, f32[128,1152]{1,0:T(8,128)S(1)}) custom-call(s32[3]{0:T(128)S(1)} %pad_add_fusion.place_ref, bf16[4,4,128,128]{3,2,1,0:T(8,128)(2,1)S(1)} %pad_maximum_fusion.1.own_ref, ...), custom_call_target="tpu_custom_call" | custom-call | flops 147456 | tf_op jit(solution)/shard_map/pallas_call | solution.py:290
  119.6 0.8 collective-permute-start.16
  120.5 3.1 %collective-permute-start.15 = (bf16[128,1152]{1,0:T(8,128)(2,1)S(1)}, bf16[128,1152]{1,0:T(8,128)(2,1)S(1)}, u32[]{:S(2)}, u32[]{:S(2)}) collective-permute-start(bf16[128,1152]{1,0:T(8,128)(2,1)S(1)} %get-tuple-element.66), channel_id=1, source_target_pairs={{8,0},{10,2},{12,4},{14,6},{16,8},{18,10},{20,12},{22,14},{24,16},... | collective-permute-start | bytes 884744 | tf_op jit(solution)/shard_map/ppermute | solution.py:383
  123.6 3.2 %shard_map.70 = (bf16[128,1152]{1,0:T(8,128)(2,1)S(1)}, bf16[128,1152]{1,0:T(8,128)(2,1)S(1)}, bf16[128,1152]{1,0:T(8,128)(2,1)S(1)}, f32[128,1152]{1,0:T(8,128)S(1)}) custom-call(s32[3]{0:T(128)S(1)} %pad_add_fusion.place_ref, bf16[4,4,128,128]{3,2,1,0:T(8,128)(2,1)S(1)} %pad_maximum_fusion.1.own_ref, ...), custom_call_target="tpu_custom_call" | custom-call | flops 147456 | tf_op jit(solution)/shard_map/pallas_call | solution.py:290
  126.9 2.0 %collective-permute-start.20 = (bf16[128,1152]{1,0:T(8,128)(2,1)S(1)}, bf16[128,1152]{1,0:T(8,128)(2,1)S(1)}, u32[]{:S(2)}, u32[]{:S(2)}) collective-permute-start(bf16[128,1152]{1,0:T(8,128)(2,1)S(1)} %get-tuple-element.72), channel_id=1, source_target_pairs={{0,8},{2,10},{4,12},{6,14},{8,16},{10,18},{12,20},{14,22},{16,24},... | collective-permute-start | bytes 884744 | tf_op jit(solution)/shard_map/ppermute | solution.py:383
  128.9 2.4 %collective-permute-done.16 = bf16[128,1152]{1,0:T(8,128)(2,1)S(1)} collective-permute-done((bf16[128,1152]{1,0:T(8,128)(2,1)S(1)}, bf16[128,1152]{1,0:T(8,128)(2,1)S(1)}, u32[]{:S(2)}, u32[]{:S(2)}) %collective-permute-start.16) | collective-permute-done | bytes 294944 | tf_op jit(solution)/shard_map/ppermute | solution.py:382
  131.4 3.4 %collective-permute-start.17 = (bf16[128,1152]{1,0:T(8,128)(2,1)S(1)}, bf16[128,1152]{1,0:T(8,128)(2,1)S(1)}, u32[]{:S(2)}, u32[]{:S(2)}) collective-permute-start(bf16[128,1152]{1,0:T(8,128)(2,1)S(1)} %add_convert_fusion.3), channel_id=1, source_target_pairs={{0,8},{2,10},{4,12},{6,14},{8,16},{10,18},{12,20},{14,22},{16,24},... | collective-permute-start | bytes 884744 | tf_op jit(solution)/shard_map/ppermute | solution.py:386
  134.8 6.9 %collective-permute-done.21 = bf16[128,1152]{1,0:T(8,128)(2,1)S(1)} collective-permute-done((bf16[128,1152]{1,0:T(8,128)(2,1)S(1)}, bf16[128,1152]{1,0:T(8,128)(2,1)S(1)}, u32[]{:S(2)}, u32[]{:S(2)}) %collective-permute-start.21) | collective-permute-done | bytes 294944 | tf_op jit(solution)/shard_map/ppermute | solution.py:382
  141.8 3.1 %collective-permute-start.22 = (bf16[128,1152]{1,0:T(8,128)(2,1)S(1)}, bf16[128,1152]{1,0:T(8,128)(2,1)S(1)}, u32[]{:S(2)}, u32[]{:S(2)}) collective-permute-start(bf16[128,1152]{1,0:T(8,128)(2,1)S(1)} %add_convert_fusion.1), channel_id=1, source_target_pairs={{8,0},{10,2},{12,4},{14,6},{16,8},{18,10},{20,12},{22,14},{24,16},... | collective-permute-start | bytes 884744 | tf_op jit(solution)/shard_map/ppermute | solution.py:386
  144.9 10.9 %collective-permute-done.17 = bf16[128,1152]{1,0:T(8,128)(2,1)S(1)} collective-permute-done((bf16[128,1152]{1,0:T(8,128)(2,1)S(1)}, bf16[128,1152]{1,0:T(8,128)(2,1)S(1)}, u32[]{:S(2)}, u32[]{:S(2)}) %collective-permute-start.17) | collective-permute-done | bytes 294944 | tf_op jit(solution)/shard_map/ppermute | solution.py:386
  155.9 1.9 %collective-permute-done.22 = bf16[128,1152]{1,0:T(8,128)(2,1)S(1)} collective-permute-done((bf16[128,1152]{1,0:T(8,128)(2,1)S(1)}, bf16[128,1152]{1,0:T(8,128)(2,1)S(1)}, u32[]{:S(2)}, u32[]{:S(2)}) %collective-permute-start.22) | collective-permute-done | bytes 294944 | tf_op jit(solution)/shard_map/ppermute | solution.py:386
  157.9 1.1 pad_maximum_fusion
  (43 shorter events, 1.1 us)
Async XLA Ops:
  6.5 2.3 %copy-start.5 = (f32[3,3,2048]{2,1,0:T(4,128)S(1)}, f32[3,3,2048]{2,1,0:T(4,128)}, u32[]{:S(2)}) copy-start(f32[3,3,2048]{2,1,0:T(4,128)} %param.9) | copy-start | bytes 221188
  6.5 2.4 %copy-start.1 = (bf16[2048,128]{1,0:T(8,128)(2,1)S(1)}, bf16[2048,128]{1,0:T(8,128)(2,1)}, u32[]{:S(2)}) copy-start(bf16[2048,128]{1,0:T(8,128)(2,1)} %key_ref.1) | copy-start | bytes 1572868
  6.5 2.4 %copy-start.2 = (bf16[2048,128]{1,0:T(8,128)(2,1)S(1)}, bf16[2048,128]{1,0:T(8,128)(2,1)}, u32[]{:S(2)}) copy-start(bf16[2048,128]{1,0:T(8,128)(2,1)} %value_ref.1) | copy-start | bytes 1572868
  6.5 68.6 %all-gather.2.cloned.1.call-start = ((), (), s32[]{:S(2)}) async-start(), calls=%async_computation.2 | async-start | bytes 4587520 | tf_op jit(solution)/shard_map/all_gather | solution.py:343
  8.9 31.5 %copy-start.3 = (f32[128,2048]{1,0:T(8,128)S(1)}, f32[128,2048]{1,0:T(8,128)}, u32[]{:S(2)}) copy-start(f32[128,2048]{1,0:T(8,128)} %h_ref.1) | copy-start | bytes 3145732
  11.4 24.6 %all-to-all-start = ((bf16[16,144,128]{2,1,0:T(8,128)(2,1)}), bf16[16,144,128]{2,1,0:T(8,128)(2,1)S(1)}, u32[]{:S(2)}, u32[]{:S(2)}) async-start(bf16[16,144,128]{2,1,0:T(8,128)(2,1)} %shard_map.64), calls=%async_computation | async-start | bytes 1179648 | tf_op jit(solution)/shard_map/all_to_all | solution.py:351
  36.0 18.6 %all-to-all-start.1 = ((bf16[16,128,128]{2,1,0:T(8,128)(2,1)}), bf16[16,128,128]{2,1,0:T(8,128)(2,1)S(1)}, u32[]{:S(2)}, u32[]{:S(2)}) async-start(bf16[16,128,128]{2,1,0:T(8,128)(2,1)} %bitcast.3), calls=%async_computation.1 | async-start | bytes 1048576 | tf_op jit(solution)/shard_map/all_to_all | solution.py:354
  54.6 18.3 %copy-start.4 = (bf16[256,4096]{1,0:T(8,128)(2,1)S(1)}, bf16[256,4096]{1,0:T(8,128)(2,1)}, u32[]{:S(2)}) copy-start(bf16[256,4096]{1,0:T(8,128)(2,1)} %param.11) | copy-start | bytes 6291460
  56.4 4.2 %collective-permute-start = (bf16[4,128,128]{2,1,0:T(8,128)(2,1)S(1)}, bf16[4,128,128]{2,1,0:T(8,128)(2,1)S(1)}, u32[]{:S(2)}, u32[]{:S(2)}) collective-permute-start(bf16[4,128,128]{2,1,0:T(8,128)(2,1)S(1)} %get-tuple-element.42), channel_id=1, source_target_pairs={{0,0},{1,16},{2,2},{3,18},{4,4},{5,20},{6,6},{7,22},{8,1},{9,17},{... | collective-permute-start | bytes 393224 | tf_op jit(solution)/shard_map/ppermute | solution.py:323
  57.1 9.2 %collective-permute-start.1 = (bf16[4,128,128]{2,1,0:T(8,128)(2,1)S(1)}, bf16[4,128,128]{2,1,0:T(8,128)(2,1)S(1)}, u32[]{:S(2)}, u32[]{:S(2)}) collective-permute-start(bf16[4,128,128]{2,1,0:T(8,128)(2,1)S(1)} %get-tuple-element.44), channel_id=1, source_target_pairs={{0,2},{1,18},{2,0},{3,16},{4,6},{5,22},{6,4},{7,20},{8,3},{9,19},{... | collective-permute-start | bytes 393224 | tf_op jit(solution)/shard_map/ppermute | solution.py:323
  58.0 8.3 %collective-permute-start.2 = (bf16[4,128,128]{2,1,0:T(8,128)(2,1)S(1)}, bf16[4,128,128]{2,1,0:T(8,128)(2,1)S(1)}, u32[]{:S(2)}, u32[]{:S(2)}) collective-permute-start(bf16[4,128,128]{2,1,0:T(8,128)(2,1)S(1)} %get-tuple-element.45), channel_id=1, source_target_pairs={{0,4},{1,20},{2,6},{3,22},{4,0},{5,16},{6,2},{7,18},{8,5},{9,21},{... | collective-permute-start | bytes 393224 | tf_op jit(solution)/shard_map/ppermute | solution.py:323
  59.5 13.2 %collective-permute-start.3 = (bf16[4,128,128]{2,1,0:T(8,128)(2,1)S(1)}, bf16[4,128,128]{2,1,0:T(8,128)(2,1)S(1)}, u32[]{:S(2)}, u32[]{:S(2)}) collective-permute-start(bf16[4,128,128]{2,1,0:T(8,128)(2,1)S(1)} %get-tuple-element.46), channel_id=1, source_target_pairs={{0,6},{1,22},{2,4},{3,20},{4,2},{5,18},{6,0},{7,16},{8,7},{9,23},{... | collective-permute-start | bytes 393224 | tf_op jit(solution)/shard_map/ppermute | solution.py:323
  72.8 2.0 %collective-permute-start.4 = (bf16[4,4,128,128]{3,2,1,0:T(8,128)(2,1)S(1)}, bf16[4,4,128,128]{3,2,1,0:T(8,128)(2,1)S(1)}, u32[]{:S(2)}, u32[]{:S(2)}) collective-permute-start(bf16[4,4,128,128]{3,2,1,0:T(8,128)(2,1)S(1)} %pad_maximum_fusion.1.own_ref), channel_id=1, source_target_pairs={{0,1},{1,0},{2,3},{3,2},{4,5},{5,4},{6,7},{7,6},{8,9},{9,8},{10,11... | collective-permute-start | bytes 1572872 | tf_op jit(solution)/shard_map/ppermute | solution.py:365
  73.0 28.4 %collective-permute-start.11 = (bf16[256,2304]{1,0:T(8,128)(2,1)S(1)}, bf16[256,2304]{1,0:T(8,128)(2,1)S(1)}, u32[]{:S(2)}, u32[]{:S(2)}) collective-permute-start(bf16[256,2304]{1,0:T(8,128)(2,1)S(1)} %slice.19.refs_0_), channel_id=1, source_target_pairs={{0,2},{2,0},{4,6},{6,4},{8,10},{10,8},{12,14},{14,12},{16,18},{18,... | collective-permute-start | bytes 3538952 | tf_op jit(solution)/shard_map/ppermute | solution.py:327
  74.0 30.6 %collective-permute-start.12 = (bf16[256,2304]{1,0:T(8,128)(2,1)S(1)}, bf16[256,2304]{1,0:T(8,128)(2,1)}, u32[]{:S(2)}, u32[]{:S(2)}) collective-permute-start(bf16[256,2304]{1,0:T(8,128)(2,1)S(1)} %slice.19.refs_0_), channel_id=1, source_target_pairs={{0,4},{2,6},{4,0},{6,2},{8,12},{10,14},{12,8},{14,10},{16,20},{18,... | collective-permute-start | bytes 3538952 | tf_op jit(solution)/shard_map/ppermute | solution.py:327
  75.1 2.0 %copy-start = (bf16[1024,1792]{1,0:T(8,128)(2,1)S(1)}, bf16[1024,1792]{1,0:T(8,128)(2,1)}, u32[]{:S(2)}) copy-start(bf16[1024,1792]{1,0:T(8,128)(2,1)} %all-gather.2.cloned.1.call-done.refs_0_) | copy-start | bytes 11010052
  79.1 10.2 %collective-permute-start.9 = (bf16[128,896]{1,0:T(8,128)(2,1)S(1)}, bf16[128,896]{1,0:T(8,128)(2,1)S(1)}, u32[]{:S(2)}, u32[]{:S(2)}) collective-permute-start(bf16[128,896]{1,0:T(8,128)(2,1)S(1)} %get-tuple-element.57), channel_id=1, source_target_pairs={{8,0},{10,2},{12,4},{14,6},{16,8},{18,10},{20,12},{22,14},{24,16},... | collective-permute-start | bytes 688136 | tf_op jit(solution)/shard_map/ppermute | solution.py:382
  85.0 10.5 %collective-permute-start.7 = (bf16[128,896]{1,0:T(8,128)(2,1)S(1)}, bf16[128,896]{1,0:T(8,128)(2,1)S(1)}, u32[]{:S(2)}, u32[]{:S(2)}) collective-permute-start(bf16[128,896]{1,0:T(8,128)(2,1)S(1)} %get-tuple-element.55), channel_id=1, source_target_pairs={{0,8},{2,10},{4,12},{6,14},{8,16},{10,18},{12,20},{14,22},{16,24},... | collective-permute-start | bytes 688136 | tf_op jit(solution)/shard_map/ppermute | solution.py:382
  85.1 21.4 %collective-permute-start.6 = (bf16[128,896]{1,0:T(8,128)(2,1)S(1)}, bf16[128,896]{1,0:T(8,128)(2,1)S(1)}, u32[]{:S(2)}, u32[]{:S(2)}) collective-permute-start(bf16[128,896]{1,0:T(8,128)(2,1)S(1)} %get-tuple-element.50), channel_id=1, source_target_pairs={{0,8},{2,10},{4,12},{6,14},{8,16},{10,18},{12,20},{14,22},{16,24},... | collective-permute-start | bytes 688136 | tf_op jit(solution)/shard_map/ppermute | solution.py:383
  89.2 18.2 %collective-permute-start.5 = (bf16[128,896]{1,0:T(8,128)(2,1)S(1)}, bf16[128,896]{1,0:T(8,128)(2,1)S(1)}, u32[]{:S(2)}, u32[]{:S(2)}) collective-permute-start(bf16[128,896]{1,0:T(8,128)(2,1)S(1)} %get-tuple-element.48), channel_id=1, source_target_pairs={{8,0},{10,2},{12,4},{14,6},{16,8},{18,10},{20,12},{22,14},{24,16},... | collective-permute-start | bytes 688136 | tf_op jit(solution)/shard_map/ppermute | solution.py:383
  95.6 24.8 %collective-permute-start.10 = (bf16[128,896]{1,0:T(8,128)(2,1)S(1)}, bf16[128,896]{1,0:T(8,128)(2,1)S(1)}, u32[]{:S(2)}, u32[]{:S(2)}) collective-permute-start(bf16[128,896]{1,0:T(8,128)(2,1)S(1)} %add_convert_fusion.6), channel_id=1, source_target_pairs={{8,0},{10,2},{12,4},{14,6},{16,8},{18,10},{20,12},{22,14},{24,16},... | collective-permute-start | bytes 688136 | tf_op jit(solution)/shard_map/ppermute | solution.py:370
  101.4 18.9 %collective-permute-start.8 = (bf16[128,896]{1,0:T(8,128)(2,1)S(1)}, bf16[128,896]{1,0:T(8,128)(2,1)S(1)}, u32[]{:S(2)}, u32[]{:S(2)}) collective-permute-start(bf16[128,896]{1,0:T(8,128)(2,1)S(1)} %add_convert_fusion.7), channel_id=1, source_target_pairs={{0,8},{2,10},{4,12},{6,14},{8,16},{10,18},{12,20},{14,22},{16,24},... | collective-permute-start | bytes 688136 | tf_op jit(solution)/shard_map/ppermute | solution.py:370
  105.7 10.0 %collective-permute-start.13 = (bf16[128,1152]{1,0:T(8,128)(2,1)S(1)}, bf16[128,1152]{1,0:T(8,128)(2,1)S(1)}, u32[]{:S(2)}, u32[]{:S(2)}) collective-permute-start(bf16[128,1152]{1,0:T(8,128)(2,1)S(1)} %get-tuple-element.77), channel_id=1, source_target_pairs={{0,2},{2,0},{4,6},{6,4},{8,10},{10,8},{12,14},{14,12},{16,18},{18,... | collective-permute-start | bytes 884744 | tf_op jit(solution)/shard_map/ppermute | solution.py:331
  106.5 9.8 %collective-permute-start.14 = (bf16[128,1152]{1,0:T(8,128)(2,1)S(1)}, bf16[128,1152]{1,0:T(8,128)(2,1)S(1)}, u32[]{:S(2)}, u32[]{:S(2)}) collective-permute-start(bf16[128,1152]{1,0:T(8,128)(2,1)S(1)} %get-tuple-element.75), channel_id=1, source_target_pairs={{0,4},{2,6},{4,0},{6,2},{8,12},{10,14},{12,8},{14,10},{16,20},{18,... | collective-permute-start | bytes 884744 | tf_op jit(solution)/shard_map/ppermute | solution.py:332
  107.5 16.1 %collective-permute-start.18 = (bf16[128,1152]{1,0:T(8,128)(2,1)S(1)}, bf16[128,1152]{1,0:T(8,128)(2,1)S(1)}, u32[]{:S(2)}, u32[]{:S(2)}) collective-permute-start(bf16[128,1152]{1,0:T(8,128)(2,1)S(1)} %get-tuple-element.78), channel_id=1, source_target_pairs={{0,2},{2,0},{4,6},{6,4},{8,10},{10,8},{12,14},{14,12},{16,18},{18,... | collective-permute-start | bytes 884744 | tf_op jit(solution)/shard_map/ppermute | solution.py:331
  115.7 7.9 %collective-permute-start.19 = (bf16[128,1152]{1,0:T(8,128)(2,1)S(1)}, bf16[128,1152]{1,0:T(8,128)(2,1)S(1)}, u32[]{:S(2)}, u32[]{:S(2)}) collective-permute-start(bf16[128,1152]{1,0:T(8,128)(2,1)S(1)} %get-tuple-element.76), channel_id=1, source_target_pairs={{0,4},{2,6},{4,0},{6,2},{8,12},{10,14},{12,8},{14,10},{16,20},{18,... | collective-permute-start | bytes 884744 | tf_op jit(solution)/shard_map/ppermute | solution.py:332
  119.6 11.8 %collective-permute-start.16 = (bf16[128,1152]{1,0:T(8,128)(2,1)S(1)}, bf16[128,1152]{1,0:T(8,128)(2,1)S(1)}, u32[]{:S(2)}, u32[]{:S(2)}) collective-permute-start(bf16[128,1152]{1,0:T(8,128)(2,1)S(1)} %get-tuple-element.68), channel_id=1, source_target_pairs={{0,8},{2,10},{4,12},{6,14},{8,16},{10,18},{12,20},{14,22},{16,24},... | collective-permute-start | bytes 884744 | tf_op jit(solution)/shard_map/ppermute | solution.py:382
  120.5 24.4 %collective-permute-start.15 = (bf16[128,1152]{1,0:T(8,128)(2,1)S(1)}, bf16[128,1152]{1,0:T(8,128)(2,1)S(1)}, u32[]{:S(2)}, u32[]{:S(2)}) collective-permute-start(bf16[128,1152]{1,0:T(8,128)(2,1)S(1)} %get-tuple-element.66), channel_id=1, source_target_pairs={{8,0},{10,2},{12,4},{14,6},{16,8},{18,10},{20,12},{22,14},{24,16},... | collective-permute-start | bytes 884744 | tf_op jit(solution)/shard_map/ppermute | solution.py:383
  126.9 14.9 %collective-permute-start.21 = (bf16[128,1152]{1,0:T(8,128)(2,1)S(1)}, bf16[128,1152]{1,0:T(8,128)(2,1)S(1)}, u32[]{:S(2)}, u32[]{:S(2)}) collective-permute-start(bf16[128,1152]{1,0:T(8,128)(2,1)S(1)} %get-tuple-element.74), channel_id=1, source_target_pairs={{8,0},{10,2},{12,4},{14,6},{16,8},{18,10},{20,12},{22,14},{24,16},... | collective-permute-start | bytes 884744 | tf_op jit(solution)/shard_map/ppermute | solution.py:382
  126.9 29.0 %collective-permute-start.20 = (bf16[128,1152]{1,0:T(8,128)(2,1)S(1)}, bf16[128,1152]{1,0:T(8,128)(2,1)S(1)}, u32[]{:S(2)}, u32[]{:S(2)}) collective-permute-start(bf16[128,1152]{1,0:T(8,128)(2,1)S(1)} %get-tuple-element.72), channel_id=1, source_target_pairs={{0,8},{2,10},{4,12},{6,14},{8,16},{10,18},{12,20},{14,22},{16,24},... | collective-permute-start | bytes 884744 | tf_op jit(solution)/shard_map/ppermute | solution.py:383
  131.4 24.4 %collective-permute-start.17 = (bf16[128,1152]{1,0:T(8,128)(2,1)S(1)}, bf16[128,1152]{1,0:T(8,128)(2,1)S(1)}, u32[]{:S(2)}, u32[]{:S(2)}) collective-permute-start(bf16[128,1152]{1,0:T(8,128)(2,1)S(1)} %add_convert_fusion.3), channel_id=1, source_target_pairs={{0,8},{2,10},{4,12},{6,14},{8,16},{10,18},{12,20},{14,22},{16,24},... | collective-permute-start | bytes 884744 | tf_op jit(solution)/shard_map/ppermute | solution.py:386
  141.8 16.0 %collective-permute-start.22 = (bf16[128,1152]{1,0:T(8,128)(2,1)S(1)}, bf16[128,1152]{1,0:T(8,128)(2,1)S(1)}, u32[]{:S(2)}, u32[]{:S(2)}) collective-permute-start(bf16[128,1152]{1,0:T(8,128)(2,1)S(1)} %add_convert_fusion.1), channel_id=1, source_target_pairs={{8,0},{10,2},{12,4},{14,6},{16,8},{18,10},{20,12},{22,14},{24,16},... | collective-permute-start | bytes 884744 | tf_op jit(solution)/shard_map/ppermute | solution.py:386
Sparse Core Ops, SparseCore 0:
  9.2 65.8 all-gather.1

commit v6 on v5

--- a/solution.py
+++ b/solution.py
@@ -113,7 +113,7 @@
     return [(key * value).astype(jnp.bfloat16).astype(jnp.float32) for key, value in zip(*short)]
 
 
-BAND = 32
+BAND = 64
 GROUP = 16
 
 
@@ -368,7 +368,7 @@
     for index in range(4):
         if index == 2:
             sent += [lax.ppermute(sums[0], "seq", up), lax.ppermute(sums[1], "seq", down)]
-            late, sums = lax.optimization_barrier((late, sums))
+            late, sums[0] = lax.optimization_barrier((late, sums[0]))
             half = spans[1][1] // 2
             halves += [(from_corner(*late, first, half), half) for first in (0, half)]
             gates, parts, sums = lax.optimization_barrier((gates, parts, sums))

time: 166 us -> 166 us (level)
  starting transfers between devices: 48.4 us -> 42.7 us
  waiting for transfers between devices: 68.7 us -> 72.9 us
    ppermute x4, starting transfers between devices: 10.2 us -> 3.08 us  [by_planes(): near = lax.ppermute(behind, 'seq', back)]
    ppermute x1, starting transfers between devices: 3.39 us -> 8.84 us  [by_planes(): lax.ppermute(sums[-2], 'seq', up)]
    ppermute x4, waiting for transfers between devices: 14.6 us -> 18.7 us  [by_planes(): far = lax.ppermute(far, 'seq', forth)]
    ppermute x1, waiting for transfers between devices: 10.9 us -> 7.2 us  [by_planes(): lax.ppermute(sums[-2], 'seq', up)]
    ppermute x4, starting transfers between devices: 5.04 us -> 8.63 us  [by_planes(): far = lax.ppermute(far, 'seq', forth)]
    ppermute x1, starting transfers between devices: 3.2 us -> 0.07 us  [by_planes(): lax.ppermute(sums[0], 'seq', up)]
    ppermute x1, starting transfers between devices: 3.1 us -> 0.06 us  [by_planes(): lax.ppermute(sums[-1], 'seq', down)]
    ppermute x1, waiting for transfers between devices: 4.2 us -> 6.78 us  [from_neighbours(): lax.ppermute(part, 'seq', across)]
where the time goes in v6:
time: 166 us
  waiting for transfers between devices  72.9 us (44%)
  starting transfers between devices  42.7 us (26%)
  Pallas kernels  28.8 us (17%)
  between operations  13.6 us (8%)
  local copies, waits for them, and re-layouts  5.61 us (3%)
  other arithmetic  1.83 us (1%)
    ppermute x4, waiting for transfers between devices, by_planes(): far = lax.ppermute(far, 'seq', forth)  18.7 us
    all_to_all x1, waiting for transfers between devices, by_planes(): lax.all_to_all(product, 'seq', split_axis=0, concat_axis=0, tiled=True)  16.3 us
    pallas_call x1, Pallas kernels, convolve(): pl.pallas_call(conv_kernel, out_shape=jax.ShapeDtypeStruct((channels * bl...  14.3 us
    ppermute x4, waiting for transfers between devices, to_plane_of_rows(): return lax.ppermute(message, ('seq', 'tp'), pairs)  13 us
    pallas_call x4, Pallas kernels, project(): pl.pallas_call(project_kernel, out_shape=[jax.ShapeDtypeStruct((rows, col...  10.3 us
    ppermute x1, starting transfers between devices, by_planes(): lax.ppermute(sums[-2], 'seq', up)  8.84 us
    ppermute x4, starting transfers between devices, by_planes(): far = lax.ppermute(far, 'seq', forth)  8.63 us
    all_to_all x1, starting transfers between devices, by_planes(): lax.all_to_all(product, 'seq', split_axis=0, concat_axis=0, tiled=True)  8.32 us
  transfers between devices with their start and end apart: 26, of which 14 were waited for; matrix products, arithmetic and copies ran while one was open for 1% of the time, Pallas kernels for 17%

profile of v6, /device:TPU:0, one launch (start us, length us, event | category | flops | bytes accessed | tf_op | source)
XLA Modules:
  0.0 165.5 jit_solution(1703242350796706679)
XLA Ops:
  6.5 2.3 %slice.18 = bf16[256,1792]{1,0:T(8,128)(2,1)} slice(bf16[256,4096]{1,0:T(8,128)(2,1)} %param.11), slice={[0:256], [0:1792]} | slice | bytes 1835008 | tf_op jit(solution)/shard_map/slice | solution.py:342
  8.9 2.5 %shard_map.64 = bf16[16,144,128]{2,1,0:T(8,128)(2,1)} custom-call(f32[16,2048]{1,0:T(8,128)S(1)} %pad.4.taps_ref, bf16[2048,128]{1,0:T(8,128)(2,1)S(1)} %copy-done.1, bf16[2048,128]{1,0:T(8,128)(2,1)S(1)} %copy-done.2), custom_call_target="tpu_custom_call" | custom-call | tf_op jit(solution)/shard_map/pallas_call | solution.py:92
  11.4 8.3 %all-to-all-start = ((bf16[16,144,128]{2,1,0:T(8,128)(2,1)}), bf16[16,144,128]{2,1,0:T(8,128)(2,1)S(1)}, u32[]{:S(2)}, u32[]{:S(2)}) async-start(bf16[16,144,128]{2,1,0:T(8,128)(2,1)} %shard_map.64), calls=%async_computation | async-start | bytes 1179648 | tf_op jit(solution)/shard_map/all_to_all | solution.py:351
  19.7 16.3 %all-to-all-done.x_ref = bf16[16,144,128]{2,1,0:T(8,128)(2,1)S(1)} async-done(((bf16[16,144,128]{2,1,0:T(8,128)(2,1)}), bf16[16,144,128]{2,1,0:T(8,128)(2,1)S(1)}, u32[]{:S(2)}, u32[]{:S(2)}) %all-to-all-start) | async-done | bytes 589856 | tf_op jit(solution)/shard_map/all_to_all | solution.py:351
  36.0 4.4 %all-to-all-start.1 = ((bf16[16,128,128]{2,1,0:T(8,128)(2,1)}), bf16[16,128,128]{2,1,0:T(8,128)(2,1)S(1)}, u32[]{:S(2)}, u32[]{:S(2)}) async-start(bf16[16,128,128]{2,1,0:T(8,128)(2,1)} %bitcast.3), calls=%async_computation.1 | async-start | bytes 1048576 | tf_op jit(solution)/shard_map/all_to_all | solution.py:354
  40.5 14.3 %shard_map.65.y_ref = f32[2048,128]{1,0:T(8,128)S(1)} custom-call(f32[16,128]{1,0:T(8,128)S(1)} %constant_dynamic-slice_fusion.taps_ref, bf16[16,144,128]{2,1,0:T(8,128)(2,1)S(1)} %all-to-all-done.x_ref, f32[128,2048]{1,0:T(8,128)S(1)} %copy-done.3), custom_call_target="tpu_custom_call" | custom-call | flops 8589934592 | bytes 2621440 | tf_op jit(solution)/shard_map/pallas_call | solution.py:198
  54.7 1.8 %shard_map.66 = (bf16[4,128,128]{2,1,0:T(8,128)(2,1)S(1)}, bf16[4,128,128]{2,1,0:T(8,128)(2,1)S(1)}, bf16[4,128,128]{2,1,0:T(8,128)(2,1)S(1)}, bf16[4,128,128]{2,1,0:T(8,128)(2,1)S(1)}) custom-call(s32[3]{0:T(128)S(1)} %pad_add_fusion.place_ref, f32[16,128]{1,0:T(8,128)S(1)} %constant_dynamic-slice_fusion.taps_ref, ...), custom_call_target="tpu_custom_call" | custom-call | tf_op jit(solution)/shard_map/pallas_call | solution.py:240
  56.6 0.7 collective-permute-start
  57.3 2.0 %collective-permute-start.1 = (bf16[4,128,128]{2,1,0:T(8,128)(2,1)S(1)}, bf16[4,128,128]{2,1,0:T(8,128)(2,1)S(1)}, u32[]{:S(2)}, u32[]{:S(2)}) collective-permute-start(bf16[4,128,128]{2,1,0:T(8,128)(2,1)S(1)} %get-tuple-element.44), channel_id=1, source_target_pairs={{0,2},{1,18},{2,0},{3,16},{4,6},{5,22},{6,4},{7,20},{8,3},{9,19},{... | collective-permute-start | bytes 393224 | tf_op jit(solution)/shard_map/ppermute | solution.py:323
  59.2 1.5 collective-permute-start.2
  60.7 0.1 collective-permute-start.3
  60.8 4.3 %collective-permute-done.1 = bf16[4,128,128]{2,1,0:T(8,128)(2,1)S(1)} collective-permute-done((bf16[4,128,128]{2,1,0:T(8,128)(2,1)S(1)}, bf16[4,128,128]{2,1,0:T(8,128)(2,1)S(1)}, u32[]{:S(2)}, u32[]{:S(2)}) %collective-permute-start.1) | collective-permute-done | bytes 131104 | tf_op jit(solution)/shard_map/ppermute | solution.py:323
  65.1 2.0 %collective-permute-done.2 = bf16[4,128,128]{2,1,0:T(8,128)(2,1)S(1)} collective-permute-done((bf16[4,128,128]{2,1,0:T(8,128)(2,1)S(1)}, bf16[4,128,128]{2,1,0:T(8,128)(2,1)S(1)}, u32[]{:S(2)}, u32[]{:S(2)}) %collective-permute-start.2) | collective-permute-done | bytes 131104 | tf_op jit(solution)/shard_map/ppermute | solution.py:323
  67.0 6.8 %collective-permute-done.3 = bf16[4,128,128]{2,1,0:T(8,128)(2,1)S(1)} collective-permute-done((bf16[4,128,128]{2,1,0:T(8,128)(2,1)S(1)}, bf16[4,128,128]{2,1,0:T(8,128)(2,1)S(1)}, u32[]{:S(2)}, u32[]{:S(2)}) %collective-permute-start.3) | collective-permute-done | bytes 131104 | tf_op jit(solution)/shard_map/ppermute | solution.py:323
  74.0 0.1 slice.19.refs_0_
  74.1 1.1 collective-permute-start.11
  75.2 0.6 collective-permute-start.12
  75.9 2.0 %copy-done = bf16[1024,1792]{1,0:T(8,128)(2,1)S(1)} copy-done((bf16[1024,1792]{1,0:T(8,128)(2,1)S(1)}, bf16[1024,1792]{1,0:T(8,128)(2,1)}, u32[]{:S(2)}) %copy-start) | copy-done | bytes 3670040
  77.9 1.9 %shard_map.67 = (bf16[128,896]{1,0:T(8,128)(2,1)S(1)}, bf16[128,896]{1,0:T(8,128)(2,1)S(1)}, bf16[128,896]{1,0:T(8,128)(2,1)S(1)}, f32[128,896]{1,0:T(8,128)S(1)}) custom-call(s32[3]{0:T(128)S(1)} %pad_add_fusion.place_ref, bf16[4,4,128,128]{3,2,1,0:T(8,128)(2,1)S(1)} %pad_maximum_fusion.1.own_ref, ...), custom_call_target="tpu_custom_call" | custom-call | flops 114688 | tf_op jit(solution)/shard_map/pallas_call | solution.py:290
  79.8 3.2 %collective-permute-start.8 = (bf16[128,896]{1,0:T(8,128)(2,1)S(1)}, bf16[128,896]{1,0:T(8,128)(2,1)S(1)}, u32[]{:S(2)}, u32[]{:S(2)}) collective-permute-start(bf16[128,896]{1,0:T(8,128)(2,1)S(1)} %get-tuple-element.57), channel_id=1, source_target_pairs={{0,8},{2,10},{4,12},{6,14},{8,16},{10,18},{12,20},{14,22},{16,24},... | collective-permute-start | bytes 688136 | tf_op jit(solution)/shard_map/ppermute | solution.py:382
  83.0 1.9 %shard_map.68 = (bf16[128,896]{1,0:T(8,128)(2,1)S(1)}, bf16[128,896]{1,0:T(8,128)(2,1)S(1)}, bf16[128,896]{1,0:T(8,128)(2,1)S(1)}, f32[128,896]{1,0:T(8,128)S(1)}) custom-call(s32[3]{0:T(128)S(1)} %pad_add_fusion.place_ref, bf16[4,4,128,128]{3,2,1,0:T(8,128)(2,1)S(1)} %pad_maximum_fusion.1.own_ref, ...), custom_call_target="tpu_custom_call" | custom-call | flops 114688 | tf_op jit(solution)/shard_map/pallas_call | solution.py:290
  84.9 0.7 collective-permute-start.7
  85.6 1.4 collective-permute-start.6
  87.0 3.1 %collective-permute-done.8 = bf16[128,896]{1,0:T(8,128)(2,1)S(1)} collective-permute-done((bf16[128,896]{1,0:T(8,128)(2,1)S(1)}, bf16[128,896]{1,0:T(8,128)(2,1)S(1)}, u32[]{:S(2)}, u32[]{:S(2)}) %collective-permute-start.8) | collective-permute-done | bytes 229408 | tf_op jit(solution)/shard_map/ppermute | solution.py:382
  90.1 0.4 collective-permute-start.5
  90.6 5.0 %collective-permute-done.7 = bf16[128,896]{1,0:T(8,128)(2,1)S(1)} collective-permute-done((bf16[128,896]{1,0:T(8,128)(2,1)S(1)}, bf16[128,896]{1,0:T(8,128)(2,1)S(1)}, u32[]{:S(2)}, u32[]{:S(2)}) %collective-permute-start.7) | collective-permute-done | bytes 229408 | tf_op jit(solution)/shard_map/ppermute | solution.py:382
  95.8 6.8 %collective-permute-done.11.refs_1_ = bf16[256,2304]{1,0:T(8,128)(2,1)S(1)} collective-permute-done((bf16[256,2304]{1,0:T(8,128)(2,1)S(1)}, bf16[256,2304]{1,0:T(8,128)(2,1)S(1)}, u32[]{:S(2)}, u32[]{:S(2)}) %collective-permute-start.11) | collective-permute-done | bytes 1179680 | tf_op jit(solution)/shard_map/ppermute | solution.py:327
  102.5 0.9 collective-permute-done.12.refs_2_
  103.4 1.1 fusion.1
  104.5 1.0 collective-permute-start.13
  105.6 0.5 collective-permute-start.14
  106.1 1.3 collective-permute-start.18
  107.5 7.1 %collective-permute-done.13.refs_3_ = bf16[128,1152]{1,0:T(8,128)(2,1)S(1)} collective-permute-done((bf16[128,1152]{1,0:T(8,128)(2,1)S(1)}, bf16[128,1152]{1,0:T(8,128)(2,1)S(1)}, u32[]{:S(2)}, u32[]{:S(2)}) %collective-permute-start.13) | collective-permute-done | bytes 294944 | tf_op jit(solution)/shard_map/ppermute | solution.py:331
  114.5 0.6 collective-permute-start.19
  115.1 3.2 %shard_map.69 = (bf16[128,1152]{1,0:T(8,128)(2,1)S(1)}, bf16[128,1152]{1,0:T(8,128)(2,1)S(1)}, bf16[128,1152]{1,0:T(8,128)(2,1)S(1)}, f32[128,1152]{1,0:T(8,128)S(1)}) custom-call(s32[3]{0:T(128)S(1)} %pad_add_fusion.place_ref, bf16[4,4,128,128]{3,2,1,0:T(8,128)(2,1)S(1)} %pad_maximum_fusion.1.own_ref, ...), custom_call_target="tpu_custom_call" | custom-call | flops 147456 | tf_op jit(solution)/shard_map/pallas_call | solution.py:290
  118.4 2.7 %collective-permute-start.16 = (bf16[128,1152]{1,0:T(8,128)(2,1)S(1)}, bf16[128,1152]{1,0:T(8,128)(2,1)S(1)}, u32[]{:S(2)}, u32[]{:S(2)}) collective-permute-start(bf16[128,1152]{1,0:T(8,128)(2,1)S(1)} %get-tuple-element.68), channel_id=1, source_target_pairs={{0,8},{2,10},{4,12},{6,14},{8,16},{10,18},{12,20},{14,22},{16,24},... | collective-permute-start | bytes 884744 | tf_op jit(solution)/shard_map/ppermute | solution.py:382
  121.2 1.2 collective-permute-start.15
  122.4 3.3 %shard_map.70 = (bf16[128,1152]{1,0:T(8,128)(2,1)S(1)}, bf16[128,1152]{1,0:T(8,128)(2,1)S(1)}, bf16[128,1152]{1,0:T(8,128)(2,1)S(1)}, f32[128,1152]{1,0:T(8,128)S(1)}) custom-call(s32[3]{0:T(128)S(1)} %pad_add_fusion.place_ref, bf16[4,4,128,128]{3,2,1,0:T(8,128)(2,1)S(1)} %pad_maximum_fusion.1.own_ref, ...), custom_call_target="tpu_custom_call" | custom-call | flops 147456 | tf_op jit(solution)/shard_map/pallas_call | solution.py:290
  125.7 1.9 %collective-permute-start.21 = (bf16[128,1152]{1,0:T(8,128)(2,1)S(1)}, bf16[128,1152]{1,0:T(8,128)(2,1)S(1)}, u32[]{:S(2)}, u32[]{:S(2)}) collective-permute-start(bf16[128,1152]{1,0:T(8,128)(2,1)S(1)} %get-tuple-element.74), channel_id=1, source_target_pairs={{8,0},{10,2},{12,4},{14,6},{16,8},{18,10},{20,12},{22,14},{24,16},... | collective-permute-start | bytes 884744 | tf_op jit(solution)/shard_map/ppermute | solution.py:382
  127.6 0.1 collective-permute-start.20
  127.7 2.4 %collective-permute-done.16 = bf16[128,1152]{1,0:T(8,128)(2,1)S(1)} collective-permute-done((bf16[128,1152]{1,0:T(8,128)(2,1)S(1)}, bf16[128,1152]{1,0:T(8,128)(2,1)S(1)}, u32[]{:S(2)}, u32[]{:S(2)}) %collective-permute-start.16) | collective-permute-done | bytes 294944 | tf_op jit(solution)/shard_map/ppermute | solution.py:382
  130.2 8.8 %collective-permute-start.17 = (bf16[128,1152]{1,0:T(8,128)(2,1)S(1)}, bf16[128,1152]{1,0:T(8,128)(2,1)S(1)}, u32[]{:S(2)}, u32[]{:S(2)}) collective-permute-start(bf16[128,1152]{1,0:T(8,128)(2,1)S(1)} %add_convert_fusion.3), channel_id=1, source_target_pairs={{0,8},{2,10},{4,12},{6,14},{8,16},{10,18},{12,20},{14,22},{16,24},... | collective-permute-start | bytes 884744 | tf_op jit(solution)/shard_map/ppermute | solution.py:386
  139.1 8.1 %collective-permute-done.21 = bf16[128,1152]{1,0:T(8,128)(2,1)S(1)} collective-permute-done((bf16[128,1152]{1,0:T(8,128)(2,1)S(1)}, bf16[128,1152]{1,0:T(8,128)(2,1)S(1)}, u32[]{:S(2)}, u32[]{:S(2)}) %collective-permute-start.21) | collective-permute-done | bytes 294944 | tf_op jit(solution)/shard_map/ppermute | solution.py:382
  147.3 7.2 %collective-permute-done.17 = bf16[128,1152]{1,0:T(8,128)(2,1)S(1)} collective-permute-done((bf16[128,1152]{1,0:T(8,128)(2,1)S(1)}, bf16[128,1152]{1,0:T(8,128)(2,1)S(1)}, u32[]{:S(2)}, u32[]{:S(2)}) %collective-permute-start.17) | collective-permute-done | bytes 294944 | tf_op jit(solution)/shard_map/ppermute | solution.py:386
  154.5 0.1 add_convert_fusion.2
  154.6 2.9 %collective-permute-done.22 = bf16[128,1152]{1,0:T(8,128)(2,1)S(1)} collective-permute-done((bf16[128,1152]{1,0:T(8,128)(2,1)S(1)}, bf16[128,1152]{1,0:T(8,128)(2,1)S(1)}, u32[]{:S(2)}, u32[]{:S(2)}) %collective-permute-start.22) | collective-permute-done | bytes 294944 | tf_op jit(solution)/shard_map/ppermute | solution.py:386
  157.5 0.1 add_convert_fusion
  157.6 1.1 pad_maximum_fusion
  (43 shorter events, 1.0 us)
Async XLA Ops:
  6.5 2.3 %copy-start.5 = (f32[3,3,2048]{2,1,0:T(4,128)S(1)}, f32[3,3,2048]{2,1,0:T(4,128)}, u32[]{:S(2)}) copy-start(f32[3,3,2048]{2,1,0:T(4,128)} %param.9) | copy-start | bytes 221188
  6.5 2.4 %copy-start.1 = (bf16[2048,128]{1,0:T(8,128)(2,1)S(1)}, bf16[2048,128]{1,0:T(8,128)(2,1)}, u32[]{:S(2)}) copy-start(bf16[2048,128]{1,0:T(8,128)(2,1)} %key_ref.1) | copy-start | bytes 1572868
  6.5 2.4 %copy-start.2 = (bf16[2048,128]{1,0:T(8,128)(2,1)S(1)}, bf16[2048,128]{1,0:T(8,128)(2,1)}, u32[]{:S(2)}) copy-start(bf16[2048,128]{1,0:T(8,128)(2,1)} %value_ref.1) | copy-start | bytes 1572868
  6.5 69.4 %all-gather.2.cloned.1.call-start = ((), (), s32[]{:S(2)}) async-start(), calls=%async_computation.2 | async-start | bytes 4587520 | tf_op jit(solution)/shard_map/all_gather | solution.py:343
  8.9 31.5 %copy-start.3 = (f32[128,2048]{1,0:T(8,128)S(1)}, f32[128,2048]{1,0:T(8,128)}, u32[]{:S(2)}) copy-start(f32[128,2048]{1,0:T(8,128)} %h_ref.1) | copy-start | bytes 3145732
  11.4 24.6 %all-to-all-start = ((bf16[16,144,128]{2,1,0:T(8,128)(2,1)}), bf16[16,144,128]{2,1,0:T(8,128)(2,1)S(1)}, u32[]{:S(2)}, u32[]{:S(2)}) async-start(bf16[16,144,128]{2,1,0:T(8,128)(2,1)} %shard_map.64), calls=%async_computation | async-start | bytes 1179648 | tf_op jit(solution)/shard_map/all_to_all | solution.py:351
  36.0 18.7 %all-to-all-start.1 = ((bf16[16,128,128]{2,1,0:T(8,128)(2,1)}), bf16[16,128,128]{2,1,0:T(8,128)(2,1)S(1)}, u32[]{:S(2)}, u32[]{:S(2)}) async-start(bf16[16,128,128]{2,1,0:T(8,128)(2,1)} %bitcast.3), calls=%async_computation.1 | async-start | bytes 1048576 | tf_op jit(solution)/shard_map/all_to_all | solution.py:354
  54.7 19.3 %copy-start.4 = (bf16[256,4096]{1,0:T(8,128)(2,1)S(1)}, bf16[256,4096]{1,0:T(8,128)(2,1)}, u32[]{:S(2)}) copy-start(bf16[256,4096]{1,0:T(8,128)(2,1)} %param.11) | copy-start | bytes 6291460
  56.6 4.2 %collective-permute-start = (bf16[4,128,128]{2,1,0:T(8,128)(2,1)S(1)}, bf16[4,128,128]{2,1,0:T(8,128)(2,1)S(1)}, u32[]{:S(2)}, u32[]{:S(2)}) collective-permute-start(bf16[4,128,128]{2,1,0:T(8,128)(2,1)S(1)} %get-tuple-element.42), channel_id=1, source_target_pairs={{0,0},{1,16},{2,2},{3,18},{4,4},{5,20},{6,6},{7,22},{8,1},{9,17},{... | collective-permute-start | bytes 393224 | tf_op jit(solution)/shard_map/ppermute | solution.py:323
  57.3 7.8 %collective-permute-start.1 = (bf16[4,128,128]{2,1,0:T(8,128)(2,1)S(1)}, bf16[4,128,128]{2,1,0:T(8,128)(2,1)S(1)}, u32[]{:S(2)}, u32[]{:S(2)}) collective-permute-start(bf16[4,128,128]{2,1,0:T(8,128)(2,1)S(1)} %get-tuple-element.44), channel_id=1, source_target_pairs={{0,2},{1,18},{2,0},{3,16},{4,6},{5,22},{6,4},{7,20},{8,3},{9,19},{... | collective-permute-start | bytes 393224 | tf_op jit(solution)/shard_map/ppermute | solution.py:323
  59.2 7.8 %collective-permute-start.2 = (bf16[4,128,128]{2,1,0:T(8,128)(2,1)S(1)}, bf16[4,128,128]{2,1,0:T(8,128)(2,1)S(1)}, u32[]{:S(2)}, u32[]{:S(2)}) collective-permute-start(bf16[4,128,128]{2,1,0:T(8,128)(2,1)S(1)} %get-tuple-element.45), channel_id=1, source_target_pairs={{0,4},{1,20},{2,6},{3,22},{4,0},{5,16},{6,2},{7,18},{8,5},{9,21},{... | collective-permute-start | bytes 393224 | tf_op jit(solution)/shard_map/ppermute | solution.py:323
  60.7 13.1 %collective-permute-start.3 = (bf16[4,128,128]{2,1,0:T(8,128)(2,1)S(1)}, bf16[4,128,128]{2,1,0:T(8,128)(2,1)S(1)}, u32[]{:S(2)}, u32[]{:S(2)}) collective-permute-start(bf16[4,128,128]{2,1,0:T(8,128)(2,1)S(1)} %get-tuple-element.46), channel_id=1, source_target_pairs={{0,6},{1,22},{2,4},{3,20},{4,2},{5,18},{6,0},{7,16},{8,7},{9,23},{... | collective-permute-start | bytes 393224 | tf_op jit(solution)/shard_map/ppermute | solution.py:323
  73.9 2.0 %collective-permute-start.4 = (bf16[4,4,128,128]{3,2,1,0:T(8,128)(2,1)S(1)}, bf16[4,4,128,128]{3,2,1,0:T(8,128)(2,1)S(1)}, u32[]{:S(2)}, u32[]{:S(2)}) collective-permute-start(bf16[4,4,128,128]{3,2,1,0:T(8,128)(2,1)S(1)} %pad_maximum_fusion.1.own_ref), channel_id=1, source_target_pairs={{0,1},{1,0},{2,3},{3,2},{4,5},{5,4},{6,7},{7,6},{8,9},{9,8},{10,11... | collective-permute-start | bytes 1572872 | tf_op jit(solution)/shard_map/ppermute | solution.py:365
  74.1 28.4 %collective-permute-start.11 = (bf16[256,2304]{1,0:T(8,128)(2,1)S(1)}, bf16[256,2304]{1,0:T(8,128)(2,1)S(1)}, u32[]{:S(2)}, u32[]{:S(2)}) collective-permute-start(bf16[256,2304]{1,0:T(8,128)(2,1)S(1)} %slice.19.refs_0_), channel_id=1, source_target_pairs={{0,2},{2,0},{4,6},{6,4},{8,10},{10,8},{12,14},{14,12},{16,18},{18,... | collective-permute-start | bytes 3538952 | tf_op jit(solution)/shard_map/ppermute | solution.py:327
  75.2 28.2 %collective-permute-start.12 = (bf16[256,2304]{1,0:T(8,128)(2,1)S(1)}, bf16[256,2304]{1,0:T(8,128)(2,1)}, u32[]{:S(2)}, u32[]{:S(2)}) collective-permute-start(bf16[256,2304]{1,0:T(8,128)(2,1)S(1)} %slice.19.refs_0_), channel_id=1, source_target_pairs={{0,4},{2,6},{4,0},{6,2},{8,12},{10,14},{12,8},{14,10},{16,20},{18,... | collective-permute-start | bytes 3538952 | tf_op jit(solution)/shard_map/ppermute | solution.py:327
  75.9 2.0 %copy-start = (bf16[1024,1792]{1,0:T(8,128)(2,1)S(1)}, bf16[1024,1792]{1,0:T(8,128)(2,1)}, u32[]{:S(2)}) copy-start(bf16[1024,1792]{1,0:T(8,128)(2,1)} %all-gather.2.cloned.1.call-done.refs_0_) | copy-start | bytes 11010052
  79.8 10.3 %collective-permute-start.8 = (bf16[128,896]{1,0:T(8,128)(2,1)S(1)}, bf16[128,896]{1,0:T(8,128)(2,1)S(1)}, u32[]{:S(2)}, u32[]{:S(2)}) collective-permute-start(bf16[128,896]{1,0:T(8,128)(2,1)S(1)} %get-tuple-element.57), channel_id=1, source_target_pairs={{0,8},{2,10},{4,12},{6,14},{8,16},{10,18},{12,20},{14,22},{16,24},... | collective-permute-start | bytes 688136 | tf_op jit(solution)/shard_map/ppermute | solution.py:382
  84.9 10.7 %collective-permute-start.7 = (bf16[128,896]{1,0:T(8,128)(2,1)S(1)}, bf16[128,896]{1,0:T(8,128)(2,1)S(1)}, u32[]{:S(2)}, u32[]{:S(2)}) collective-permute-start(bf16[128,896]{1,0:T(8,128)(2,1)S(1)} %get-tuple-element.52), channel_id=1, source_target_pairs={{8,0},{10,2},{12,4},{14,6},{16,8},{18,10},{20,12},{22,14},{24,16},... | collective-permute-start | bytes 688136 | tf_op jit(solution)/shard_map/ppermute | solution.py:382
  85.6 20.0 %collective-permute-start.6 = (bf16[128,896]{1,0:T(8,128)(2,1)S(1)}, bf16[128,896]{1,0:T(8,128)(2,1)S(1)}, u32[]{:S(2)}, u32[]{:S(2)}) collective-permute-start(bf16[128,896]{1,0:T(8,128)(2,1)S(1)} %get-tuple-element.50), channel_id=1, source_target_pairs={{0,8},{2,10},{4,12},{6,14},{8,16},{10,18},{12,20},{14,22},{16,24},... | collective-permute-start | bytes 688136 | tf_op jit(solution)/shard_map/ppermute | solution.py:383
  90.1 16.0 %collective-permute-start.5 = (bf16[128,896]{1,0:T(8,128)(2,1)S(1)}, bf16[128,896]{1,0:T(8,128)(2,1)S(1)}, u32[]{:S(2)}, u32[]{:S(2)}) collective-permute-start(bf16[128,896]{1,0:T(8,128)(2,1)S(1)} %get-tuple-element.48), channel_id=1, source_target_pairs={{8,0},{10,2},{12,4},{14,6},{16,8},{18,10},{20,12},{22,14},{24,16},... | collective-permute-start | bytes 688136 | tf_op jit(solution)/shard_map/ppermute | solution.py:383
  95.6 25.5 %collective-permute-start.9 = (bf16[128,896]{1,0:T(8,128)(2,1)S(1)}, bf16[128,896]{1,0:T(8,128)(2,1)S(1)}, u32[]{:S(2)}, u32[]{:S(2)}) collective-permute-start(bf16[128,896]{1,0:T(8,128)(2,1)S(1)} %add_convert_fusion.6), channel_id=1, source_target_pairs={{0,8},{2,10},{4,12},{6,14},{8,16},{10,18},{12,20},{14,22},{16,24},... | collective-permute-start | bytes 688136 | tf_op jit(solution)/shard_map/ppermute | solution.py:370
  102.5 18.6 %collective-permute-start.10 = (bf16[128,896]{1,0:T(8,128)(2,1)S(1)}, bf16[128,896]{1,0:T(8,128)(2,1)S(1)}, u32[]{:S(2)}, u32[]{:S(2)}) collective-permute-start(bf16[128,896]{1,0:T(8,128)(2,1)S(1)} %add_convert_fusion.7), channel_id=1, source_target_pairs={{8,0},{10,2},{12,4},{14,6},{16,8},{18,10},{20,12},{22,14},{24,16},... | collective-permute-start | bytes 688136 | tf_op jit(solution)/shard_map/ppermute | solution.py:370
  104.5 10.0 %collective-permute-start.13 = (bf16[128,1152]{1,0:T(8,128)(2,1)S(1)}, bf16[128,1152]{1,0:T(8,128)(2,1)S(1)}, u32[]{:S(2)}, u32[]{:S(2)}) collective-permute-start(bf16[128,1152]{1,0:T(8,128)(2,1)S(1)} %get-tuple-element.77), channel_id=1, source_target_pairs={{0,2},{2,0},{4,6},{6,4},{8,10},{10,8},{12,14},{14,12},{16,18},{18,... | collective-permute-start | bytes 884744 | tf_op jit(solution)/shard_map/ppermute | solution.py:331
  105.6 9.5 %collective-permute-start.14 = (bf16[128,1152]{1,0:T(8,128)(2,1)S(1)}, bf16[128,1152]{1,0:T(8,128)(2,1)S(1)}, u32[]{:S(2)}, u32[]{:S(2)}) collective-permute-start(bf16[128,1152]{1,0:T(8,128)(2,1)S(1)} %get-tuple-element.75), channel_id=1, source_target_pairs={{0,4},{2,6},{4,0},{6,2},{8,12},{10,14},{12,8},{14,10},{16,20},{18,... | collective-permute-start | bytes 884744 | tf_op jit(solution)/shard_map/ppermute | solution.py:332
  106.1 16.3 %collective-permute-start.18 = (bf16[128,1152]{1,0:T(8,128)(2,1)S(1)}, bf16[128,1152]{1,0:T(8,128)(2,1)S(1)}, u32[]{:S(2)}, u32[]{:S(2)}) collective-permute-start(bf16[128,1152]{1,0:T(8,128)(2,1)S(1)} %get-tuple-element.78), channel_id=1, source_target_pairs={{0,2},{2,0},{4,6},{6,4},{8,10},{10,8},{12,14},{14,12},{16,18},{18,... | collective-permute-start | bytes 884744 | tf_op jit(solution)/shard_map/ppermute | solution.py:331
  114.5 7.9 %collective-permute-start.19 = (bf16[128,1152]{1,0:T(8,128)(2,1)S(1)}, bf16[128,1152]{1,0:T(8,128)(2,1)S(1)}, u32[]{:S(2)}, u32[]{:S(2)}) collective-permute-start(bf16[128,1152]{1,0:T(8,128)(2,1)S(1)} %get-tuple-element.76), channel_id=1, source_target_pairs={{0,4},{2,6},{4,0},{6,2},{8,12},{10,14},{12,8},{14,10},{16,20},{18,... | collective-permute-start | bytes 884744 | tf_op jit(solution)/shard_map/ppermute | solution.py:332
  118.4 11.8 %collective-permute-start.16 = (bf16[128,1152]{1,0:T(8,128)(2,1)S(1)}, bf16[128,1152]{1,0:T(8,128)(2,1)S(1)}, u32[]{:S(2)}, u32[]{:S(2)}) collective-permute-start(bf16[128,1152]{1,0:T(8,128)(2,1)S(1)} %get-tuple-element.68), channel_id=1, source_target_pairs={{0,8},{2,10},{4,12},{6,14},{8,16},{10,18},{12,20},{14,22},{16,24},... | collective-permute-start | bytes 884744 | tf_op jit(solution)/shard_map/ppermute | solution.py:382
  121.2 26.1 %collective-permute-start.15 = (bf16[128,1152]{1,0:T(8,128)(2,1)S(1)}, bf16[128,1152]{1,0:T(8,128)(2,1)S(1)}, u32[]{:S(2)}, u32[]{:S(2)}) collective-permute-start(bf16[128,1152]{1,0:T(8,128)(2,1)S(1)} %get-tuple-element.66), channel_id=1, source_target_pairs={{8,0},{10,2},{12,4},{14,6},{16,8},{18,10},{20,12},{22,14},{24,16},... | collective-permute-start | bytes 884744 | tf_op jit(solution)/shard_map/ppermute | solution.py:383
  125.7 21.5 %collective-permute-start.21 = (bf16[128,1152]{1,0:T(8,128)(2,1)S(1)}, bf16[128,1152]{1,0:T(8,128)(2,1)S(1)}, u32[]{:S(2)}, u32[]{:S(2)}) collective-permute-start(bf16[128,1152]{1,0:T(8,128)(2,1)S(1)} %get-tuple-element.74), channel_id=1, source_target_pairs={{8,0},{10,2},{12,4},{14,6},{16,8},{18,10},{20,12},{22,14},{24,16},... | collective-permute-start | bytes 884744 | tf_op jit(solution)/shard_map/ppermute | solution.py:382
  127.6 27.0 %collective-permute-start.20 = (bf16[128,1152]{1,0:T(8,128)(2,1)S(1)}, bf16[128,1152]{1,0:T(8,128)(2,1)S(1)}, u32[]{:S(2)}, u32[]{:S(2)}) collective-permute-start(bf16[128,1152]{1,0:T(8,128)(2,1)S(1)} %get-tuple-element.72), channel_id=1, source_target_pairs={{0,8},{2,10},{4,12},{6,14},{8,16},{10,18},{12,20},{14,22},{16,24},... | collective-permute-start | bytes 884744 | tf_op jit(solution)/shard_map/ppermute | solution.py:383
  130.2 24.3 %collective-permute-start.17 = (bf16[128,1152]{1,0:T(8,128)(2,1)S(1)}, bf16[128,1152]{1,0:T(8,128)(2,1)S(1)}, u32[]{:S(2)}, u32[]{:S(2)}) collective-permute-start(bf16[128,1152]{1,0:T(8,128)(2,1)S(1)} %add_convert_fusion.3), channel_id=1, source_target_pairs={{0,8},{2,10},{4,12},{6,14},{8,16},{10,18},{12,20},{14,22},{16,24},... | collective-permute-start | bytes 884744 | tf_op jit(solution)/shard_map/ppermute | solution.py:386
  147.2 10.3 %collective-permute-start.22 = (bf16[128,1152]{1,0:T(8,128)(2,1)S(1)}, bf16[128,1152]{1,0:T(8,128)(2,1)S(1)}, u32[]{:S(2)}, u32[]{:S(2)}) collective-permute-start(bf16[128,1152]{1,0:T(8,128)(2,1)S(1)} %add_convert_fusion.1), channel_id=1, source_target_pairs={{8,0},{10,2},{12,4},{14,6},{16,8},{18,10},{20,12},{22,14},{24,16},... | collective-permute-start | bytes 884744 | tf_op jit(solution)/shard_map/ppermute | solution.py:386
Sparse Core Ops, SparseCore 0:
  9.2 66.0 all-gather.1

commit v7 on v6

--- a/solution.py
+++ b/solution.py
@@ -197,11 +197,11 @@
     channels = filters.shape[0]
     return pl.pallas_call(
         conv_kernel,
-        out_shape=jax.ShapeDtypeStruct((channels * blocks, width), jnp.float32),
+        out_shape=jax.ShapeDtypeStruct(((channels + 1) * blocks, width), jnp.float32),
         in_specs=[VMEM] * 3,
         out_specs=VMEM,
         scratch_shapes=[
-            pltpu.VMEM((blocks * channels, width), jnp.float32),
+            pltpu.VMEM(((blocks + 1) * channels, width), jnp.float32),
             pltpu.VMEM((blocks, channels, width), jnp.float32),
             pltpu.VMEM((GROUP, width // BAND, 2 * blocks + 8, width), jnp.float32),
         ],

time: 166 us -> 166 us (level)
  no operation moved by 1% of the time
where the time goes in v7:
time: 166 us
  waiting for transfers between devices  72.9 us (44%)
  starting transfers between devices  42.7 us (26%)
  Pallas kernels  28.8 us (17%)
  between operations  13.6 us (8%)
  local copies, waits for them, and re-layouts  5.61 us (3%)
  other arithmetic  1.83 us (1%)
    ppermute x4, waiting for transfers between devices, by_planes(): far = lax.ppermute(far, 'seq', forth)  18.6 us
    all_to_all x1, waiting for transfers between devices, by_planes(): lax.all_to_all(product, 'seq', split_axis=0, concat_axis=0, tiled=True)  16.3 us
    pallas_call x1, Pallas kernels, convolve(): pl.pallas_call(conv_kernel, out_shape=jax.ShapeDtypeStruct(((channels + 1...  14.3 us
    ppermute x4, waiting for transfers between devices, to_plane_of_rows(): return lax.ppermute(message, ('seq', 'tp'), pairs)  13 us
    pallas_call x4, Pallas kernels, project(): pl.pallas_call(project_kernel, out_shape=[jax.ShapeDtypeStruct((rows, col...  10.3 us
    ppermute x1, starting transfers between devices, by_planes(): lax.ppermute(sums[-2], 'seq', up)  8.85 us
    ppermute x4, starting transfers between devices, by_planes(): far = lax.ppermute(far, 'seq', forth)  8.64 us
    all_to_all x1, starting transfers between devices, by_planes(): lax.all_to_all(product, 'seq', split_axis=0, concat_axis=0, tiled=True)  8.32 us
  transfers between devices with their start and end apart: 26, of which 14 were waited for; matrix products, arithmetic and copies ran while one was open for 1% of the time, Pallas kernels for 17%

profile of v7, /device:TPU:0, one launch (start us, length us, event | category | flops | bytes accessed | tf_op | source)
XLA Modules:
  0.0 165.5 jit_solution(17518961902722600810)
XLA Ops:
  6.5 2.3 %slice.18 = bf16[256,1792]{1,0:T(8,128)(2,1)} slice(bf16[256,4096]{1,0:T(8,128)(2,1)} %param.11), slice={[0:256], [0:1792]} | slice | bytes 1835008 | tf_op jit(solution)/shard_map/slice | solution.py:342
  8.9 2.5 %shard_map.64 = bf16[16,144,128]{2,1,0:T(8,128)(2,1)} custom-call(f32[16,2048]{1,0:T(8,128)S(1)} %pad.4.taps_ref, bf16[2048,128]{1,0:T(8,128)(2,1)S(1)} %copy-done.1, bf16[2048,128]{1,0:T(8,128)(2,1)S(1)} %copy-done.2), custom_call_target="tpu_custom_call" | custom-call | tf_op jit(solution)/shard_map/pallas_call | solution.py:92
  11.4 8.3 %all-to-all-start = ((bf16[16,144,128]{2,1,0:T(8,128)(2,1)}), bf16[16,144,128]{2,1,0:T(8,128)(2,1)S(1)}, u32[]{:S(2)}, u32[]{:S(2)}) async-start(bf16[16,144,128]{2,1,0:T(8,128)(2,1)} %shard_map.64), calls=%async_computation | async-start | bytes 1179648 | tf_op jit(solution)/shard_map/all_to_all | solution.py:351
  19.7 16.3 %all-to-all-done.x_ref = bf16[16,144,128]{2,1,0:T(8,128)(2,1)S(1)} async-done(((bf16[16,144,128]{2,1,0:T(8,128)(2,1)}), bf16[16,144,128]{2,1,0:T(8,128)(2,1)S(1)}, u32[]{:S(2)}, u32[]{:S(2)}) %all-to-all-start) | async-done | bytes 589856 | tf_op jit(solution)/shard_map/all_to_all | solution.py:351
  36.0 4.4 %all-to-all-start.1 = ((bf16[16,128,128]{2,1,0:T(8,128)(2,1)}), bf16[16,128,128]{2,1,0:T(8,128)(2,1)S(1)}, u32[]{:S(2)}, u32[]{:S(2)}) async-start(bf16[16,128,128]{2,1,0:T(8,128)(2,1)} %bitcast.3), calls=%async_computation.1 | async-start | bytes 1048576 | tf_op jit(solution)/shard_map/all_to_all | solution.py:354
  40.5 14.3 %shard_map.65.y_ref = f32[2064,128]{1,0:T(8,128)S(1)} custom-call(f32[16,128]{1,0:T(8,128)S(1)} %constant_dynamic-slice_fusion.taps_ref, bf16[16,144,128]{2,1,0:T(8,128)(2,1)S(1)} %all-to-all-done.x_ref, f32[128,2048]{1,0:T(8,128)S(1)} %copy-done.3), custom_call_target="tpu_custom_call" | custom-call | flops 8589934592 | bytes 2621440 | tf_op jit(solution)/shard_map/pallas_call | solution.py:198
  54.7 1.8 %shard_map.66 = (bf16[4,128,128]{2,1,0:T(8,128)(2,1)S(1)}, bf16[4,128,128]{2,1,0:T(8,128)(2,1)S(1)}, bf16[4,128,128]{2,1,0:T(8,128)(2,1)S(1)}, bf16[4,128,128]{2,1,0:T(8,128)(2,1)S(1)}) custom-call(s32[3]{0:T(128)S(1)} %pad_add_fusion.place_ref, f32[16,128]{1,0:T(8,128)S(1)} %constant_dynamic-slice_fusion.taps_ref, ...), custom_call_target="tpu_custom_call" | custom-call | tf_op jit(solution)/shard_map/pallas_call | solution.py:240
  56.6 0.7 collective-permute-start
  57.3 2.0 %collective-permute-start.1 = (bf16[4,128,128]{2,1,0:T(8,128)(2,1)S(1)}, bf16[4,128,128]{2,1,0:T(8,128)(2,1)S(1)}, u32[]{:S(2)}, u32[]{:S(2)}) collective-permute-start(bf16[4,128,128]{2,1,0:T(8,128)(2,1)S(1)} %get-tuple-element.44), channel_id=1, source_target_pairs={{0,2},{1,18},{2,0},{3,16},{4,6},{5,22},{6,4},{7,20},{8,3},{9,19},{... | collective-permute-start | bytes 393224 | tf_op jit(solution)/shard_map/ppermute | solution.py:323
  59.2 1.5 collective-permute-start.2
  60.7 0.1 collective-permute-start.3
  60.8 4.2 %collective-permute-done.1 = bf16[4,128,128]{2,1,0:T(8,128)(2,1)S(1)} collective-permute-done((bf16[4,128,128]{2,1,0:T(8,128)(2,1)S(1)}, bf16[4,128,128]{2,1,0:T(8,128)(2,1)S(1)}, u32[]{:S(2)}, u32[]{:S(2)}) %collective-permute-start.1) | collective-permute-done | bytes 131104 | tf_op jit(solution)/shard_map/ppermute | solution.py:323
  65.1 2.0 %collective-permute-done.2 = bf16[4,128,128]{2,1,0:T(8,128)(2,1)S(1)} collective-permute-done((bf16[4,128,128]{2,1,0:T(8,128)(2,1)S(1)}, bf16[4,128,128]{2,1,0:T(8,128)(2,1)S(1)}, u32[]{:S(2)}, u32[]{:S(2)}) %collective-permute-start.2) | collective-permute-done | bytes 131104 | tf_op jit(solution)/shard_map/ppermute | solution.py:323
  67.0 6.8 %collective-permute-done.3 = bf16[4,128,128]{2,1,0:T(8,128)(2,1)S(1)} collective-permute-done((bf16[4,128,128]{2,1,0:T(8,128)(2,1)S(1)}, bf16[4,128,128]{2,1,0:T(8,128)(2,1)S(1)}, u32[]{:S(2)}, u32[]{:S(2)}) %collective-permute-start.3) | collective-permute-done | bytes 131104 | tf_op jit(solution)/shard_map/ppermute | solution.py:323
  74.0 0.1 slice.19.refs_0_
  74.1 1.1 collective-permute-start.11
  75.2 0.6 collective-permute-start.12
  75.9 2.0 %copy-done = bf16[1024,1792]{1,0:T(8,128)(2,1)S(1)} copy-done((bf16[1024,1792]{1,0:T(8,128)(2,1)S(1)}, bf16[1024,1792]{1,0:T(8,128)(2,1)}, u32[]{:S(2)}) %copy-start) | copy-done | bytes 3670040
  77.9 1.9 %shard_map.67 = (bf16[128,896]{1,0:T(8,128)(2,1)S(1)}, bf16[128,896]{1,0:T(8,128)(2,1)S(1)}, bf16[128,896]{1,0:T(8,128)(2,1)S(1)}, f32[128,896]{1,0:T(8,128)S(1)}) custom-call(s32[3]{0:T(128)S(1)} %pad_add_fusion.place_ref, bf16[4,4,128,128]{3,2,1,0:T(8,128)(2,1)S(1)} %pad_maximum_fusion.1.own_ref, ...), custom_call_target="tpu_custom_call" | custom-call | flops 114688 | tf_op jit(solution)/shard_map/pallas_call | solution.py:290
  79.8 3.3 %collective-permute-start.8 = (bf16[128,896]{1,0:T(8,128)(2,1)S(1)}, bf16[128,896]{1,0:T(8,128)(2,1)S(1)}, u32[]{:S(2)}, u32[]{:S(2)}) collective-permute-start(bf16[128,896]{1,0:T(8,128)(2,1)S(1)} %get-tuple-element.57), channel_id=1, source_target_pairs={{0,8},{2,10},{4,12},{6,14},{8,16},{10,18},{12,20},{14,22},{16,24},... | collective-permute-start | bytes 688136 | tf_op jit(solution)/shard_map/ppermute | solution.py:382
  83.1 1.9 %shard_map.68 = (bf16[128,896]{1,0:T(8,128)(2,1)S(1)}, bf16[128,896]{1,0:T(8,128)(2,1)S(1)}, bf16[128,896]{1,0:T(8,128)(2,1)S(1)}, f32[128,896]{1,0:T(8,128)S(1)}) custom-call(s32[3]{0:T(128)S(1)} %pad_add_fusion.place_ref, bf16[4,4,128,128]{3,2,1,0:T(8,128)(2,1)S(1)} %pad_maximum_fusion.1.own_ref, ...), custom_call_target="tpu_custom_call" | custom-call | flops 114688 | tf_op jit(solution)/shard_map/pallas_call | solution.py:290
  85.0 0.7 collective-permute-start.7
  85.6 1.4 collective-permute-start.6
  87.0 3.1 %collective-permute-done.8 = bf16[128,896]{1,0:T(8,128)(2,1)S(1)} collective-permute-done((bf16[128,896]{1,0:T(8,128)(2,1)S(1)}, bf16[128,896]{1,0:T(8,128)(2,1)S(1)}, u32[]{:S(2)}, u32[]{:S(2)}) %collective-permute-start.8) | collective-permute-done | bytes 229408 | tf_op jit(solution)/shard_map/ppermute | solution.py:382
  90.1 0.4 collective-permute-start.5
  90.6 5.0 %collective-permute-done.7 = bf16[128,896]{1,0:T(8,128)(2,1)S(1)} collective-permute-done((bf16[128,896]{1,0:T(8,128)(2,1)S(1)}, bf16[128,896]{1,0:T(8,128)(2,1)S(1)}, u32[]{:S(2)}, u32[]{:S(2)}) %collective-permute-start.7) | collective-permute-done | bytes 229408 | tf_op jit(solution)/shard_map/ppermute | solution.py:382
  95.8 6.8 %collective-permute-done.11.refs_1_ = bf16[256,2304]{1,0:T(8,128)(2,1)S(1)} collective-permute-done((bf16[256,2304]{1,0:T(8,128)(2,1)S(1)}, bf16[256,2304]{1,0:T(8,128)(2,1)S(1)}, u32[]{:S(2)}, u32[]{:S(2)}) %collective-permute-start.11) | collective-permute-done | bytes 1179680 | tf_op jit(solution)/shard_map/ppermute | solution.py:327
  102.5 0.9 collective-permute-done.12.refs_2_
  103.4 1.1 fusion.1
  104.5 1.0 collective-permute-start.13
  105.6 0.5 collective-permute-start.14
  106.2 1.3 collective-permute-start.18
  107.5 7.1 %collective-permute-done.13.refs_3_ = bf16[128,1152]{1,0:T(8,128)(2,1)S(1)} collective-permute-done((bf16[128,1152]{1,0:T(8,128)(2,1)S(1)}, bf16[128,1152]{1,0:T(8,128)(2,1)S(1)}, u32[]{:S(2)}, u32[]{:S(2)}) %collective-permute-start.13) | collective-permute-done | bytes 294944 | tf_op jit(solution)/shard_map/ppermute | solution.py:331
  114.5 0.6 collective-permute-start.19
  115.1 3.2 %shard_map.69 = (bf16[128,1152]{1,0:T(8,128)(2,1)S(1)}, bf16[128,1152]{1,0:T(8,128)(2,1)S(1)}, bf16[128,1152]{1,0:T(8,128)(2,1)S(1)}, f32[128,1152]{1,0:T(8,128)S(1)}) custom-call(s32[3]{0:T(128)S(1)} %pad_add_fusion.place_ref, bf16[4,4,128,128]{3,2,1,0:T(8,128)(2,1)S(1)} %pad_maximum_fusion.1.own_ref, ...), custom_call_target="tpu_custom_call" | custom-call | flops 147456 | tf_op jit(solution)/shard_map/pallas_call | solution.py:290
  118.3 2.8 %collective-permute-start.16 = (bf16[128,1152]{1,0:T(8,128)(2,1)S(1)}, bf16[128,1152]{1,0:T(8,128)(2,1)S(1)}, u32[]{:S(2)}, u32[]{:S(2)}) collective-permute-start(bf16[128,1152]{1,0:T(8,128)(2,1)S(1)} %get-tuple-element.68), channel_id=1, source_target_pairs={{0,8},{2,10},{4,12},{6,14},{8,16},{10,18},{12,20},{14,22},{16,24},... | collective-permute-start | bytes 884744 | tf_op jit(solution)/shard_map/ppermute | solution.py:382
  121.2 1.2 collective-permute-start.15
  122.4 3.3 %shard_map.70 = (bf16[128,1152]{1,0:T(8,128)(2,1)S(1)}, bf16[128,1152]{1,0:T(8,128)(2,1)S(1)}, bf16[128,1152]{1,0:T(8,128)(2,1)S(1)}, f32[128,1152]{1,0:T(8,128)S(1)}) custom-call(s32[3]{0:T(128)S(1)} %pad_add_fusion.place_ref, bf16[4,4,128,128]{3,2,1,0:T(8,128)(2,1)S(1)} %pad_maximum_fusion.1.own_ref, ...), custom_call_target="tpu_custom_call" | custom-call | flops 147456 | tf_op jit(solution)/shard_map/pallas_call | solution.py:290
  125.6 2.0 %collective-permute-start.21 = (bf16[128,1152]{1,0:T(8,128)(2,1)S(1)}, bf16[128,1152]{1,0:T(8,128)(2,1)S(1)}, u32[]{:S(2)}, u32[]{:S(2)}) collective-permute-start(bf16[128,1152]{1,0:T(8,128)(2,1)S(1)} %get-tuple-element.74), channel_id=1, source_target_pairs={{8,0},{10,2},{12,4},{14,6},{16,8},{18,10},{20,12},{22,14},{24,16},... | collective-permute-start | bytes 884744 | tf_op jit(solution)/shard_map/ppermute | solution.py:382
  127.6 0.1 collective-permute-start.20
  127.7 2.4 %collective-permute-done.16 = bf16[128,1152]{1,0:T(8,128)(2,1)S(1)} collective-permute-done((bf16[128,1152]{1,0:T(8,128)(2,1)S(1)}, bf16[128,1152]{1,0:T(8,128)(2,1)S(1)}, u32[]{:S(2)}, u32[]{:S(2)}) %collective-permute-start.16) | collective-permute-done | bytes 294944 | tf_op jit(solution)/shard_map/ppermute | solution.py:382
  130.2 8.8 %collective-permute-start.17 = (bf16[128,1152]{1,0:T(8,128)(2,1)S(1)}, bf16[128,1152]{1,0:T(8,128)(2,1)S(1)}, u32[]{:S(2)}, u32[]{:S(2)}) collective-permute-start(bf16[128,1152]{1,0:T(8,128)(2,1)S(1)} %add_convert_fusion.3), channel_id=1, source_target_pairs={{0,8},{2,10},{4,12},{6,14},{8,16},{10,18},{12,20},{14,22},{16,24},... | collective-permute-start | bytes 884744 | tf_op jit(solution)/shard_map/ppermute | solution.py:386
  139.1 8.1 %collective-permute-done.21 = bf16[128,1152]{1,0:T(8,128)(2,1)S(1)} collective-permute-done((bf16[128,1152]{1,0:T(8,128)(2,1)S(1)}, bf16[128,1152]{1,0:T(8,128)(2,1)S(1)}, u32[]{:S(2)}, u32[]{:S(2)}) %collective-permute-start.21) | collective-permute-done | bytes 294944 | tf_op jit(solution)/shard_map/ppermute | solution.py:382
  147.3 7.2 %collective-permute-done.17 = bf16[128,1152]{1,0:T(8,128)(2,1)S(1)} collective-permute-done((bf16[128,1152]{1,0:T(8,128)(2,1)S(1)}, bf16[128,1152]{1,0:T(8,128)(2,1)S(1)}, u32[]{:S(2)}, u32[]{:S(2)}) %collective-permute-start.17) | collective-permute-done | bytes 294944 | tf_op jit(solution)/shard_map/ppermute | solution.py:386
  154.5 0.1 add_convert_fusion.2
  154.6 2.9 %collective-permute-done.22 = bf16[128,1152]{1,0:T(8,128)(2,1)S(1)} collective-permute-done((bf16[128,1152]{1,0:T(8,128)(2,1)S(1)}, bf16[128,1152]{1,0:T(8,128)(2,1)S(1)}, u32[]{:S(2)}, u32[]{:S(2)}) %collective-permute-start.22) | collective-permute-done | bytes 294944 | tf_op jit(solution)/shard_map/ppermute | solution.py:386
  157.5 0.1 add_convert_fusion
  157.6 1.1 pad_maximum_fusion
  (43 shorter events, 1.0 us)
Async XLA Ops:
  6.5 2.3 %copy-start.5 = (f32[3,3,2048]{2,1,0:T(4,128)S(1)}, f32[3,3,2048]{2,1,0:T(4,128)}, u32[]{:S(2)}) copy-start(f32[3,3,2048]{2,1,0:T(4,128)} %param.9) | copy-start | bytes 221188
  6.5 2.4 %copy-start.1 = (bf16[2048,128]{1,0:T(8,128)(2,1)S(1)}, bf16[2048,128]{1,0:T(8,128)(2,1)}, u32[]{:S(2)}) copy-start(bf16[2048,128]{1,0:T(8,128)(2,1)} %key_ref.1) | copy-start | bytes 1572868
  6.5 2.4 %copy-start.2 = (bf16[2048,128]{1,0:T(8,128)(2,1)S(1)}, bf16[2048,128]{1,0:T(8,128)(2,1)}, u32[]{:S(2)}) copy-start(bf16[2048,128]{1,0:T(8,128)(2,1)} %value_ref.1) | copy-start | bytes 1572868
  6.5 69.3 %all-gather.2.cloned.1.call-start = ((), (), s32[]{:S(2)}) async-start(), calls=%async_computation.2 | async-start | bytes 4587520 | tf_op jit(solution)/shard_map/all_gather | solution.py:343
  8.9 31.5 %copy-start.3 = (f32[128,2048]{1,0:T(8,128)S(1)}, f32[128,2048]{1,0:T(8,128)}, u32[]{:S(2)}) copy-start(f32[128,2048]{1,0:T(8,128)} %h_ref.1) | copy-start | bytes 3145732
  11.4 24.6 %all-to-all-start = ((bf16[16,144,128]{2,1,0:T(8,128)(2,1)}), bf16[16,144,128]{2,1,0:T(8,128)(2,1)S(1)}, u32[]{:S(2)}, u32[]{:S(2)}) async-start(bf16[16,144,128]{2,1,0:T(8,128)(2,1)} %shard_map.64), calls=%async_computation | async-start | bytes 1179648 | tf_op jit(solution)/shard_map/all_to_all | solution.py:351
  36.0 18.7 %all-to-all-start.1 = ((bf16[16,128,128]{2,1,0:T(8,128)(2,1)}), bf16[16,128,128]{2,1,0:T(8,128)(2,1)S(1)}, u32[]{:S(2)}, u32[]{:S(2)}) async-start(bf16[16,128,128]{2,1,0:T(8,128)(2,1)} %bitcast.3), calls=%async_computation.1 | async-start | bytes 1048576 | tf_op jit(solution)/shard_map/all_to_all | solution.py:354
  54.7 19.3 %copy-start.4 = (bf16[256,4096]{1,0:T(8,128)(2,1)S(1)}, bf16[256,4096]{1,0:T(8,128)(2,1)}, u32[]{:S(2)}) copy-start(bf16[256,4096]{1,0:T(8,128)(2,1)} %param.11) | copy-start | bytes 6291460
  56.6 4.2 %collective-permute-start = (bf16[4,128,128]{2,1,0:T(8,128)(2,1)S(1)}, bf16[4,128,128]{2,1,0:T(8,128)(2,1)S(1)}, u32[]{:S(2)}, u32[]{:S(2)}) collective-permute-start(bf16[4,128,128]{2,1,0:T(8,128)(2,1)S(1)} %get-tuple-element.42), channel_id=1, source_target_pairs={{0,0},{1,16},{2,2},{3,18},{4,4},{5,20},{6,6},{7,22},{8,1},{9,17},{... | collective-permute-start | bytes 393224 | tf_op jit(solution)/shard_map/ppermute | solution.py:323
  57.3 7.8 %collective-permute-start.1 = (bf16[4,128,128]{2,1,0:T(8,128)(2,1)S(1)}, bf16[4,128,128]{2,1,0:T(8,128)(2,1)S(1)}, u32[]{:S(2)}, u32[]{:S(2)}) collective-permute-start(bf16[4,128,128]{2,1,0:T(8,128)(2,1)S(1)} %get-tuple-element.44), channel_id=1, source_target_pairs={{0,2},{1,18},{2,0},{3,16},{4,6},{5,22},{6,4},{7,20},{8,3},{9,19},{... | collective-permute-start | bytes 393224 | tf_op jit(solution)/shard_map/ppermute | solution.py:323
  59.2 7.8 %collective-permute-start.2 = (bf16[4,128,128]{2,1,0:T(8,128)(2,1)S(1)}, bf16[4,128,128]{2,1,0:T(8,128)(2,1)S(1)}, u32[]{:S(2)}, u32[]{:S(2)}) collective-permute-start(bf16[4,128,128]{2,1,0:T(8,128)(2,1)S(1)} %get-tuple-element.45), channel_id=1, source_target_pairs={{0,4},{1,20},{2,6},{3,22},{4,0},{5,16},{6,2},{7,18},{8,5},{9,21},{... | collective-permute-start | bytes 393224 | tf_op jit(solution)/shard_map/ppermute | solution.py:323
  60.7 13.1 %collective-permute-start.3 = (bf16[4,128,128]{2,1,0:T(8,128)(2,1)S(1)}, bf16[4,128,128]{2,1,0:T(8,128)(2,1)S(1)}, u32[]{:S(2)}, u32[]{:S(2)}) collective-permute-start(bf16[4,128,128]{2,1,0:T(8,128)(2,1)S(1)} %get-tuple-element.46), channel_id=1, source_target_pairs={{0,6},{1,22},{2,4},{3,20},{4,2},{5,18},{6,0},{7,16},{8,7},{9,23},{... | collective-permute-start | bytes 393224 | tf_op jit(solution)/shard_map/ppermute | solution.py:323
  73.9 2.0 %collective-permute-start.4 = (bf16[4,4,128,128]{3,2,1,0:T(8,128)(2,1)S(1)}, bf16[4,4,128,128]{3,2,1,0:T(8,128)(2,1)S(1)}, u32[]{:S(2)}, u32[]{:S(2)}) collective-permute-start(bf16[4,4,128,128]{3,2,1,0:T(8,128)(2,1)S(1)} %pad_maximum_fusion.1.own_ref), channel_id=1, source_target_pairs={{0,1},{1,0},{2,3},{3,2},{4,5},{5,4},{6,7},{7,6},{8,9},{9,8},{10,11... | collective-permute-start | bytes 1572872 | tf_op jit(solution)/shard_map/ppermute | solution.py:365
  74.1 28.4 %collective-permute-start.11 = (bf16[256,2304]{1,0:T(8,128)(2,1)S(1)}, bf16[256,2304]{1,0:T(8,128)(2,1)S(1)}, u32[]{:S(2)}, u32[]{:S(2)}) collective-permute-start(bf16[256,2304]{1,0:T(8,128)(2,1)S(1)} %slice.19.refs_0_), channel_id=1, source_target_pairs={{0,2},{2,0},{4,6},{6,4},{8,10},{10,8},{12,14},{14,12},{16,18},{18,... | collective-permute-start | bytes 3538952 | tf_op jit(solution)/shard_map/ppermute | solution.py:327
  75.2 28.2 %collective-permute-start.12 = (bf16[256,2304]{1,0:T(8,128)(2,1)S(1)}, bf16[256,2304]{1,0:T(8,128)(2,1)}, u32[]{:S(2)}, u32[]{:S(2)}) collective-permute-start(bf16[256,2304]{1,0:T(8,128)(2,1)S(1)} %slice.19.refs_0_), channel_id=1, source_target_pairs={{0,4},{2,6},{4,0},{6,2},{8,12},{10,14},{12,8},{14,10},{16,20},{18,... | collective-permute-start | bytes 3538952 | tf_op jit(solution)/shard_map/ppermute | solution.py:327
  75.9 2.0 %copy-start = (bf16[1024,1792]{1,0:T(8,128)(2,1)S(1)}, bf16[1024,1792]{1,0:T(8,128)(2,1)}, u32[]{:S(2)}) copy-start(bf16[1024,1792]{1,0:T(8,128)(2,1)} %all-gather.2.cloned.1.call-done.refs_0_) | copy-start | bytes 11010052
  79.8 10.3 %collective-permute-start.8 = (bf16[128,896]{1,0:T(8,128)(2,1)S(1)}, bf16[128,896]{1,0:T(8,128)(2,1)S(1)}, u32[]{:S(2)}, u32[]{:S(2)}) collective-permute-start(bf16[128,896]{1,0:T(8,128)(2,1)S(1)} %get-tuple-element.57), channel_id=1, source_target_pairs={{0,8},{2,10},{4,12},{6,14},{8,16},{10,18},{12,20},{14,22},{16,24},... | collective-permute-start | bytes 688136 | tf_op jit(solution)/shard_map/ppermute | solution.py:382
  85.0 10.7 %collective-permute-start.7 = (bf16[128,896]{1,0:T(8,128)(2,1)S(1)}, bf16[128,896]{1,0:T(8,128)(2,1)S(1)}, u32[]{:S(2)}, u32[]{:S(2)}) collective-permute-start(bf16[128,896]{1,0:T(8,128)(2,1)S(1)} %get-tuple-element.52), channel_id=1, source_target_pairs={{8,0},{10,2},{12,4},{14,6},{16,8},{18,10},{20,12},{22,14},{24,16},... | collective-permute-start | bytes 688136 | tf_op jit(solution)/shard_map/ppermute | solution.py:382
  85.6 20.0 %collective-permute-start.6 = (bf16[128,896]{1,0:T(8,128)(2,1)S(1)}, bf16[128,896]{1,0:T(8,128)(2,1)S(1)}, u32[]{:S(2)}, u32[]{:S(2)}) collective-permute-start(bf16[128,896]{1,0:T(8,128)(2,1)S(1)} %get-tuple-element.50), channel_id=1, source_target_pairs={{0,8},{2,10},{4,12},{6,14},{8,16},{10,18},{12,20},{14,22},{16,24},... | collective-permute-start | bytes 688136 | tf_op jit(solution)/shard_map/ppermute | solution.py:383
  90.1 16.0 %collective-permute-start.5 = (bf16[128,896]{1,0:T(8,128)(2,1)S(1)}, bf16[128,896]{1,0:T(8,128)(2,1)S(1)}, u32[]{:S(2)}, u32[]{:S(2)}) collective-permute-start(bf16[128,896]{1,0:T(8,128)(2,1)S(1)} %get-tuple-element.48), channel_id=1, source_target_pairs={{8,0},{10,2},{12,4},{14,6},{16,8},{18,10},{20,12},{22,14},{24,16},... | collective-permute-start | bytes 688136 | tf_op jit(solution)/shard_map/ppermute | solution.py:383
  95.6 25.5 %collective-permute-start.9 = (bf16[128,896]{1,0:T(8,128)(2,1)S(1)}, bf16[128,896]{1,0:T(8,128)(2,1)S(1)}, u32[]{:S(2)}, u32[]{:S(2)}) collective-permute-start(bf16[128,896]{1,0:T(8,128)(2,1)S(1)} %add_convert_fusion.6), channel_id=1, source_target_pairs={{0,8},{2,10},{4,12},{6,14},{8,16},{10,18},{12,20},{14,22},{16,24},... | collective-permute-start | bytes 688136 | tf_op jit(solution)/shard_map/ppermute | solution.py:370
  102.5 18.6 %collective-permute-start.10 = (bf16[128,896]{1,0:T(8,128)(2,1)S(1)}, bf16[128,896]{1,0:T(8,128)(2,1)S(1)}, u32[]{:S(2)}, u32[]{:S(2)}) collective-permute-start(bf16[128,896]{1,0:T(8,128)(2,1)S(1)} %add_convert_fusion.7), channel_id=1, source_target_pairs={{8,0},{10,2},{12,4},{14,6},{16,8},{18,10},{20,12},{22,14},{24,16},... | collective-permute-start | bytes 688136 | tf_op jit(solution)/shard_map/ppermute | solution.py:370
  104.5 10.0 %collective-permute-start.13 = (bf16[128,1152]{1,0:T(8,128)(2,1)S(1)}, bf16[128,1152]{1,0:T(8,128)(2,1)S(1)}, u32[]{:S(2)}, u32[]{:S(2)}) collective-permute-start(bf16[128,1152]{1,0:T(8,128)(2,1)S(1)} %get-tuple-element.77), channel_id=1, source_target_pairs={{0,2},{2,0},{4,6},{6,4},{8,10},{10,8},{12,14},{14,12},{16,18},{18,... | collective-permute-start | bytes 884744 | tf_op jit(solution)/shard_map/ppermute | solution.py:331
  105.6 9.5 %collective-permute-start.14 = (bf16[128,1152]{1,0:T(8,128)(2,1)S(1)}, bf16[128,1152]{1,0:T(8,128)(2,1)S(1)}, u32[]{:S(2)}, u32[]{:S(2)}) collective-permute-start(bf16[128,1152]{1,0:T(8,128)(2,1)S(1)} %get-tuple-element.75), channel_id=1, source_target_pairs={{0,4},{2,6},{4,0},{6,2},{8,12},{10,14},{12,8},{14,10},{16,20},{18,... | collective-permute-start | bytes 884744 | tf_op jit(solution)/shard_map/ppermute | solution.py:332
  106.2 16.2 %collective-permute-start.18 = (bf16[128,1152]{1,0:T(8,128)(2,1)S(1)}, bf16[128,1152]{1,0:T(8,128)(2,1)S(1)}, u32[]{:S(2)}, u32[]{:S(2)}) collective-permute-start(bf16[128,1152]{1,0:T(8,128)(2,1)S(1)} %get-tuple-element.78), channel_id=1, source_target_pairs={{0,2},{2,0},{4,6},{6,4},{8,10},{10,8},{12,14},{14,12},{16,18},{18,... | collective-permute-start | bytes 884744 | tf_op jit(solution)/shard_map/ppermute | solution.py:331
  114.5 7.9 %collective-permute-start.19 = (bf16[128,1152]{1,0:T(8,128)(2,1)S(1)}, bf16[128,1152]{1,0:T(8,128)(2,1)S(1)}, u32[]{:S(2)}, u32[]{:S(2)}) collective-permute-start(bf16[128,1152]{1,0:T(8,128)(2,1)S(1)} %get-tuple-element.76), channel_id=1, source_target_pairs={{0,4},{2,6},{4,0},{6,2},{8,12},{10,14},{12,8},{14,10},{16,20},{18,... | collective-permute-start | bytes 884744 | tf_op jit(solution)/shard_map/ppermute | solution.py:332
  118.3 11.8 %collective-permute-start.16 = (bf16[128,1152]{1,0:T(8,128)(2,1)S(1)}, bf16[128,1152]{1,0:T(8,128)(2,1)S(1)}, u32[]{:S(2)}, u32[]{:S(2)}) collective-permute-start(bf16[128,1152]{1,0:T(8,128)(2,1)S(1)} %get-tuple-element.68), channel_id=1, source_target_pairs={{0,8},{2,10},{4,12},{6,14},{8,16},{10,18},{12,20},{14,22},{16,24},... | collective-permute-start | bytes 884744 | tf_op jit(solution)/shard_map/ppermute | solution.py:382
  121.2 26.1 %collective-permute-start.15 = (bf16[128,1152]{1,0:T(8,128)(2,1)S(1)}, bf16[128,1152]{1,0:T(8,128)(2,1)S(1)}, u32[]{:S(2)}, u32[]{:S(2)}) collective-permute-start(bf16[128,1152]{1,0:T(8,128)(2,1)S(1)} %get-tuple-element.66), channel_id=1, source_target_pairs={{8,0},{10,2},{12,4},{14,6},{16,8},{18,10},{20,12},{22,14},{24,16},... | collective-permute-start | bytes 884744 | tf_op jit(solution)/shard_map/ppermute | solution.py:383
  125.6 21.5 %collective-permute-start.21 = (bf16[128,1152]{1,0:T(8,128)(2,1)S(1)}, bf16[128,1152]{1,0:T(8,128)(2,1)S(1)}, u32[]{:S(2)}, u32[]{:S(2)}) collective-permute-start(bf16[128,1152]{1,0:T(8,128)(2,1)S(1)} %get-tuple-element.74), channel_id=1, source_target_pairs={{8,0},{10,2},{12,4},{14,6},{16,8},{18,10},{20,12},{22,14},{24,16},... | collective-permute-start | bytes 884744 | tf_op jit(solution)/shard_map/ppermute | solution.py:382
  127.6 27.0 %collective-permute-start.20 = (bf16[128,1152]{1,0:T(8,128)(2,1)S(1)}, bf16[128,1152]{1,0:T(8,128)(2,1)S(1)}, u32[]{:S(2)}, u32[]{:S(2)}) collective-permute-start(bf16[128,1152]{1,0:T(8,128)(2,1)S(1)} %get-tuple-element.72), channel_id=1, source_target_pairs={{0,8},{2,10},{4,12},{6,14},{8,16},{10,18},{12,20},{14,22},{16,24},... | collective-permute-start | bytes 884744 | tf_op jit(solution)/shard_map/ppermute | solution.py:383
  130.2 24.3 %collective-permute-start.17 = (bf16[128,1152]{1,0:T(8,128)(2,1)S(1)}, bf16[128,1152]{1,0:T(8,128)(2,1)S(1)}, u32[]{:S(2)}, u32[]{:S(2)}) collective-permute-start(bf16[128,1152]{1,0:T(8,128)(2,1)S(1)} %add_convert_fusion.3), channel_id=1, source_target_pairs={{0,8},{2,10},{4,12},{6,14},{8,16},{10,18},{12,20},{14,22},{16,24},... | collective-permute-start | bytes 884744 | tf_op jit(solution)/shard_map/ppermute | solution.py:386
  147.2 10.3 %collective-permute-start.22 = (bf16[128,1152]{1,0:T(8,128)(2,1)S(1)}, bf16[128,1152]{1,0:T(8,128)(2,1)S(1)}, u32[]{:S(2)}, u32[]{:S(2)}) collective-permute-start(bf16[128,1152]{1,0:T(8,128)(2,1)S(1)} %add_convert_fusion.1), channel_id=1, source_target_pairs={{8,0},{10,2},{12,4},{14,6},{16,8},{18,10},{20,12},{22,14},{24,16},... | collective-permute-start | bytes 884744 | tf_op jit(solution)/shard_map/ppermute | solution.py:386
Sparse Core Ops, SparseCore 0:
  9.2 66.0 all-gather.1

commit v8 on v7

--- a/solution.py
+++ b/solution.py
@@ -359,7 +359,7 @@
         to_plane_of_rows(message, offset)
         for offset, message in enumerate(gate(place, taps_here, query, mixed, PLANE))
     ]
-    landed[0], out_weight = lax.optimization_barrier((landed[0], out_weight))
+    mixed, out_weight = lax.optimization_barrier((mixed, out_weight))
     late = from_neighbours(*spans[1])
     own = jnp.stack(landed)
     gates = [own, lax.ppermute(own, "tp", [(0, 1), (1, 0)])]

time: 166 us -> 166 us (level)
  no operation moved by 1% of the time
where the time goes in v8:
time: 166 us
  waiting for transfers between devices  72.9 us (44%)
  starting transfers between devices  42.7 us (26%)
  Pallas kernels  28.8 us (17%)
  between operations  13.6 us (8%)
  local copies, waits for them, and re-layouts  5.61 us (3%)
  other arithmetic  1.83 us (1%)
    ppermute x4, waiting for transfers between devices, by_planes(): far = lax.ppermute(far, 'seq', forth)  18.6 us
    all_to_all x1, waiting for transfers between devices, by_planes(): lax.all_to_all(product, 'seq', split_axis=0, concat_axis=0, tiled=True)  16.3 us
    pallas_call x1, Pallas kernels, convolve(): pl.pallas_call(conv_kernel, out_shape=jax.ShapeDtypeStruct(((channels + 1...  14.3 us
    ppermute x4, waiting for transfers between devices, to_plane_of_rows(): return lax.ppermute(message, ('seq', 'tp'), pairs)  13 us
    pallas_call x4, Pallas kernels, project(): pl.pallas_call(project_kernel, out_shape=[jax.ShapeDtypeStruct((rows, col...  10.3 us
    ppermute x1, starting transfers between devices, by_planes(): lax.ppermute(sums[-2], 'seq', up)  8.85 us
    ppermute x4, starting transfers between devices, by_planes(): far = lax.ppermute(far, 'seq', forth)  8.64 us
    all_to_all x1, starting transfers between devices, by_planes(): lax.all_to_all(product, 'seq', split_axis=0, concat_axis=0, tiled=True)  8.32 us
  transfers between devices with their start and end apart: 26, of which 14 were waited for; matrix products, arithmetic and copies ran while one was open for 1% of the time, Pallas kernels for 17%

profile of v8, /device:TPU:0, one launch (start us, length us, event | category | flops | bytes accessed | tf_op | source)
XLA Modules:
  0.0 165.5 jit_solution(17518961902722600810)
XLA Ops:
  6.5 2.3 %slice.18 = bf16[256,1792]{1,0:T(8,128)(2,1)} slice(bf16[256,4096]{1,0:T(8,128)(2,1)} %param.11), slice={[0:256], [0:1792]} | slice | bytes 1835008 | tf_op jit(solution)/shard_map/slice | solution.py:342
  8.9 2.5 %shard_map.64 = bf16[16,144,128]{2,1,0:T(8,128)(2,1)} custom-call(f32[16,2048]{1,0:T(8,128)S(1)} %pad.4.taps_ref, bf16[2048,128]{1,0:T(8,128)(2,1)S(1)} %copy-done.1, bf16[2048,128]{1,0:T(8,128)(2,1)S(1)} %copy-done.2), custom_call_target="tpu_custom_call" | custom-call | tf_op jit(solution)/shard_map/pallas_call | solution.py:92
  11.4 8.3 %all-to-all-start = ((bf16[16,144,128]{2,1,0:T(8,128)(2,1)}), bf16[16,144,128]{2,1,0:T(8,128)(2,1)S(1)}, u32[]{:S(2)}, u32[]{:S(2)}) async-start(bf16[16,144,128]{2,1,0:T(8,128)(2,1)} %shard_map.64), calls=%async_computation | async-start | bytes 1179648 | tf_op jit(solution)/shard_map/all_to_all | solution.py:351
  19.7 16.3 %all-to-all-done.x_ref = bf16[16,144,128]{2,1,0:T(8,128)(2,1)S(1)} async-done(((bf16[16,144,128]{2,1,0:T(8,128)(2,1)}), bf16[16,144,128]{2,1,0:T(8,128)(2,1)S(1)}, u32[]{:S(2)}, u32[]{:S(2)}) %all-to-all-start) | async-done | bytes 589856 | tf_op jit(solution)/shard_map/all_to_all | solution.py:351
  36.0 4.4 %all-to-all-start.1 = ((bf16[16,128,128]{2,1,0:T(8,128)(2,1)}), bf16[16,128,128]{2,1,0:T(8,128)(2,1)S(1)}, u32[]{:S(2)}, u32[]{:S(2)}) async-start(bf16[16,128,128]{2,1,0:T(8,128)(2,1)} %bitcast.3), calls=%async_computation.1 | async-start | bytes 1048576 | tf_op jit(solution)/shard_map/all_to_all | solution.py:354
  40.5 14.3 %shard_map.65.y_ref = f32[2064,128]{1,0:T(8,128)S(1)} custom-call(f32[16,128]{1,0:T(8,128)S(1)} %constant_dynamic-slice_fusion.taps_ref, bf16[16,144,128]{2,1,0:T(8,128)(2,1)S(1)} %all-to-all-done.x_ref, f32[128,2048]{1,0:T(8,128)S(1)} %copy-done.3), custom_call_target="tpu_custom_call" | custom-call | flops 8589934592 | bytes 2621440 | tf_op jit(solution)/shard_map/pallas_call | solution.py:198
  54.7 1.8 %shard_map.66 = (bf16[4,128,128]{2,1,0:T(8,128)(2,1)S(1)}, bf16[4,128,128]{2,1,0:T(8,128)(2,1)S(1)}, bf16[4,128,128]{2,1,0:T(8,128)(2,1)S(1)}, bf16[4,128,128]{2,1,0:T(8,128)(2,1)S(1)}) custom-call(s32[3]{0:T(128)S(1)} %pad_add_fusion.place_ref, f32[16,128]{1,0:T(8,128)S(1)} %constant_dynamic-slice_fusion.taps_ref, ...), custom_call_target="tpu_custom_call" | custom-call | tf_op jit(solution)/shard_map/pallas_call | solution.py:240
  56.6 0.7 collective-permute-start
  57.3 2.0 %collective-permute-start.1 = (bf16[4,128,128]{2,1,0:T(8,128)(2,1)S(1)}, bf16[4,128,128]{2,1,0:T(8,128)(2,1)S(1)}, u32[]{:S(2)}, u32[]{:S(2)}) collective-permute-start(bf16[4,128,128]{2,1,0:T(8,128)(2,1)S(1)} %get-tuple-element.42), channel_id=1, source_target_pairs={{0,2},{1,18},{2,0},{3,16},{4,6},{5,22},{6,4},{7,20},{8,3},{9,19},{... | collective-permute-start | bytes 393224 | tf_op jit(solution)/shard_map/ppermute | solution.py:323
  59.2 1.5 collective-permute-start.2
  60.7 0.1 collective-permute-start.3
  60.8 4.2 %collective-permute-done.1 = bf16[4,128,128]{2,1,0:T(8,128)(2,1)S(1)} collective-permute-done((bf16[4,128,128]{2,1,0:T(8,128)(2,1)S(1)}, bf16[4,128,128]{2,1,0:T(8,128)(2,1)S(1)}, u32[]{:S(2)}, u32[]{:S(2)}) %collective-permute-start.1) | collective-permute-done | bytes 131104 | tf_op jit(solution)/shard_map/ppermute | solution.py:323
  65.1 2.0 %collective-permute-done.2 = bf16[4,128,128]{2,1,0:T(8,128)(2,1)S(1)} collective-permute-done((bf16[4,128,128]{2,1,0:T(8,128)(2,1)S(1)}, bf16[4,128,128]{2,1,0:T(8,128)(2,1)S(1)}, u32[]{:S(2)}, u32[]{:S(2)}) %collective-permute-start.2) | collective-permute-done | bytes 131104 | tf_op jit(solution)/shard_map/ppermute | solution.py:323
  67.0 6.8 %collective-permute-done.3 = bf16[4,128,128]{2,1,0:T(8,128)(2,1)S(1)} collective-permute-done((bf16[4,128,128]{2,1,0:T(8,128)(2,1)S(1)}, bf16[4,128,128]{2,1,0:T(8,128)(2,1)S(1)}, u32[]{:S(2)}, u32[]{:S(2)}) %collective-permute-start.3) | collective-permute-done | bytes 131104 | tf_op jit(solution)/shard_map/ppermute | solution.py:323
  74.0 0.1 slice.19.refs_0_
  74.1 1.1 collective-permute-start.11
  75.2 0.6 collective-permute-start.12
  75.9 2.0 %copy-done = bf16[1024,1792]{1,0:T(8,128)(2,1)S(1)} copy-done((bf16[1024,1792]{1,0:T(8,128)(2,1)S(1)}, bf16[1024,1792]{1,0:T(8,128)(2,1)}, u32[]{:S(2)}) %copy-start) | copy-done | bytes 3670040
  77.9 1.9 %shard_map.67 = (bf16[128,896]{1,0:T(8,128)(2,1)S(1)}, bf16[128,896]{1,0:T(8,128)(2,1)S(1)}, bf16[128,896]{1,0:T(8,128)(2,1)S(1)}, f32[128,896]{1,0:T(8,128)S(1)}) custom-call(s32[3]{0:T(128)S(1)} %pad_add_fusion.place_ref, bf16[4,4,128,128]{3,2,1,0:T(8,128)(2,1)S(1)} %pad_maximum_fusion.1.own_ref, ...), custom_call_target="tpu_custom_call" | custom-call | flops 114688 | tf_op jit(solution)/shard_map/pallas_call | solution.py:290
  79.8 3.3 %collective-permute-start.8 = (bf16[128,896]{1,0:T(8,128)(2,1)S(1)}, bf16[128,896]{1,0:T(8,128)(2,1)S(1)}, u32[]{:S(2)}, u32[]{:S(2)}) collective-permute-start(bf16[128,896]{1,0:T(8,128)(2,1)S(1)} %get-tuple-element.55), channel_id=1, source_target_pairs={{0,8},{2,10},{4,12},{6,14},{8,16},{10,18},{12,20},{14,22},{16,24},... | collective-permute-start | bytes 688136 | tf_op jit(solution)/shard_map/ppermute | solution.py:382
  83.1 1.9 %shard_map.68 = (bf16[128,896]{1,0:T(8,128)(2,1)S(1)}, bf16[128,896]{1,0:T(8,128)(2,1)S(1)}, bf16[128,896]{1,0:T(8,128)(2,1)S(1)}, f32[128,896]{1,0:T(8,128)S(1)}) custom-call(s32[3]{0:T(128)S(1)} %pad_add_fusion.place_ref, bf16[4,4,128,128]{3,2,1,0:T(8,128)(2,1)S(1)} %pad_maximum_fusion.1.own_ref, ...), custom_call_target="tpu_custom_call" | custom-call | flops 114688 | tf_op jit(solution)/shard_map/pallas_call | solution.py:290
  85.0 0.7 collective-permute-start.7
  85.6 1.4 collective-permute-start.6
  87.0 3.1 %collective-permute-done.8 = bf16[128,896]{1,0:T(8,128)(2,1)S(1)} collective-permute-done((bf16[128,896]{1,0:T(8,128)(2,1)S(1)}, bf16[128,896]{1,0:T(8,128)(2,1)S(1)}, u32[]{:S(2)}, u32[]{:S(2)}) %collective-permute-start.8) | collective-permute-done | bytes 229408 | tf_op jit(solution)/shard_map/ppermute | solution.py:382
  90.1 0.4 collective-permute-start.5
  90.6 5.0 %collective-permute-done.7 = bf16[128,896]{1,0:T(8,128)(2,1)S(1)} collective-permute-done((bf16[128,896]{1,0:T(8,128)(2,1)S(1)}, bf16[128,896]{1,0:T(8,128)(2,1)S(1)}, u32[]{:S(2)}, u32[]{:S(2)}) %collective-permute-start.7) | collective-permute-done | bytes 229408 | tf_op jit(solution)/shard_map/ppermute | solution.py:382
  95.8 6.8 %collective-permute-done.11.refs_1_ = bf16[256,2304]{1,0:T(8,128)(2,1)S(1)} collective-permute-done((bf16[256,2304]{1,0:T(8,128)(2,1)S(1)}, bf16[256,2304]{1,0:T(8,128)(2,1)S(1)}, u32[]{:S(2)}, u32[]{:S(2)}) %collective-permute-start.11) | collective-permute-done | bytes 1179680 | tf_op jit(solution)/shard_map/ppermute | solution.py:327
  102.5 0.9 collective-permute-done.12.refs_2_
  103.4 1.1 fusion.1
  104.5 1.0 collective-permute-start.13
  105.6 0.5 collective-permute-start.14
  106.2 1.3 collective-permute-start.18
  107.5 7.1 %collective-permute-done.13.refs_3_ = bf16[128,1152]{1,0:T(8,128)(2,1)S(1)} collective-permute-done((bf16[128,1152]{1,0:T(8,128)(2,1)S(1)}, bf16[128,1152]{1,0:T(8,128)(2,1)S(1)}, u32[]{:S(2)}, u32[]{:S(2)}) %collective-permute-start.13) | collective-permute-done | bytes 294944 | tf_op jit(solution)/shard_map/ppermute | solution.py:331
  114.5 0.6 collective-permute-start.19
  115.1 3.2 %shard_map.69 = (bf16[128,1152]{1,0:T(8,128)(2,1)S(1)}, bf16[128,1152]{1,0:T(8,128)(2,1)S(1)}, bf16[128,1152]{1,0:T(8,128)(2,1)S(1)}, f32[128,1152]{1,0:T(8,128)S(1)}) custom-call(s32[3]{0:T(128)S(1)} %pad_add_fusion.place_ref, bf16[4,4,128,128]{3,2,1,0:T(8,128)(2,1)S(1)} %pad_maximum_fusion.1.own_ref, ...), custom_call_target="tpu_custom_call" | custom-call | flops 147456 | tf_op jit(solution)/shard_map/pallas_call | solution.py:290
  118.3 2.8 %collective-permute-start.16 = (bf16[128,1152]{1,0:T(8,128)(2,1)S(1)}, bf16[128,1152]{1,0:T(8,128)(2,1)S(1)}, u32[]{:S(2)}, u32[]{:S(2)}) collective-permute-start(bf16[128,1152]{1,0:T(8,128)(2,1)S(1)} %get-tuple-element.66), channel_id=1, source_target_pairs={{0,8},{2,10},{4,12},{6,14},{8,16},{10,18},{12,20},{14,22},{16,24},... | collective-permute-start | bytes 884744 | tf_op jit(solution)/shard_map/ppermute | solution.py:382
  121.2 1.2 collective-permute-start.15
  122.4 3.3 %shard_map.70 = (bf16[128,1152]{1,0:T(8,128)(2,1)S(1)}, bf16[128,1152]{1,0:T(8,128)(2,1)S(1)}, bf16[128,1152]{1,0:T(8,128)(2,1)S(1)}, f32[128,1152]{1,0:T(8,128)S(1)}) custom-call(s32[3]{0:T(128)S(1)} %pad_add_fusion.place_ref, bf16[4,4,128,128]{3,2,1,0:T(8,128)(2,1)S(1)} %pad_maximum_fusion.1.own_ref, ...), custom_call_target="tpu_custom_call" | custom-call | flops 147456 | tf_op jit(solution)/shard_map/pallas_call | solution.py:290
  125.6 2.0 %collective-permute-start.21 = (bf16[128,1152]{1,0:T(8,128)(2,1)S(1)}, bf16[128,1152]{1,0:T(8,128)(2,1)S(1)}, u32[]{:S(2)}, u32[]{:S(2)}) collective-permute-start(bf16[128,1152]{1,0:T(8,128)(2,1)S(1)} %get-tuple-element.72), channel_id=1, source_target_pairs={{8,0},{10,2},{12,4},{14,6},{16,8},{18,10},{20,12},{22,14},{24,16},... | collective-permute-start | bytes 884744 | tf_op jit(solution)/shard_map/ppermute | solution.py:382
  127.6 0.1 collective-permute-start.20
  127.7 2.4 %collective-permute-done.16 = bf16[128,1152]{1,0:T(8,128)(2,1)S(1)} collective-permute-done((bf16[128,1152]{1,0:T(8,128)(2,1)S(1)}, bf16[128,1152]{1,0:T(8,128)(2,1)S(1)}, u32[]{:S(2)}, u32[]{:S(2)}) %collective-permute-start.16) | collective-permute-done | bytes 294944 | tf_op jit(solution)/shard_map/ppermute | solution.py:382
  130.2 8.8 %collective-permute-start.17 = (bf16[128,1152]{1,0:T(8,128)(2,1)S(1)}, bf16[128,1152]{1,0:T(8,128)(2,1)S(1)}, u32[]{:S(2)}, u32[]{:S(2)}) collective-permute-start(bf16[128,1152]{1,0:T(8,128)(2,1)S(1)} %add_convert_fusion.3), channel_id=1, source_target_pairs={{0,8},{2,10},{4,12},{6,14},{8,16},{10,18},{12,20},{14,22},{16,24},... | collective-permute-start | bytes 884744 | tf_op jit(solution)/shard_map/ppermute | solution.py:386
  139.1 8.1 %collective-permute-done.21 = bf16[128,1152]{1,0:T(8,128)(2,1)S(1)} collective-permute-done((bf16[128,1152]{1,0:T(8,128)(2,1)S(1)}, bf16[128,1152]{1,0:T(8,128)(2,1)S(1)}, u32[]{:S(2)}, u32[]{:S(2)}) %collective-permute-start.21) | collective-permute-done | bytes 294944 | tf_op jit(solution)/shard_map/ppermute | solution.py:382
  147.3 7.2 %collective-permute-done.17 = bf16[128,1152]{1,0:T(8,128)(2,1)S(1)} collective-permute-done((bf16[128,1152]{1,0:T(8,128)(2,1)S(1)}, bf16[128,1152]{1,0:T(8,128)(2,1)S(1)}, u32[]{:S(2)}, u32[]{:S(2)}) %collective-permute-start.17) | collective-permute-done | bytes 294944 | tf_op jit(solution)/shard_map/ppermute | solution.py:386
  154.5 0.1 add_convert_fusion.2
  154.6 2.9 %collective-permute-done.22 = bf16[128,1152]{1,0:T(8,128)(2,1)S(1)} collective-permute-done((bf16[128,1152]{1,0:T(8,128)(2,1)S(1)}, bf16[128,1152]{1,0:T(8,128)(2,1)S(1)}, u32[]{:S(2)}, u32[]{:S(2)}) %collective-permute-start.22) | collective-permute-done | bytes 294944 | tf_op jit(solution)/shard_map/ppermute | solution.py:386
  157.5 0.1 add_convert_fusion
  157.6 1.1 pad_maximum_fusion
  (43 shorter events, 1.0 us)
Async XLA Ops:
  6.5 2.3 %copy-start.5 = (f32[3,3,2048]{2,1,0:T(4,128)S(1)}, f32[3,3,2048]{2,1,0:T(4,128)}, u32[]{:S(2)}) copy-start(f32[3,3,2048]{2,1,0:T(4,128)} %param.9) | copy-start | bytes 221188
  6.5 2.4 %copy-start.1 = (bf16[2048,128]{1,0:T(8,128)(2,1)S(1)}, bf16[2048,128]{1,0:T(8,128)(2,1)}, u32[]{:S(2)}) copy-start(bf16[2048,128]{1,0:T(8,128)(2,1)} %key_ref.1) | copy-start | bytes 1572868
  6.5 2.4 %copy-start.2 = (bf16[2048,128]{1,0:T(8,128)(2,1)S(1)}, bf16[2048,128]{1,0:T(8,128)(2,1)}, u32[]{:S(2)}) copy-start(bf16[2048,128]{1,0:T(8,128)(2,1)} %value_ref.1) | copy-start | bytes 1572868
  6.5 69.3 %all-gather.2.cloned.1.call-start = ((), (), s32[]{:S(2)}) async-start(), calls=%async_computation.2 | async-start | bytes 4587520 | tf_op jit(solution)/shard_map/all_gather | solution.py:343
  8.9 31.5 %copy-start.3 = (f32[128,2048]{1,0:T(8,128)S(1)}, f32[128,2048]{1,0:T(8,128)}, u32[]{:S(2)}) copy-start(f32[128,2048]{1,0:T(8,128)} %h_ref.1) | copy-start | bytes 3145732
  11.4 24.6 %all-to-all-start = ((bf16[16,144,128]{2,1,0:T(8,128)(2,1)}), bf16[16,144,128]{2,1,0:T(8,128)(2,1)S(1)}, u32[]{:S(2)}, u32[]{:S(2)}) async-start(bf16[16,144,128]{2,1,0:T(8,128)(2,1)} %shard_map.64), calls=%async_computation | async-start | bytes 1179648 | tf_op jit(solution)/shard_map/all_to_all | solution.py:351
  36.0 18.7 %all-to-all-start.1 = ((bf16[16,128,128]{2,1,0:T(8,128)(2,1)}), bf16[16,128,128]{2,1,0:T(8,128)(2,1)S(1)}, u32[]{:S(2)}, u32[]{:S(2)}) async-start(bf16[16,128,128]{2,1,0:T(8,128)(2,1)} %bitcast.3), calls=%async_computation.1 | async-start | bytes 1048576 | tf_op jit(solution)/shard_map/all_to_all | solution.py:354
  54.7 19.3 %copy-start.4 = (bf16[256,4096]{1,0:T(8,128)(2,1)S(1)}, bf16[256,4096]{1,0:T(8,128)(2,1)}, u32[]{:S(2)}) copy-start(bf16[256,4096]{1,0:T(8,128)(2,1)} %param.11) | copy-start | bytes 6291460
  56.6 4.2 %collective-permute-start = (bf16[4,128,128]{2,1,0:T(8,128)(2,1)S(1)}, bf16[4,128,128]{2,1,0:T(8,128)(2,1)S(1)}, u32[]{:S(2)}, u32[]{:S(2)}) collective-permute-start(bf16[4,128,128]{2,1,0:T(8,128)(2,1)S(1)} %get-tuple-element.41), channel_id=1, source_target_pairs={{0,0},{1,16},{2,2},{3,18},{4,4},{5,20},{6,6},{7,22},{8,1},{9,17},{... | collective-permute-start | bytes 393224 | tf_op jit(solution)/shard_map/ppermute | solution.py:323
  57.3 7.8 %collective-permute-start.1 = (bf16[4,128,128]{2,1,0:T(8,128)(2,1)S(1)}, bf16[4,128,128]{2,1,0:T(8,128)(2,1)S(1)}, u32[]{:S(2)}, u32[]{:S(2)}) collective-permute-start(bf16[4,128,128]{2,1,0:T(8,128)(2,1)S(1)} %get-tuple-element.42), channel_id=1, source_target_pairs={{0,2},{1,18},{2,0},{3,16},{4,6},{5,22},{6,4},{7,20},{8,3},{9,19},{... | collective-permute-start | bytes 393224 | tf_op jit(solution)/shard_map/ppermute | solution.py:323
  59.2 7.8 %collective-permute-start.2 = (bf16[4,128,128]{2,1,0:T(8,128)(2,1)S(1)}, bf16[4,128,128]{2,1,0:T(8,128)(2,1)S(1)}, u32[]{:S(2)}, u32[]{:S(2)}) collective-permute-start(bf16[4,128,128]{2,1,0:T(8,128)(2,1)S(1)} %get-tuple-element.43), channel_id=1, source_target_pairs={{0,4},{1,20},{2,6},{3,22},{4,0},{5,16},{6,2},{7,18},{8,5},{9,21},{... | collective-permute-start | bytes 393224 | tf_op jit(solution)/shard_map/ppermute | solution.py:323
  60.7 13.1 %collective-permute-start.3 = (bf16[4,128,128]{2,1,0:T(8,128)(2,1)S(1)}, bf16[4,128,128]{2,1,0:T(8,128)(2,1)S(1)}, u32[]{:S(2)}, u32[]{:S(2)}) collective-permute-start(bf16[4,128,128]{2,1,0:T(8,128)(2,1)S(1)} %get-tuple-element.44), channel_id=1, source_target_pairs={{0,6},{1,22},{2,4},{3,20},{4,2},{5,18},{6,0},{7,16},{8,7},{9,23},{... | collective-permute-start | bytes 393224 | tf_op jit(solution)/shard_map/ppermute | solution.py:323
  73.9 2.0 %collective-permute-start.4 = (bf16[4,4,128,128]{3,2,1,0:T(8,128)(2,1)S(1)}, bf16[4,4,128,128]{3,2,1,0:T(8,128)(2,1)S(1)}, u32[]{:S(2)}, u32[]{:S(2)}) collective-permute-start(bf16[4,4,128,128]{3,2,1,0:T(8,128)(2,1)S(1)} %pad_maximum_fusion.1.own_ref), channel_id=1, source_target_pairs={{0,1},{1,0},{2,3},{3,2},{4,5},{5,4},{6,7},{7,6},{8,9},{9,8},{10,11... | collective-permute-start | bytes 1572872 | tf_op jit(solution)/shard_map/ppermute | solution.py:365
  74.1 28.4 %collective-permute-start.11 = (bf16[256,2304]{1,0:T(8,128)(2,1)S(1)}, bf16[256,2304]{1,0:T(8,128)(2,1)S(1)}, u32[]{:S(2)}, u32[]{:S(2)}) collective-permute-start(bf16[256,2304]{1,0:T(8,128)(2,1)S(1)} %slice.19.refs_0_), channel_id=1, source_target_pairs={{0,2},{2,0},{4,6},{6,4},{8,10},{10,8},{12,14},{14,12},{16,18},{18,... | collective-permute-start | bytes 3538952 | tf_op jit(solution)/shard_map/ppermute | solution.py:327
  75.2 28.2 %collective-permute-start.12 = (bf16[256,2304]{1,0:T(8,128)(2,1)S(1)}, bf16[256,2304]{1,0:T(8,128)(2,1)}, u32[]{:S(2)}, u32[]{:S(2)}) collective-permute-start(bf16[256,2304]{1,0:T(8,128)(2,1)S(1)} %slice.19.refs_0_), channel_id=1, source_target_pairs={{0,4},{2,6},{4,0},{6,2},{8,12},{10,14},{12,8},{14,10},{16,20},{18,... | collective-permute-start | bytes 3538952 | tf_op jit(solution)/shard_map/ppermute | solution.py:327
  75.9 2.0 %copy-start = (bf16[1024,1792]{1,0:T(8,128)(2,1)S(1)}, bf16[1024,1792]{1,0:T(8,128)(2,1)}, u32[]{:S(2)}) copy-start(bf16[1024,1792]{1,0:T(8,128)(2,1)} %all-gather.2.cloned.1.call-done.refs_0_) | copy-start | bytes 11010052
  79.8 10.3 %collective-permute-start.8 = (bf16[128,896]{1,0:T(8,128)(2,1)S(1)}, bf16[128,896]{1,0:T(8,128)(2,1)S(1)}, u32[]{:S(2)}, u32[]{:S(2)}) collective-permute-start(bf16[128,896]{1,0:T(8,128)(2,1)S(1)} %get-tuple-element.55), channel_id=1, source_target_pairs={{0,8},{2,10},{4,12},{6,14},{8,16},{10,18},{12,20},{14,22},{16,24},... | collective-permute-start | bytes 688136 | tf_op jit(solution)/shard_map/ppermute | solution.py:382
  85.0 10.7 %collective-permute-start.7 = (bf16[128,896]{1,0:T(8,128)(2,1)S(1)}, bf16[128,896]{1,0:T(8,128)(2,1)S(1)}, u32[]{:S(2)}, u32[]{:S(2)}) collective-permute-start(bf16[128,896]{1,0:T(8,128)(2,1)S(1)} %get-tuple-element.50), channel_id=1, source_target_pairs={{8,0},{10,2},{12,4},{14,6},{16,8},{18,10},{20,12},{22,14},{24,16},... | collective-permute-start | bytes 688136 | tf_op jit(solution)/shard_map/ppermute | solution.py:382
  85.6 20.0 %collective-permute-start.6 = (bf16[128,896]{1,0:T(8,128)(2,1)S(1)}, bf16[128,896]{1,0:T(8,128)(2,1)S(1)}, u32[]{:S(2)}, u32[]{:S(2)}) collective-permute-start(bf16[128,896]{1,0:T(8,128)(2,1)S(1)} %get-tuple-element.48), channel_id=1, source_target_pairs={{0,8},{2,10},{4,12},{6,14},{8,16},{10,18},{12,20},{14,22},{16,24},... | collective-permute-start | bytes 688136 | tf_op jit(solution)/shard_map/ppermute | solution.py:383
  90.1 16.0 %collective-permute-start.5 = (bf16[128,896]{1,0:T(8,128)(2,1)S(1)}, bf16[128,896]{1,0:T(8,128)(2,1)S(1)}, u32[]{:S(2)}, u32[]{:S(2)}) collective-permute-start(bf16[128,896]{1,0:T(8,128)(2,1)S(1)} %get-tuple-element.46), channel_id=1, source_target_pairs={{8,0},{10,2},{12,4},{14,6},{16,8},{18,10},{20,12},{22,14},{24,16},... | collective-permute-start | bytes 688136 | tf_op jit(solution)/shard_map/ppermute | solution.py:383
  95.6 25.5 %collective-permute-start.9 = (bf16[128,896]{1,0:T(8,128)(2,1)S(1)}, bf16[128,896]{1,0:T(8,128)(2,1)S(1)}, u32[]{:S(2)}, u32[]{:S(2)}) collective-permute-start(bf16[128,896]{1,0:T(8,128)(2,1)S(1)} %add_convert_fusion.6), channel_id=1, source_target_pairs={{0,8},{2,10},{4,12},{6,14},{8,16},{10,18},{12,20},{14,22},{16,24},... | collective-permute-start | bytes 688136 | tf_op jit(solution)/shard_map/ppermute | solution.py:370
  102.5 18.6 %collective-permute-start.10 = (bf16[128,896]{1,0:T(8,128)(2,1)S(1)}, bf16[128,896]{1,0:T(8,128)(2,1)S(1)}, u32[]{:S(2)}, u32[]{:S(2)}) collective-permute-start(bf16[128,896]{1,0:T(8,128)(2,1)S(1)} %add_convert_fusion.7), channel_id=1, source_target_pairs={{8,0},{10,2},{12,4},{14,6},{16,8},{18,10},{20,12},{22,14},{24,16},... | collective-permute-start | bytes 688136 | tf_op jit(solution)/shard_map/ppermute | solution.py:370
  104.5 10.0 %collective-permute-start.13 = (bf16[128,1152]{1,0:T(8,128)(2,1)S(1)}, bf16[128,1152]{1,0:T(8,128)(2,1)S(1)}, u32[]{:S(2)}, u32[]{:S(2)}) collective-permute-start(bf16[128,1152]{1,0:T(8,128)(2,1)S(1)} %get-tuple-element.75), channel_id=1, source_target_pairs={{0,2},{2,0},{4,6},{6,4},{8,10},{10,8},{12,14},{14,12},{16,18},{18,... | collective-permute-start | bytes 884744 | tf_op jit(solution)/shard_map/ppermute | solution.py:331
  105.6 9.5 %collective-permute-start.14 = (bf16[128,1152]{1,0:T(8,128)(2,1)S(1)}, bf16[128,1152]{1,0:T(8,128)(2,1)S(1)}, u32[]{:S(2)}, u32[]{:S(2)}) collective-permute-start(bf16[128,1152]{1,0:T(8,128)(2,1)S(1)} %get-tuple-element.73), channel_id=1, source_target_pairs={{0,4},{2,6},{4,0},{6,2},{8,12},{10,14},{12,8},{14,10},{16,20},{18,... | collective-permute-start | bytes 884744 | tf_op jit(solution)/shard_map/ppermute | solution.py:332
  106.2 16.2 %collective-permute-start.18 = (bf16[128,1152]{1,0:T(8,128)(2,1)S(1)}, bf16[128,1152]{1,0:T(8,128)(2,1)S(1)}, u32[]{:S(2)}, u32[]{:S(2)}) collective-permute-start(bf16[128,1152]{1,0:T(8,128)(2,1)S(1)} %get-tuple-element.76), channel_id=1, source_target_pairs={{0,2},{2,0},{4,6},{6,4},{8,10},{10,8},{12,14},{14,12},{16,18},{18,... | collective-permute-start | bytes 884744 | tf_op jit(solution)/shard_map/ppermute | solution.py:331
  114.5 7.9 %collective-permute-start.19 = (bf16[128,1152]{1,0:T(8,128)(2,1)S(1)}, bf16[128,1152]{1,0:T(8,128)(2,1)S(1)}, u32[]{:S(2)}, u32[]{:S(2)}) collective-permute-start(bf16[128,1152]{1,0:T(8,128)(2,1)S(1)} %get-tuple-element.74), channel_id=1, source_target_pairs={{0,4},{2,6},{4,0},{6,2},{8,12},{10,14},{12,8},{14,10},{16,20},{18,... | collective-permute-start | bytes 884744 | tf_op jit(solution)/shard_map/ppermute | solution.py:332
  118.3 11.8 %collective-permute-start.16 = (bf16[128,1152]{1,0:T(8,128)(2,1)S(1)}, bf16[128,1152]{1,0:T(8,128)(2,1)S(1)}, u32[]{:S(2)}, u32[]{:S(2)}) collective-permute-start(bf16[128,1152]{1,0:T(8,128)(2,1)S(1)} %get-tuple-element.66), channel_id=1, source_target_pairs={{0,8},{2,10},{4,12},{6,14},{8,16},{10,18},{12,20},{14,22},{16,24},... | collective-permute-start | bytes 884744 | tf_op jit(solution)/shard_map/ppermute | solution.py:382
  121.2 26.1 %collective-permute-start.15 = (bf16[128,1152]{1,0:T(8,128)(2,1)S(1)}, bf16[128,1152]{1,0:T(8,128)(2,1)S(1)}, u32[]{:S(2)}, u32[]{:S(2)}) collective-permute-start(bf16[128,1152]{1,0:T(8,128)(2,1)S(1)} %get-tuple-element.64), channel_id=1, source_target_pairs={{8,0},{10,2},{12,4},{14,6},{16,8},{18,10},{20,12},{22,14},{24,16},... | collective-permute-start | bytes 884744 | tf_op jit(solution)/shard_map/ppermute | solution.py:383
  125.6 21.5 %collective-permute-start.21 = (bf16[128,1152]{1,0:T(8,128)(2,1)S(1)}, bf16[128,1152]{1,0:T(8,128)(2,1)S(1)}, u32[]{:S(2)}, u32[]{:S(2)}) collective-permute-start(bf16[128,1152]{1,0:T(8,128)(2,1)S(1)} %get-tuple-element.72), channel_id=1, source_target_pairs={{8,0},{10,2},{12,4},{14,6},{16,8},{18,10},{20,12},{22,14},{24,16},... | collective-permute-start | bytes 884744 | tf_op jit(solution)/shard_map/ppermute | solution.py:382
  127.6 27.0 %collective-permute-start.20 = (bf16[128,1152]{1,0:T(8,128)(2,1)S(1)}, bf16[128,1152]{1,0:T(8,128)(2,1)S(1)}, u32[]{:S(2)}, u32[]{:S(2)}) collective-permute-start(bf16[128,1152]{1,0:T(8,128)(2,1)S(1)} %get-tuple-element.70), channel_id=1, source_target_pairs={{0,8},{2,10},{4,12},{6,14},{8,16},{10,18},{12,20},{14,22},{16,24},... | collective-permute-start | bytes 884744 | tf_op jit(solution)/shard_map/ppermute | solution.py:383
  130.2 24.3 %collective-permute-start.17 = (bf16[128,1152]{1,0:T(8,128)(2,1)S(1)}, bf16[128,1152]{1,0:T(8,128)(2,1)S(1)}, u32[]{:S(2)}, u32[]{:S(2)}) collective-permute-start(bf16[128,1152]{1,0:T(8,128)(2,1)S(1)} %add_convert_fusion.3), channel_id=1, source_target_pairs={{0,8},{2,10},{4,12},{6,14},{8,16},{10,18},{12,20},{14,22},{16,24},... | collective-permute-start | bytes 884744 | tf_op jit(solution)/shard_map/ppermute | solution.py:386
  147.2 10.3 %collective-permute-start.22 = (bf16[128,1152]{1,0:T(8,128)(2,1)S(1)}, bf16[128,1152]{1,0:T(8,128)(2,1)S(1)}, u32[]{:S(2)}, u32[]{:S(2)}) collective-permute-start(bf16[128,1152]{1,0:T(8,128)(2,1)S(1)} %add_convert_fusion.1), channel_id=1, source_target_pairs={{8,0},{10,2},{12,4},{14,6},{16,8},{18,10},{20,12},{22,14},{24,16},... | collective-permute-start | bytes 884744 | tf_op jit(solution)/shard_map/ppermute | solution.py:386
Sparse Core Ops, SparseCore 0:
  9.2 66.0 all-gather.1
